TPU v7x, 256 devices: a whole 4x4x8 slice. The times are simulated.
256 devices in a mesh: wall: 8 (over y, core), surf: 32 (over x, z).
Axes of the slice: x: 4, y: 4, z: 8, core: 2. Of those that a mesh axis runs over, the one named last changes fastest.
Arguments:
- vector: bfloat16 [128, 32, 320, 256], P('surf', 'wall'), may hold values from -40 to 40
- lengths: int32 [128], P('surf'), may hold values from 1 to 32, as said below
- north_of: int32 [32, 4], P('surf'), may hold values from 0 to 3, each once within a row
- diagonal: bfloat16 [128, 32, 320, 320], P('surf', 'wall'), may hold values from -1 to 8
- lifting: bfloat16 [128, 32, 6, 80, 320], P('surf', 'wall'), may hold values from -0.625 to 0.625
- inverse_rows: bfloat16 [128, 32, 80, 320], P('surf', 'wall'), may hold values from -0.25 to 0.25
Outputs:
- next_basis: bfloat16 [128, 32, 320, 256], P('surf', 'wall')
- coefs: float32 [2, 256], replicated
Inputs may be any that keep to these rules, and one draw needn't show every extreme that they name: `lengths`: in every patch of 4 lines one line has 32 elements and another has 1.
All inputs are finite; a program needn't handle non-finite values.
Results may differ from a plain program's by a relative error of at most 0.00135.
Values may be sent and summed in bfloat16 or wider, within the bound.
No kernel may reach another device: no remote copies, remote signals or barrier semaphores. Data moves between devices by JAX's collectives and lax.ppermute only.
A program may use at most 64 MiB of HBM per device.

v0:
```python
import jax
import jax.numpy as jnp
from jax import lax
from jax.sharding import Mesh
from jax.sharding import PartitionSpec as P

VARS = 5
NODE1D = 4
FACE = 80
WALL = ("wall_0", "wall_1")
SURF = ("surf_0", "surf_1")
WALL_SURF = ("wall_0", "wall_1", "surf_0", "surf_1")


FULL_ACCURACY = lax.Precision.HIGHEST


def with_halo(cells, sides, width, closed):
    for axis, dim in sides:
        count = lax.axis_size(axis)
        ends = count if closed else count - 1
        head = lax.slice_in_dim(cells, 0, width, axis=dim)
        tail = lax.slice_in_dim(cells, cells.shape[dim] - width, cells.shape[dim], axis=dim)
        cells = jnp.concatenate(
            [
                lax.ppermute(tail, axis, [(i, (i + 1) % count) for i in range(ends)]),
                cells,
                lax.ppermute(head, axis, [((i + 1) % count, i) for i in range(ends)]),
            ],
            axis=dim,
        )
    return cells


def carried_in(value, axis, join, neutral):
    count, mine = (lax.axis_size(axis), lax.axis_index(axis))
    pieces = jax.tree.map(lambda part: lax.all_gather(part, axis), value)
    so_far = jax.tree.map(
        lambda part, zero: jnp.full_like(part, 0) + jnp.asarray(zero, part.dtype), value, neutral
    )

    def hop(position, so_far):
        longer = join(so_far, jax.tree.map(lambda part: part[position], pieces))
        return jax.tree.map(lambda new, old: jnp.where(position < mine, new, old), longer, so_far)

    return lax.fori_loop(0, count - 1, hop, so_far)


def over_axes(shard, axes):
    for axis in axes:
        shard = lax.psum(shard, axis)
    return shard


def face_traces(values):
    leading = values.shape[:-2]
    column_entries = values.shape[-1]
    nodal_cube = values.reshape(leading + (VARS, NODE1D, NODE1D, NODE1D, column_entries))
    last_node = NODE1D - 1

    def flatten(piece):
        return piece.reshape(leading + (FACE, column_entries))

    bottom_face = flatten(nodal_cube[..., 0, :])
    top_face = flatten(nodal_cube[..., last_node, :])
    west_face = flatten(nodal_cube[..., 0, :, :, :])
    east_face = flatten(nodal_cube[..., last_node, :, :, :])
    south_face = flatten(nodal_cube[..., 0, :, :])
    north_face = flatten(nodal_cube[..., last_node, :, :])
    return (bottom_face, top_face, west_face, east_face, south_face, north_face)


def exact_times(form, left, right):
    return jnp.einsum(
        form, left.astype(jnp.float32), right.astype(jnp.float32), precision=FULL_ACCURACY
    )


def apply_map(matrices, states):
    return exact_times("lfg,lgr->lfr", matrices, states)


def compose(earlier, latter):
    joined = exact_times("lfg,lgh->lfh", latter[0], earlier[0])
    return (joined, apply_map(latter[0], earlier[1]) + latter[1])


def per_device(vector, lengths, north_of, diagonal, lifting, inverse_rows):
    lines_here, segment, block_size, column_entries = vector.shape
    face_size = inverse_rows.shape[2]
    positions = lax.axis_index(WALL) * segment + jnp.arange(segment, dtype=jnp.int32)
    alive_mask = positions[None, :] < lengths[:, None]
    living = alive_mask.astype(jnp.float32)
    masked = vector * alive_mask.astype(jnp.bfloat16)[:, :, None, None]
    bottom_face, top_face, west_face, east_face, south_face, north_face = face_traces(masked)
    wall_edges = jnp.stack([bottom_face[:, 0], top_face[:, -1]], axis=1)
    wall_padded = with_halo(wall_edges, ((WALL, 1),), 1, False)
    from_below = jnp.concatenate([wall_padded[:, 0:1], top_face[:, :-1]], axis=1)
    from_above = jnp.concatenate([bottom_face[:, 1:], wall_padded[:, 3:4]], axis=1)
    patch_edges = jnp.stack([west_face[0], east_face[-1]], axis=0)
    patch_padded = with_halo(patch_edges, ((SURF, 0),), 1, True)
    from_west = jnp.concatenate([patch_padded[0:1], east_face[:-1]], axis=0)
    from_east = jnp.concatenate([west_face[1:], patch_padded[3:4]], axis=0)
    selector = (north_of[0][:, None] == jnp.arange(lines_here, dtype=jnp.int32)[None, :]).astype(
        jnp.bfloat16
    )
    from_north = jnp.einsum(
        "ij,jsfr->isfr", selector, south_face, preferred_element_type=jnp.float32
    ).astype(jnp.bfloat16)
    from_south = jnp.einsum(
        "ij,isfr->jsfr", selector, north_face, preferred_element_type=jnp.float32
    ).astype(jnp.bfloat16)
    neighbours = jnp.stack(
        [from_below, from_above, from_west, from_east, from_south, from_north], axis=2
    )
    matrix_product = jnp.einsum(
        "lsbc,lscr->lsbr", diagonal, masked, preferred_element_type=jnp.float32
    )
    matrix_product = matrix_product + jnp.einsum(
        "lsgfb,lsgfr->lsbr", lifting, neighbours, preferred_element_type=jnp.float32
    )
    matrix_product = matrix_product * living[:, :, None, None]
    lower_lift = lifting[:, :, 0]
    identity_map = jnp.broadcast_to(
        jnp.eye(face_size, dtype=jnp.float32), (lines_here, face_size, face_size)
    )
    carried = jnp.zeros((lines_here, face_size, column_entries), jnp.float32)
    prefix = identity_map
    free_part = []
    prefixes = []
    for position in range(segment):
        alive_now = living[:, position][:, None, None]
        eliminated = alive_now * (
            matrix_product[:, position]
            - exact_times("lfb,lfr->lbr", lower_lift[:, position], carried)
        )
        free_part.append(eliminated)
        prefixes.append(prefix)
        carried = exact_times("lfb,lbr->lfr", inverse_rows[:, position], eliminated)
        step_map = -alive_now * exact_times(
            "lfb,lgb->lfg", inverse_rows[:, position], lower_lift[:, position]
        )
        prefix = exact_times("lfg,lgh->lfh", step_map, prefix)
    start_pair = (identity_map, jnp.zeros_like(carried))
    _, incoming = carried_in((prefix, carried), WALL, compose, start_pair)
    finished = []
    for position in range(segment):
        alive_now = living[:, position][:, None, None]
        arriving = apply_map(prefixes[position], incoming)
        correction = exact_times("lfb,lfr->lbr", lower_lift[:, position], arriving)
        finished.append(free_part[position] - alive_now * correction)
    eliminated = jnp.stack(finished, axis=1)
    masked_wide = masked.astype(jnp.float32)
    entries = lines_here * segment * block_size * lax.axis_size(SURF) * lax.axis_size(WALL)
    coupling_total, self_sum = (
        over_axes(jnp.sum(masked_wide * eliminated, axis=(0, 1, 2)), WALL_SURF),
        over_axes(jnp.sum(masked_wide * masked_wide, axis=(0, 1, 2)), WALL_SURF),
    )
    projection = coupling_total / self_sum
    remainder = eliminated - projection * masked_wide
    squares = over_axes(jnp.sum(remainder * remainder, axis=(0, 1, 2)), WALL_SURF)
    spread = jnp.sqrt(squares / entries + 1e-06)
    next_basis = (remainder / spread).astype(jnp.bfloat16)
    return (next_basis, jnp.stack([projection, spread]))


def solution(mesh):
    split = Mesh(mesh.devices.reshape(4, 2, 4, 8), ("wall_0", "wall_1", "surf_0", "surf_1"))
    placed = (
        P(SURF, WALL, None, None),
        P(SURF),
        P(SURF, None),
        P(SURF, WALL, None, None),
        P(SURF, WALL, None, None, None),
        P(SURF, WALL, None, None),
    )
    return jax.shard_map(
        per_device,
        mesh=split,
        in_specs=placed,
        out_specs=(P(SURF, WALL, None, None), P()),
        check_vma=False,
    )
```

profile of v0, /device:TPU:10, one launch (start us, length us, event | category | flops | bytes accessed | tf_op | source)
XLA Modules:
  0.0 210.6 jit_solution(498464699104618996)
XLA Ops:
  8.0 3.5 %copy_multiply_fusion = bf16[4,4,320,256]{3,2,0,1:T(8,128)(2,1)} fusion(bf16[4,4,320,256]{3,2,1,0:T(8,128)(2,1)} %param.8, bf16[4,4]{0,1:T(4,128)(2,1)S(1)} %get-tuple-element.158), kind=kLoop, calls=%fused_computation.25 | loop fusion | flops 1310720 | bytes 5242912 | tf_op jit(solution)/shard_map/mul | solution.py:94
  11.4 3.5 %reshape.104 = bf16[4,4,5,4,4,4,256]{6,5,4,3,2,0,1:T(4,128)(2,1)S(1)} reshape(bf16[4,4,320,256]{3,2,0,1:T(8,128)(2,1)} %copy_multiply_fusion) | data formatting | bytes 5242880 | tf_op jit(solution)/shard_map/reshape | solution.py:58
  15.0 3.0 %fusion.85 = (bf16[4,4,5,4,4,1,256]{6,5,4,3,2,0,1:T(2,128)(2,1)S(1)}, bf16[4,4,5,4,4,1,256]{6,5,4,3,2,0,1:T(2,128)(2,1)S(1)}) fusion(bf16[4,4,5,4,4,4,256]{6,5,4,3,2,0,1:T(4,128)(2,1)S(1)} %reshape.104), kind=kLoop, calls=%fused_computation.129 | loop fusion | bytes 2621440 | tf_op jit(solution)/shard_map/slice | solution.py:64
  19.7 1.9 collective-permute-start
  23.3 3.6 %collective-permute-start.1 = (bf16[4,1,80,256]{3,0,2,1:T(4,128)(2,1)}, bf16[4,1,80,256]{3,0,2,1:T(4,128)(2,1)}, u32[]{:S(2)}, u32[]{:S(2)}) collective-permute-start(bf16[4,1,80,256]{3,0,2,1:T(4,128)(2,1)} %slice.159), channel_id=1, source_target_pairs={{32,0},{64,32},{96,64},{128,96},{160,128},{192,160},{224,192},{33,... | collective-permute-start | bytes 491528 | tf_op jit(solution)/shard_map/ppermute | solution.py:28
  28.1 1.9 collective-permute-start.2
  31.1 3.9 %collective-permute-start.3 = (bf16[1,4,80,256]{3,0,2,1:T(2,128)(2,1)}, bf16[1,4,80,256]{3,0,2,1:T(2,128)(2,1)}, u32[]{:S(2)}, u32[]{:S(2)}) collective-permute-start(bf16[1,4,80,256]{3,0,2,1:T(2,128)(2,1)} %copy.55), channel_id=1, source_target_pairs={{1,0},{2,1},{3,2},{4,3},{5,4},{6,5},{7,6},{8,7},{9,8},{10,9},{11,1... | collective-permute-start | bytes 491528 | tf_op jit(solution)/shard_map/ppermute | solution.py:28
  35.0 1.4 fusion.83
  36.4 1.4 fusion.82
  37.8 1.3 copy_bitcast_fusion
  39.6 1.5 copy.52
  41.1 1.4 copy.53
  43.2 1.1 fusion.43
  44.3 2.2 %fusion.44 = bf16[4,4,6,80,256]{4,0,3,1,2:T(4,128)(2,1)} fusion(bf16[4,4,6,80,256]{4,0,3,1,2:T(4,128)(2,1)} %fusion.43, bf16[4,1,80,256]{3,0,2,1:T(4,128)(2,1)} %collective-permute-done.1, bf16[4,3,80,256]{3,0,2,1:T(4,128)(2,1)S(1)} %slice.158), kind=kLoop, calls=%fused_computation.73 | loop fusion | flops 1310720 | bytes 1310720
  46.5 2.5 %fusion.45 = bf16[4,4,6,80,256]{4,0,3,1,2:T(4,128)(2,1)} fusion(bf16[4,4,6,80,256]{4,0,3,1,2:T(4,128)(2,1)} %fusion.44, bf16[3,4,80,256]{3,0,2,1:T(4,128)(2,1)S(1)} %bitcast.245, bf16[1,4,80,256]{3,0,2,1:T(2,128)(2,1)} %collective-permute-done.2), kind=kLoop, calls=%fused_computation.75 | loop fusion | flops 1310720 | bytes 1474560
  49.0 2.5 %fusion.46 = bf16[4,4,6,80,256]{4,0,3,1,2:T(4,128)(2,1)} fusion(bf16[4,4,6,80,256]{4,0,3,1,2:T(4,128)(2,1)} %fusion.45, bf16[1,4,80,256]{3,0,2,1:T(2,128)(2,1)} %collective-permute-done.3, bf16[3,4,80,256]{3,0,2,1:T(4,128)(2,1)S(1)} %bitcast.244), kind=kLoop, calls=%fused_computation.77 | loop fusion | flops 1310720 | bytes 1474560
  51.5 1.5 fusion.40
  53.0 1.4 fusion.42
  54.4 4.4 %fusion.13 = f32[4,4,256,320,1]{2,3,4,1,0:T(8,128)S(1)} fusion(bf16[4,4,6,80,320]{4,3,2,1,0:T(8,128)(2,1)S(1)} %bitcast.242, bf16[4,4,6,80,256]{4,0,3,1,2:T(4,128)(2,1)} %fusion.42), kind=kOutput, calls=%fused_computation.21 | convolution fusion | flops 1258291200 | bytes 14090240 | tf_op jit(solution)/shard_map/lsgfb,lsgfr->lsbr/dot_general | solution.py:119
  58.8 3.7 %fusion.12 = f32[4,4,320,256]{3,2,1,0:T(8,128)S(1)} fusion(f32[4,4,256,320,1]{2,3,4,1,0:T(8,128)S(1)} %fusion.13, f32[4,4]{1,0:T(4,128)S(1)} %copy.60, bf16[4,4,320,320]{3,2,1,0:T(8,128)(2,1)} %param.11, bf16[4,4,320,256]{3,2,0,1:T(8,128)(2,1)S(1)} %copy-done.1), kind=kOutput, calls=%fused_computation.18 | convolution fusion | flops 841482240 | bytes 16384064 | tf_op jit(solution)/shard_map/lsbc,lscr->lsbr/dot_general | solution.py:116
  64.5 1.8 fusion.36
  70.9 1.4 convolution_bitcast_fusion.4
  72.4 1.3 convolution_multiply_fusion.4
  74.0 1.3 convolution_multiply_fusion.5
  75.7 1.3 convolution_multiply_fusion.6
  77.3 1.3 convolution_multiply_fusion.7
  78.9 17.8 %all-gather = f32[32,80,80]{2,1,0:T(8,128)} all-gather(f32[4,80,80]{2,1,0:T(8,128)S(1)} %fusion.88), channel_id=2, replica_groups=mesh['wall_0'=4,'wall_1'=2,'surf_0'=4,'surf_1'=8] {'wall_0','wall_1'}, dimensions={0}, use_global_device_ids=true | all-gather | bytes 921600 | tf_op jit(solution)/shard_map/all_gather | solution.py:37
  96.7 6.5 %all-gather.4.cloned.1.call-done = f32[32,80,256]{2,1,0:T(8,128)} async-done(((f32[4,80,256]{2,1,0:T(8,128)}), f32[32,80,256]{2,1,0:T(8,128)}) %all-gather.4.cloned.1.call-update) | async-done | bytes 2621456 | tf_op jit(solution)/shard_map/all_gather | solution.py:37
  103.2 10.9 %while.14 = (s32[]{:T(128)}, f32[4,80,256]{2,1,0:T(8,128)S(1)}, s32[]{:T(128)}, f32[8,4,80,80]{3,2,1,0:T(8,128)}, f32[8,4,80,256]{3,2,1,0:T(8,128)}, /*index=5*/s32[]{:T(128)}, s32[]{:T(128)}) while((s32[]{:T(128)}, f32[4,80,256]{2,1,0:T(8,128)S(1)}, s32[]{:T(128)}, f32[8,4,80,80]{3,2,1,0:T(8,128)}, f32[8,4,80,256]{3,2,1,0:T(8,128)}, ...), condition=%wide.region_1.2_spmd.clone, body=%wide.region_0.1_spmd.clone.sunk | while | flops 78970880 | bytes 2132575 | solution.py:46
  103.2 1.5 fusion.127
  104.7 1.5 fusion.127
  106.3 1.5 fusion.127
  107.9 1.5 fusion.127
  109.4 1.5 fusion.127
  111.0 1.5 fusion.127
  112.5 1.5 fusion.127
  119.9 1.6 fusion.9
  121.5 8.9 %all-reduce.2 = (f32[256]{0:T(256)S(1)}, f32[256]{0:T(256)S(1)}) all-reduce(f32[256]{0:T(256)S(1)} %get-tuple-element.122, f32[256]{0:T(256)S(1)} %get-tuple-element.121), channel_id=1, replica_groups=mesh['wall_0'=4,'wall_1'=2,'surf_0'=4,'surf_1'=8] {'wall_0'}, use_global_device_ids=true, to_apply=%region_3.4 | all-reduce | flops 512 | bytes 4096 | tf_op jit(solution)/shard_map/psum | solution.py:51
  130.4 2.4 %all-reduce.3 = (f32[256]{0:T(256)S(1)}, f32[256]{0:T(256)S(1)}) all-reduce(f32[256]{0:T(256)S(1)} %get-tuple-element.137, f32[256]{0:T(256)S(1)} %get-tuple-element.138), channel_id=1, replica_groups=mesh['wall_0'=4,'wall_1'=2,'surf_0'=4,'surf_1'=8] {'wall_1'}, use_global_device_ids=true, to_apply=%region_4.5 | all-reduce | flops 512 | bytes 4096 | tf_op jit(solution)/shard_map/psum | solution.py:51
  132.9 8.9 %all-reduce.1 = (f32[256]{0:T(256)S(1)}, f32[256]{0:T(256)S(1)}) all-reduce(f32[256]{0:T(256)S(1)} %get-tuple-element.139, f32[256]{0:T(256)S(1)} %get-tuple-element.140), channel_id=1, replica_groups=mesh['wall_0'=4,'wall_1'=2,'surf_0'=4,'surf_1'=8] {'surf_0'}, use_global_device_ids=true, to_apply=%region_5.6 | all-reduce | flops 512 | bytes 4096 | tf_op jit(solution)/shard_map/psum | solution.py:51
  141.8 16.1 %all-reduce = (f32[256]{0:T(256)S(1)}, f32[256]{0:T(256)S(1)}) all-reduce(f32[256]{0:T(256)S(1)} %get-tuple-element.135, f32[256]{0:T(256)S(1)} %get-tuple-element.136), channel_id=1, replica_groups=mesh['wall_0'=4,'wall_1'=2,'surf_0'=4,'surf_1'=8] {'surf_1'}, use_global_device_ids=true, to_apply=%region_6.7 | all-reduce | flops 512 | bytes 4096 | tf_op jit(solution)/shard_map/psum | solution.py:51
  157.9 3.1 %multiply_reduce_fusion = f32[256]{0:T(256)S(1)} fusion(f32[256]{0:T(256)S(1)} %div.17, f32[4,1,320,256]{3,2,0,1:T(8,128)} %copy-done.5, f32[4,1,320,256]{3,2,0,1:T(8,128)} %copy-done.4, f32[4,1,320,256]{3,2,0,1:T(8,128)} %copy-done.3, f32[4,1,320,256]{3,2,0,1:T(8,128)} %copy-done.2, bf16[4,4]{0,1:T(4,128)(2,1)S(1)} %get-tuple-element.158, ...), kind=kLoop, calls=%fused_computation.20 | loop fusion | flops 11796224 | bytes 7866400 | tf_op jit(solution)/shard_map/reduce_sum | solution.py:161
  161.0 9.7 %psum.92 = f32[256]{0:T(256)S(1)} all-reduce(f32[256]{0:T(256)S(1)} %multiply_reduce_fusion), channel_id=1, replica_groups=mesh['wall_0'=4,'wall_1'=2,'surf_0'=4,'surf_1'=8] {'wall_0'}, use_global_device_ids=true, to_apply=%region_13.14 | all-reduce | flops 256 | bytes 2048 | tf_op jit(solution)/shard_map/psum | solution.py:51
  170.8 2.4 %psum.93 = f32[256]{0:T(256)S(1)} all-reduce(f32[256]{0:T(256)S(1)} %psum.92), channel_id=1, replica_groups=mesh['wall_0'=4,'wall_1'=2,'surf_0'=4,'surf_1'=8] {'wall_1'}, use_global_device_ids=true, to_apply=%region_14.15 | all-reduce | flops 256 | bytes 2048 | tf_op jit(solution)/shard_map/psum | solution.py:51
  173.2 10.1 %psum.94 = f32[256]{0:T(256)S(1)} all-reduce(f32[256]{0:T(256)S(1)} %psum.93), channel_id=1, replica_groups=mesh['wall_0'=4,'wall_1'=2,'surf_0'=4,'surf_1'=8] {'surf_0'}, use_global_device_ids=true, to_apply=%region_15.16 | all-reduce | flops 256 | bytes 2048 | tf_op jit(solution)/shard_map/psum | solution.py:51
  183.3 15.1 %psum.95 = f32[256]{0:T(256)S(1)} all-reduce(f32[256]{0:T(256)S(1)} %psum.94), channel_id=1, replica_groups=mesh['wall_0'=4,'wall_1'=2,'surf_0'=4,'surf_1'=8] {'surf_1'}, use_global_device_ids=true, to_apply=%region_16.17 | all-reduce | flops 256 | bytes 2048 | tf_op jit(solution)/shard_map/psum | solution.py:51
  198.5 3.0 %divide_convert_fusion = bf16[4,4,320,256]{3,2,0,1:T(8,128)(2,1)S(1)} fusion(f32[256]{0:T(256)S(1)} %add_sqrt_fusion, f32[256]{0:T(256)S(1)} %div.17, f32[4,1,320,256]{3,2,0,1:T(8,128)} %copy-done.5, f32[4,1,320,256]{3,2,0,1:T(8,128)} %copy-done.4, f32[4,1,320,256]{3,2,0,1:T(8,128)} %copy-done.3, f32[4,1,320,256]{3,2,0,1:T(8,128)} %copy-done.2, ...), kind=kLoop, calls=%fused_computation.19 | loop fusion | flops 11796480 | bytes 10487840 | tf_op jit(solution)/shard_map/convert_element_type | solution.py:163
  201.5 1.7 copy.69
  (91 shorter events, 21.8 us)
Async XLA Ops:
  7.2 96.0 %all-gather.4.cloned.1.call-start = ((), (), s32[]{:S(2)}) async-start(), calls=%async_computation | async-start | bytes 2949120 | tf_op jit(solution)/shard_map/all_gather | solution.py:37
  19.7 23.5 %collective-permute-start = (bf16[4,1,80,256]{3,0,2,1:T(4,128)(2,1)}, bf16[4,1,80,256]{3,0,2,1:T(4,128)(2,1)S(1)}, u32[]{:S(2)}, u32[]{:S(2)}) collective-permute-start(bf16[4,1,80,256]{3,0,2,1:T(4,128)(2,1)} %slice.155), channel_id=1, source_target_pairs={{0,32},{32,64},{64,96},{96,128},{128,160},{160,192},{192,224},{1,3... | collective-permute-start | bytes 491528 | tf_op jit(solution)/shard_map/ppermute | solution.py:26
  23.3 21.0 %collective-permute-start.1 = (bf16[4,1,80,256]{3,0,2,1:T(4,128)(2,1)}, bf16[4,1,80,256]{3,0,2,1:T(4,128)(2,1)}, u32[]{:S(2)}, u32[]{:S(2)}) collective-permute-start(bf16[4,1,80,256]{3,0,2,1:T(4,128)(2,1)} %slice.159), channel_id=1, source_target_pairs={{32,0},{64,32},{96,64},{128,96},{160,128},{192,160},{224,192},{33,... | collective-permute-start | bytes 491528 | tf_op jit(solution)/shard_map/ppermute | solution.py:28
  28.1 18.4 %collective-permute-start.2 = (bf16[1,4,80,256]{3,0,2,1:T(2,128)(2,1)}, bf16[1,4,80,256]{3,0,2,1:T(2,128)(2,1)}, u32[]{:S(2)}, u32[]{:S(2)}) collective-permute-start(bf16[1,4,80,256]{3,0,2,1:T(2,128)(2,1)} %copy.51), channel_id=1, source_target_pairs={{0,1},{1,2},{2,3},{3,4},{4,5},{5,6},{6,7},{7,8},{8,9},{9,10},{10,1... | collective-permute-start | bytes 491528 | tf_op jit(solution)/shard_map/ppermute | solution.py:26
  31.1 17.9 %collective-permute-start.3 = (bf16[1,4,80,256]{3,0,2,1:T(2,128)(2,1)}, bf16[1,4,80,256]{3,0,2,1:T(2,128)(2,1)}, u32[]{:S(2)}, u32[]{:S(2)}) collective-permute-start(bf16[1,4,80,256]{3,0,2,1:T(2,128)(2,1)} %copy.55), channel_id=1, source_target_pairs={{1,0},{2,1},{3,2},{4,3},{5,4},{6,5},{7,6},{8,7},{9,8},{10,9},{11,1... | collective-permute-start | bytes 491528 | tf_op jit(solution)/shard_map/ppermute | solution.py:28
  39.1 23.5 %copy-start.10 = (bf16[4,4,80,320]{3,2,0,1:T(8,128)(2,1)}, bf16[4,4,80,320]{3,2,0,1:T(8,128)(2,1)S(1)}, u32[]{:S(2)}) copy-start(bf16[4,4,80,320]{3,2,0,1:T(8,128)(2,1)S(1)} %copy_bitcast_fusion) | copy-start | bytes 2457604
  39.1 3.4 %copy-start.13 = (bf16[4,4,5,4,1,4,256]{6,5,4,3,2,0,1:T(4,128)(2,1)S(1)}, bf16[4,4,5,4,1,4,256]{6,5,4,3,2,0,1:T(4,128)(2,1)}, u32[]{:S(2)}) copy-start(bf16[4,4,5,4,1,4,256]{6,5,4,3,2,0,1:T(4,128)(2,1)} %get-tuple-element.142) | copy-start | bytes 1966084
  39.6 14.8 %slice-start = ((s8[5898240]{0:T(1024)(128)(4,1)}), s8[4194304]{0:T(1024)(128)(4,1)S(1)}, s32[]{:S(2)}) async-start(s8[5898240]{0:T(1024)(128)(4,1)} %bitcast.241), calls=%async_computation.1 | async-start | bytes 8388608
  44.3 7.2 %copy-start.15 = (s32[1,4]{1,0:T(1,128)S(1)}, s32[1,4]{1,0:T(1,128)}, u32[]{:S(2)}) copy-start(s32[1,4]{1,0:T(1,128)} %param.10) | copy-start | bytes 52
  44.3 10.1 %slice-start.1 = ((s8[5898240]{0:T(1024)(128)(4,1)}), s8[1703936]{0:T(1024)(128)(4,1)S(1)}, s32[]{:S(2)}) async-start(s8[5898240]{0:T(1024)(128)(4,1)} %bitcast.241), calls=%async_computation.2 | async-start | bytes 3407872
  54.4 4.4 %copy-start.1 = (bf16[4,4,320,256]{3,2,0,1:T(8,128)(2,1)S(1)}, bf16[4,4,320,256]{3,2,0,1:T(8,128)(2,1)}, u32[]{:S(2)}) copy-start(bf16[4,4,320,256]{3,2,0,1:T(8,128)(2,1)} %copy_multiply_fusion) | copy-start | bytes 7864324
  62.5 1.2 copy-start.14
  64.4 2.5 %copy-start.11 = (bf16[4,4,80,320]{3,2,0,1:T(8,128)(2,1)S(1)}, bf16[4,4,80,320]{3,2,0,1:T(8,128)(2,1)}, u32[]{:S(2)}) copy-start(bf16[4,4,80,320]{3,2,0,1:T(8,128)(2,1)} %copy-done.10) | copy-start | bytes 2457604
  68.0 1.1 copy-start.8
  69.9 1.1 copy-start.6
  114.0 1.7 copy-start.12
  115.8 1.6 copy-start.9
  116.5 2.8 %copy-start.2 = (f32[4,1,320,256]{3,2,0,1:T(8,128)}, f32[4,1,320,256]{3,2,0,1:T(8,128)S(1)}, u32[]{:S(2)}) copy-start(f32[4,1,320,256]{3,2,0,1:T(8,128)S(1)} %fusion.24) | copy-start | bytes 3932164
  116.5 2.0 copy-start.7
  117.4 2.0 copy-start.3
  117.4 2.6 %copy-start = (bf16[4,4,320,256]{3,2,1,0:T(8,128)(2,1)S(1)}, bf16[4,4,320,256]{3,2,1,0:T(8,128)(2,1)}, u32[]{:S(2)}) copy-start(bf16[4,4,320,256]{3,2,1,0:T(8,128)(2,1)} %param.8) | copy-start | bytes 7864324
  118.6 2.9 %copy-start.4 = (f32[4,1,320,256]{3,2,0,1:T(8,128)}, f32[4,1,320,256]{3,2,0,1:T(8,128)S(1)}, u32[]{:S(2)}) copy-start(f32[4,1,320,256]{3,2,0,1:T(8,128)S(1)} %fusion.28) | copy-start | bytes 3932164
  119.9 1.6 copy-start.5
Sparse Core Ops, SparseCore 0:
  72.5 30.5 all-gather.3
where the time goes:
time: 212 us; the launch traced here: 211 us
  blocking collectives  91.6 us (43%)
  matrix products  40.3 us (19%)
  local copies, waits for them, and re-layouts  25.2 us (12%)
  other arithmetic  20.8 us (10%)
  between operations  14.6 us (7%)
  starting transfers between devices  11.4 us (5%)
  waiting for transfers between devices  6.53 us (3%)
    psum x8, blocking collectives, over_axes(): shard = lax.psum(shard, axis)  73.8 us
    dot_general x31, matrix products, exact_times(): jnp.einsum(form, left.astype(jnp.float32), right.astype(jnp.float32), pre...  29.3 us
    all_gather x1, blocking collectives, carried_in(): pieces = jax.tree.map(lambda part: lax.all_gather(part, axis), value)  17.8 us
    unnamed x6, other arithmetic  8.3 us
    ppermute x2, starting transfers between devices, with_halo(): lax.ppermute(head, axis, [((i + 1) % count, i) for i in range(ends)])  7.55 us
    all_gather x1, waiting for transfers between devices, carried_in(): pieces = jax.tree.map(lambda part: lax.all_gather(part, axis), value)  6.5 us
    unnamed x39, local copies, waits for them, and re-layouts  4.94 us
    dot_general x1, matrix products, per_device(): jnp.einsum('lsgfb,lsgfr->lsbr', lifting, neighbours, preferred_element_ty...  4.35 us
  transfers between devices with their start and end apart: 5, of which 1 were waited for; matrix products, arithmetic and copies ran while one was open for 12% of the time, Pallas kernels for 0%

commit v1 on v0

v1 whole, which is shorter than its diff:
```python
import functools

import jax
import jax.numpy as jnp
from jax import lax
from jax.experimental import pallas as pl
from jax.experimental.pallas import tpu as pltpu
from jax.sharding import Mesh
from jax.sharding import PartitionSpec as P

BLOCK = 320
FACE = 80
LINES_HERE = 4
SEGMENT = 4
MOVING = 3
R = 256
HALF = 128
WALL = ("y", "core")
SURF = ("x", "z")
F32 = jnp.float32
BF16 = jnp.bfloat16
EXACT = lax.Precision.HIGHEST
VMEM = pltpu.VMEM
SMEM = pltpu.SMEM

AT_WALL, AT_CORE, AT_Y, AT_ODD, AT_LENGTH, AT_NORTH = 0, 1, 2, 3, 4, 8


def in_vmem():
    return pl.BlockSpec(memory_space=VMEM)


def in_smem():
    return pl.BlockSpec(memory_space=SMEM)


def living_here(info, line):
    return jnp.clip(info[AT_LENGTH + line] - SEGMENT * info[AT_WALL], 0, SEGMENT)


def shortest_line(info):
    at = jnp.int32(3)
    for line in (2, 1, 0):
        at = jnp.where(info[AT_LENGTH + line] == 1, line, at)
    return at


def line_in_slot(slot, short):
    return jnp.where(slot == MOVING, short, slot + (slot >= short).astype(jnp.int32))


def list_living(info, listed):
    short = shortest_line(info)
    count = jnp.int32(0)
    for slot in range(LINES_HERE):
        here = living_here(info, line_in_slot(slot, short))
        for position in range(SEGMENT):
            listed[count] = slot * SEGMENT + position
            count = count + (position < here).astype(jnp.int32)
    return count


def for_living(info, listed, body, together=2):
    count = list_living(info, listed)
    short = shortest_line(info)

    @pl.loop(0, (count + together - 1) // together)
    def _(trip):
        for part in range(together):
            entry = listed[jnp.minimum(trip * together + part, count - 1)]
            slot = entry // SEGMENT
            body(slot, line_in_slot(slot, short), entry % SEGMENT)


def face_rows(first_face):
    row = lax.broadcasted_iota(jnp.int32, (2 * FACE, BLOCK), 0)
    column = lax.broadcasted_iota(jnp.int32, (2 * FACE, BLOCK), 1)
    second = (row >= FACE).astype(jnp.int32)
    entry = row - FACE * second
    if first_face == 0:
        source = 4 * entry + 3 * second
    else:
        source = 16 * (entry >> 2) + (entry & 3) + 12 * second
    return (column == source).astype(BF16)


def pick(rows, values):
    return jnp.dot(rows, values, preferred_element_type=F32).astype(BF16)


def a_face(block, end):
    return jnp.concatenate([block[64 * v + 16 * end : 64 * v + 16 * end + 16] for v in range(5)], axis=0)


def split_exactly(values):
    high = values.astype(BF16)
    low = (values - high.astype(F32)).astype(BF16)
    return high, low


def transposed_times(left, right):
    return lax.dot_general(left, right, (((0,), (0,)), ((), ())), preferred_element_type=F32)


def mapped(matrix, state):
    return jnp.dot(matrix, state, precision=EXACT, preferred_element_type=F32)


def edges_kernel(info, vector, over_core, over_y, over_pair, over_next):
    core, odd = info[AT_CORE], info[AT_ODD]
    short = shortest_line(info)
    rows = face_rows(0)
    zero = jnp.zeros((FACE, R), BF16)
    for slot in range(MOVING):
        line = line_in_slot(slot, short)
        here = living_here(info, line)
        down = jnp.where(here > 0, pick(rows[:FACE], vector[line, 0]), zero)
        up = jnp.where(here > SEGMENT - 1, pick(rows[FACE:], vector[line, SEGMENT - 1]), zero)
        over_core[slot] = jnp.where(core == 0, up, down)
        over_y[slot] = jnp.where(core == 0, down, up)
    first, last = living_here(info, 0), living_here(info, LINES_HERE - 1)
    for position in range(SEGMENT):
        west = jnp.where(position < first, a_face(vector[0, position], 0), zero)
        east = jnp.where(position < last, a_face(vector[LINES_HERE - 1, position], 3), zero)
        over_pair[position] = jnp.where(odd == 0, east, west)
        over_next[position] = jnp.where(odd == 0, west, east)


def maps_kernel(info, lifting_below, inverse, steps, prefixes, whole):
    short = shortest_line(info)
    for slot in range(MOVING):
        line = line_in_slot(slot, short)
        here = living_here(info, line)
        so_far = None
        for position in range(SEGMENT):
            step = lax.dot_general(
                inverse[line, position],
                lifting_below[line, position, 0],
                (((1,), (1,)), ((), ())),
                preferred_element_type=F32,
            )
            step = jnp.where(position < here, -step, 0.0)
            steps[slot, position] = step
            so_far = step if position == 0 else jnp.dot(step, so_far, precision=EXACT, preferred_element_type=F32)
            prefixes[slot, position] = so_far
        whole[slot] = jnp.concatenate([so_far, jnp.zeros((FACE, HALF - FACE), F32)], axis=1)


def diagonal_kernel(info, vector, diagonal, map_here, map_beside, product, traces, chip_map, listed):
    core = info[AT_CORE]
    for slot in range(MOVING):
        first = jnp.where(core == 0, map_here[slot], map_beside[slot])
        second = jnp.where(core == 0, map_beside[slot], map_here[slot])
        chip_map[slot] = mapped(second[:, :FACE], first)
    wall_rows, b_rows = face_rows(0), face_rows(4)
    for line in range(LINES_HERE):
        here = living_here(info, line)
        for position in range(SEGMENT):

            @pl.when(position >= here)
            def _():
                traces[line, position] = jnp.zeros((6, FACE, R), BF16)

    def body(slot, line, position):
        values = vector[line, position]
        product[line, position] = jnp.dot(diagonal[line, position], values, preferred_element_type=F32)
        wall_faces = pick(wall_rows, values)
        b_faces = pick(b_rows, values)
        traces[line, position, 0] = wall_faces[:FACE]
        traces[line, position, 1] = wall_faces[FACE:]
        traces[line, position, 2] = a_face(values, 0)
        traces[line, position, 3] = a_face(values, 3)
        traces[line, position, 4] = b_faces[:FACE]
        traces[line, position, 5] = b_faces[FACE:]

    for_living(info, listed, body)


def product_kernel(
    info,
    traces,
    over_core,
    over_y,
    over_pair,
    over_next,
    lifting,
    inverse,
    steps,
    product_in,
    product,
    carries,
    outgoing,
    listed,
    driven,
):
    core, odd = info[AT_CORE], info[AT_ODD]
    short = shortest_line(info)
    driven[...] = jnp.zeros_like(driven)
    zero = jnp.zeros((FACE, R), BF16)

    def body(slot, line, position):
        wall_slot = jnp.minimum(slot, MOVING - 1)
        moving = slot < MOVING
        from_core = jnp.where(moving, over_core[wall_slot], zero)
        from_y = jnp.where(moving, over_y[wall_slot], zero)
        below_edge = jnp.where(core == 0, from_y, from_core)
        above_edge = jnp.where(core == 0, from_core, from_y)
        below = jnp.where(position == 0, below_edge, traces[line, jnp.maximum(position - 1, 0), 1])
        above = jnp.where(
            position == SEGMENT - 1, above_edge, traces[line, jnp.minimum(position + 1, SEGMENT - 1), 0]
        )
        west_edge = jnp.where(odd == 0, over_next[position], over_pair[position])
        east_edge = jnp.where(odd == 0, over_pair[position], over_next[position])
        west = jnp.where(line == 0, west_edge, traces[jnp.maximum(line - 1, 0), position, 3])
        east = jnp.where(
            line == LINES_HERE - 1, east_edge, traces[jnp.minimum(line + 1, LINES_HERE - 1), position, 2]
        )
        north_line = info[AT_NORTH + line]
        south_line = jnp.int32(0)
        for other in range(1, LINES_HERE):
            south_line = jnp.where(info[AT_NORTH + other] == line, other, south_line)
        south = traces[south_line, position, 5]
        north = traces[north_line, position, 4]
        neighbours = jnp.concatenate([below, above, west, east, south, north], axis=0)
        blocks = lifting[line, position].reshape(6 * FACE, BLOCK)
        total = product_in[line, position] + transposed_times(blocks, neighbours)
        product[line, position] = total
        high, low = split_exactly(total)
        here = jnp.dot(inverse[line, position], jnp.concatenate([high, low], axis=1), preferred_element_type=F32)
        driven[slot, position] = here[:, :R] + here[:, R:]

    for_living(info, listed, body)
    for slot in range(MOVING):
        carried = driven[slot, 0]
        for position in range(1, SEGMENT):
            carries[slot, position - 1] = carried
            carried = driven[slot, position] + jnp.dot(
                steps[slot, position], carried, precision=EXACT, preferred_element_type=F32
            )
        outgoing[slot] = carried


def chip_kernel(info, mine, other, map_here, map_beside, chip):
    core = info[AT_CORE]
    for slot in range(MOVING):
        own, away = mine[slot], other[slot]
        first_value = jnp.where(core == 0, own[:, :HALF], away[:, HALF:])
        second_value = jnp.where(core == 0, away[:, :HALF], own[:, HALF:])
        second_map = jnp.where(core == 0, map_beside[slot], map_here[slot])
        chip[slot] = mapped(second_map[:, :FACE], first_value) + second_value


def arriving_kernel(info, one, two, three, nearest_map, next_map, arriving):
    for slot in range(MOVING):
        value = two[slot] + mapped(next_map[slot][:, :FACE], three[slot])
        arriving[slot] = one[slot] + mapped(nearest_map[slot][:, :FACE], value)


def eliminate_kernel(
    info,
    vector,
    product,
    lifting_below,
    prefixes,
    map_beside,
    carries,
    mine,
    other,
    below_out,
    eliminated,
    tiles,
    listed,
    entering,
):
    core = info[AT_CORE]
    short = shortest_line(info)
    entering[...] = jnp.zeros_like(entering)
    for slot in range(MOVING):
        left = jnp.where(core == 0, mine[slot], other[slot])
        right = jnp.where(core == 0, other[slot], mine[slot])
        value = jnp.concatenate([left, right], axis=1)
        passed = mapped(map_beside[slot][:, :FACE], value) + below_out[slot]
        value = jnp.where(core == 0, value, passed)
        entering[slot, 0] = value
        stacked = prefixes[slot].reshape(SEGMENT * FACE, FACE)[: (SEGMENT - 1) * FACE]
        moved = mapped(stacked, value)
        for position in range(1, SEGMENT):
            entering[slot, position] = carries[slot, position - 1] + moved[(position - 1) * FACE : position * FACE]

    count = list_living(info, listed)
    nothing = jnp.zeros((8, R), F32)

    def of(trip):
        entry = listed[trip]
        slot = entry // SEGMENT
        return slot, line_in_slot(slot, short), entry % SEGMENT

    def partial(values):
        return values.reshape(BLOCK // 8, 8, R).sum(axis=0)

    def correct(slot, line, position):
        high, low = split_exactly(entering[slot, position])
        block = lifting_below[line, position, 0]
        correction = transposed_times(jnp.concatenate([block, block], axis=0), jnp.concatenate([high, low], axis=0))
        eliminated[line, position] = product[line, position] - correction

    for_living(info, listed, correct)

    def products(trip, sums):
        _, line, position = of(trip)
        masked, value = vector[line, position].astype(F32), eliminated[line, position]
        return sums[0] + partial(masked * value), sums[1] + partial(masked * masked)

    cross, square = lax.fori_loop(0, count, products, (nothing, nothing))
    cross = cross.sum(axis=0, keepdims=True)
    square = square.sum(axis=0, keepdims=True)
    share = jnp.where(square > 0, cross / square, 0.0)

    def left_over(trip, total):
        _, line, position = of(trip)
        rest = eliminated[line, position] - share * vector[line, position].astype(F32)
        return total + partial(rest * rest)

    rest = lax.fori_loop(0, count, left_over, nothing).sum(axis=0, keepdims=True)
    pieces = [part[:, at : at + HALF] for part in (cross, square, rest) for at in (0, HALF)]
    tile = jnp.concatenate(pieces + [jnp.zeros((2, HALF), F32)], axis=0)
    for copy in range(tiles.shape[0]):
        tiles[copy] = tile


def merged(tiles):
    cross, square, rest = tiles[:, 0:2], tiles[:, 2:4], tiles[:, 4:6]
    all_cross, all_square = cross.sum(axis=0), square.sum(axis=0)
    own = jnp.where(square > 0, cross / square, 0.0)
    ratio = all_cross / all_square
    away = jnp.where(square > 0, own - ratio[None], 0.0)
    all_rest = (rest + (square * away) * away).sum(axis=0)
    return all_cross, all_square, all_rest, ratio


def merge_kernel(tiles_in, tiles):
    cross, square, rest, _ = merged(tiles_in[...])
    tile = jnp.concatenate([cross, square, rest, jnp.zeros((2, HALF), F32)], axis=0)
    for copy in range(tiles.shape[0]):
        tiles[copy] = tile


def finish_kernel(entries, info, tiles, vector, eliminated, basis, coefs, held, sems):
    _, _, rest, ratio = merged(tiles[...])
    spread = jnp.sqrt(rest / entries + 1e-06)
    ratio = jnp.concatenate([ratio[0:1], ratio[1:2]], axis=1)
    spread = jnp.concatenate([spread[0:1], spread[1:2]], axis=1)
    coefs[...] = jnp.concatenate([ratio, spread], axis=0)
    scale = 1.0 / spread
    copies = []
    for line in range(LINES_HERE):
        here = living_here(info, line)

        @pl.loop(0, here)
        def _(position):
            masked = vector[line, position].astype(F32)
            held[line, position] = ((eliminated[line, position] - ratio * masked) * scale).astype(BF16)

        @pl.loop(here, SEGMENT)
        def _(position):
            held[line, position] = jnp.zeros((BLOCK, R), BF16)

        copy = pltpu.make_async_copy(held.at[line], basis.at[line], sems.at[line])
        copy.start()
        copies.append(copy)
    for copy in copies:
        copy.wait()


def call(kernel, outs, ins, scratch=(), limit=12, flops=0, moved=0, out_specs=None):
    return pl.pallas_call(
        kernel,
        out_shape=outs,
        in_specs=[in_smem() if arg.dtype == jnp.int32 else in_vmem() for arg in ins],
        out_specs=out_specs or jax.tree.map(lambda _: in_vmem(), outs),
        scratch_shapes=list(scratch),
        compiler_params=pltpu.CompilerParams(vmem_limit_bytes=limit * 2**20),
        cost_estimate=pl.CostEstimate(flops=flops, bytes_accessed=moved, transcendentals=0),
        name=getattr(kernel, "__name__", "finish_kernel"),
    )(*ins)


def shaped(*shape, dtype=F32):
    return jax.ShapeDtypeStruct(shape, dtype)


LISTED = pltpu.SMEM((LINES_HERE * SEGMENT + 1,), jnp.int32)


def per_device(vector, lengths, north_of, diagonal, lifting, inverse_rows):
    wall, core, y = lax.axis_index(WALL), lax.axis_index("core"), lax.axis_index("y")
    odd = lax.axis_index("z") % 2
    info = jnp.concatenate([jnp.stack([wall, core, y, odd]).astype(jnp.int32), lengths, north_of[0]])
    edge = shaped(MOVING, FACE, R, dtype=BF16)
    side = shaped(SEGMENT, FACE, R, dtype=BF16)
    over_core, over_y, over_pair, over_next = call(edges_kernel, (edge, edge, side, side), (info, vector))
    walls, surfs = lax.axis_size(WALL), lax.axis_size(SURF)
    swap = [(0, 1), (1, 0)]
    over_core = lax.ppermute(over_core, "core", swap)
    rungs = [(i, i + 1) for i in range(1, walls - 1, 2)]
    over_y = lax.ppermute(over_y, WALL, rungs + [(b, a) for a, b in rungs])
    over_pair = lax.ppermute(over_pair, SURF, [(i, i ^ 1) for i in range(surfs)])
    nexts = [(i, (i + 1) % surfs) for i in range(1, surfs, 2)]
    over_next = lax.ppermute(over_next, SURF, nexts + [(b, a) for a, b in nexts])

    lower = lifting[:, :, 0:1]
    steps, prefixes, whole = call(
        maps_kernel,
        (shaped(MOVING, SEGMENT, FACE, FACE), shaped(MOVING, SEGMENT, FACE, FACE), shaped(MOVING, FACE, HALF)),
        (info, lower, inverse_rows),
        flops=10**8,
        moved=2 * 10**6,
    )
    map_beside = lax.ppermute(whole, "core", swap)
    product, traces, chip_map = call(
        diagonal_kernel,
        (
            shaped(LINES_HERE, SEGMENT, BLOCK, R),
            shaped(LINES_HERE, SEGMENT, 6, FACE, R, dtype=BF16),
            shaped(MOVING, FACE, HALF),
        ),
        (info, vector, diagonal, whole, map_beside),
        (LISTED,),
        flops=2 * 10**9,
        moved=14 * 10**6,
    )
    ranks = lax.axis_size("y")

    def up_chips(value, far):
        return lax.ppermute(value, "y", [(i, i + far) for i in range(ranks - far)])

    maps_below = [up_chips(chip_map, far) for far in (1, 2)]
    product, carries, outgoing = call(
        product_kernel,
        (
            shaped(LINES_HERE, SEGMENT, BLOCK, R),
            shaped(MOVING, SEGMENT - 1, FACE, R),
            shaped(MOVING, FACE, R),
        ),
        (info, traces, over_core, over_y, over_pair, over_next, lifting, inverse_rows, steps, product),
        (LISTED, pltpu.VMEM((LINES_HERE, SEGMENT, FACE, R), F32)),
        flops=2 * 10**9,
        moved=20 * 10**6,
    )
    beside = lax.ppermute(outgoing, "core", swap)
    chip = call(chip_kernel, shaped(MOVING, FACE, HALF), (info, outgoing, beside, whole, map_beside), flops=10**7)
    from_chips = [up_chips(chip, far) for far in range(1, ranks)]
    arriving = call(arriving_kernel, shaped(MOVING, FACE, HALF), (info, *from_chips, *maps_below), flops=10**7)
    arriving_beside = lax.ppermute(arriving, "core", swap)
    eliminated, tiles = call(
        eliminate_kernel,
        (shaped(LINES_HERE, SEGMENT, BLOCK, R), shaped(surfs, 8, HALF)),
        (info, vector, product, lower, prefixes, map_beside, carries, arriving, arriving_beside, beside),
        (LISTED, pltpu.VMEM((LINES_HERE, SEGMENT, FACE, R), F32)),
        flops=10**9,
        moved=10**7,
    )
    tiles = lax.all_to_all(tiles, SURF, 0, 0, tiled=True)
    tiles = call(merge_kernel, shaped(walls, 8, HALF), (tiles,))
    tiles = lax.all_to_all(tiles, WALL, 0, 0, tiled=True)
    entries = LINES_HERE * SEGMENT * BLOCK * walls * surfs
    return call(
        functools.partial(finish_kernel, entries),
        (shaped(LINES_HERE, SEGMENT, BLOCK, R, dtype=BF16), shaped(2, R)),
        (info, tiles, vector, eliminated),
        (pltpu.VMEM((LINES_HERE, SEGMENT, BLOCK, R), BF16), pltpu.SemaphoreType.DMA((LINES_HERE,))),
        out_specs=(pl.BlockSpec(memory_space=pl.ANY), in_vmem()),
    )


def solution(mesh):
    split = Mesh(mesh.devices.reshape(4, 2, 4, 8), ("y", "core", "x", "z"))
    placed = (
        P(SURF, WALL, None, None),
        P(SURF),
        P(SURF, None),
        P(SURF, WALL, None, None),
        P(SURF, WALL, None, None, None),
        P(SURF, WALL, None, None),
    )
    return jax.shard_map(
        per_device,
        mesh=split,
        in_specs=placed,
        out_specs=(P(SURF, WALL, None, None), P()),
        check_vma=False,
    )
```

time: 212 us -> 89.4 us (0.42)
  the two profiles are of different devices: /device:TPU:10 before, /device:TPU:1 now
where the time goes in v1:
time: 89.4 us; the launch traced here: 89.1 us
  Pallas kernels  25.4 us (28%)
  blocking collectives  25.1 us (28%)
  starting transfers between devices  24.4 us (27%)
  local copies, waits for them, and re-layouts  7.69 us (9%)
  waiting for transfers between devices  5.63 us (6%)
    pallas_call x9, Pallas kernels, call(): pl.pallas_call(kernel, out_shape=outs, in_specs=[in_smem() if arg.dtype =...  25.4 us
    all_to_all x1, blocking collectives, per_device(): tiles = lax.all_to_all(tiles, SURF, 0, 0, tiled=True)  13.8 us
    all_to_all x1, blocking collectives, per_device(): tiles = lax.all_to_all(tiles, WALL, 0, 0, tiled=True)  11.2 us
    ppermute x5, starting transfers between devices, up_chips(): return lax.ppermute(value, 'y', [(i, i + far) for i in range(ranks - far)])  9.45 us
    ppermute x1, starting transfers between devices, per_device(): lax.ppermute(over_next, SURF, nexts + [(b, a) for a, b in nexts])  6.86 us
    ppermute x5, waiting for transfers between devices, up_chips(): return lax.ppermute(value, 'y', [(i, i + far) for i in range(ranks - far)])  4.64 us
    unnamed x14, local copies, waits for them, and re-layouts  4.54 us
    ppermute x1, starting transfers between devices, per_device(): map_beside = lax.ppermute(whole, 'core', swap)  3.32 us
  transfers between devices with their start and end apart: 12, of which 3 were waited for; matrix products, arithmetic and copies ran while one was open for 0% of the time, Pallas kernels for 7%

profile of v1, /device:TPU:1, one launch (start us, length us, event | category | flops | bytes accessed | tf_op | source)
XLA Modules:
  0.0 89.1 jit_solution(18152690409363822025)
XLA Ops:
  0.6 0.0 copy-start
  0.6 2.4 %slice.3.lifting_below = bf16[4,4,1,80,320]{4,3,2,1,0:T(8,128)(2,1)} slice(bf16[4,4,6,80,320]{4,3,2,1,0:T(8,128)(2,1)} %lifting.1), slice={[0:4], [0:4], [0:1], [0:80], [0:320]} | slice | bytes 1638400 | tf_op jit(solution)/shard_map/slice | solution.py:411
  3.1 0.7 concatenate.3.info
  3.8 1.2 %copy-done.1 = bf16[4,4,1,80,320]{4,3,2,1,0:T(8,128)(2,1)S(1)} copy-done((bf16[4,4,1,80,320]{4,3,2,1,0:T(8,128)(2,1)S(1)}, bf16[4,4,1,80,320]{4,3,2,1,0:T(8,128)(2,1)}, u32[]{:S(2)}) %copy-start.1) | copy-done | bytes 819224
  5.0 1.2 %copy-done.4 = bf16[4,4,80,320]{3,2,1,0:T(8,128)(2,1)S(1)} copy-done((bf16[4,4,80,320]{3,2,1,0:T(8,128)(2,1)S(1)}, bf16[4,4,80,320]{3,2,1,0:T(8,128)(2,1)}, u32[]{:S(2)}) %copy-start.4) | copy-done | bytes 819224
  6.2 2.3 %maps_kernel.1 = (f32[3,4,80,80]{3,2,1,0:T(8,128)S(1)}, f32[3,4,80,80]{3,2,1,0:T(8,128)S(1)}, f32[3,80,128]{2,1,0:T(8,128)S(1)}) custom-call(s32[12]{0:T(128)S(1)} %concatenate.3.info, bf16[4,4,1,80,320]{4,3,2,1,0:T(8,128)(2,1)S(1)} %copy-done.1, bf16[4,4,80,320]{3,2,1,0:T(8,128)(2,1)S(1)} %copy-done.4), custom_call_target="tpu_custom_call" | custom-call | flops 100000000 | bytes 2000000 | tf_op jit(solution)/shard_map/maps_kernel/pallas_call | solution.py:376
  8.6 0.0 copy-start.3
  8.6 0.0 copy-start.5
  8.6 3.3 %collective-permute-start = (f32[3,80,128]{2,1,0:T(8,128)S(1)}, f32[3,80,128]{2,1,0:T(8,128)S(1)}, u32[]{:S(2)}, u32[]{:S(2)}) collective-permute-start(f32[3,80,128]{2,1,0:T(8,128)S(1)} %get-tuple-element.17.map_here), channel_id=1, source_target_pairs={{0,32},{32,0},{1,33},{33,1},{2,34},{34,2},{3,35},{35,3},{4,36},{36... | collective-permute-start | bytes 368648 | tf_op jit(solution)/shard_map/ppermute | solution.py:419
  11.9 0.0 copy-done
  11.9 0.9 %edges_kernel.1 = (bf16[3,80,256]{2,1,0:T(8,128)(2,1)S(1)}, bf16[3,80,256]{2,1,0:T(8,128)(2,1)S(1)}, bf16[4,80,256]{2,1,0:T(8,128)(2,1)S(1)}, bf16[4,80,256]{2,1,0:T(8,128)(2,1)S(1)}) custom-call(s32[12]{0:T(128)S(1)} %concatenate.3.info, bf16[4,4,320,256]{3,2,1,0:T(8,128)(2,1)S(1)} %copy-done), custom_call_target="tpu_custom_call" | custom-call | tf_op jit(solution)/shard_map/edges_kernel/pallas_call | solution.py:376
  12.8 0.1 collective-permute-start.1
  12.9 2.0 %collective-permute-start.2 = (bf16[3,80,256]{2,1,0:T(8,128)(2,1)S(1)}, bf16[3,80,256]{2,1,0:T(8,128)(2,1)S(1)}, u32[]{:S(2)}, u32[]{:S(2)}) collective-permute-start(bf16[3,80,256]{2,1,0:T(8,128)(2,1)S(1)} %get-tuple-element.20), channel_id=1, source_target_pairs={{32,64},{96,128},{160,192},{64,32},{128,96},{192,160},{33,65},{97,... | collective-permute-start | bytes 368648 | tf_op jit(solution)/shard_map/ppermute | solution.py:406
  14.9 1.7 %collective-permute-start.3 = (bf16[4,80,256]{2,1,0:T(8,128)(2,1)S(1)}, bf16[4,80,256]{2,1,0:T(8,128)(2,1)S(1)}, u32[]{:S(2)}, u32[]{:S(2)}) collective-permute-start(bf16[4,80,256]{2,1,0:T(8,128)(2,1)S(1)} %get-tuple-element.21), channel_id=1, source_target_pairs={{0,1},{1,0},{2,3},{3,2},{4,5},{5,4},{6,7},{7,6},{8,9},{9,8},{10,11... | collective-permute-start | bytes 491528 | tf_op jit(solution)/shard_map/ppermute | solution.py:407
  16.6 6.9 %collective-permute-start.4 = (bf16[4,80,256]{2,1,0:T(8,128)(2,1)S(1)}, bf16[4,80,256]{2,1,0:T(8,128)(2,1)S(1)}, u32[]{:S(2)}, u32[]{:S(2)}) collective-permute-start(bf16[4,80,256]{2,1,0:T(8,128)(2,1)S(1)} %get-tuple-element.22), channel_id=1, source_target_pairs={{1,2},{3,4},{5,6},{7,8},{9,10},{11,12},{13,14},{15,16},{17,18},{19... | collective-permute-start | bytes 491528 | tf_op jit(solution)/shard_map/ppermute | solution.py:409
  23.5 0.0 collective-permute-done.map_beside
  23.5 2.1 %copy-done.6 = bf16[4,4,320,320]{3,2,1,0:T(8,128)(2,1)S(1)} copy-done((bf16[4,4,320,320]{3,2,1,0:T(8,128)(2,1)S(1)}, bf16[4,4,320,320]{3,2,1,0:T(8,128)(2,1)}, u32[]{:S(2)}) %copy-start.6) | copy-done | bytes 3276824
  25.6 4.1 %diagonal_kernel.1 = (f32[4,4,320,256]{3,2,1,0:T(8,128)S(1)}, bf16[4,4,6,80,256]{4,3,2,1,0:T(8,128)(2,1)S(1)}, f32[3,80,128]{2,1,0:T(8,128)S(1)}) custom-call(s32[12]{0:T(128)S(1)} %concatenate.3.info, bf16[4,4,320,256]{3,2,1,0:T(8,128)(2,1)S(1)} %copy-done, bf16[4,4,320,320]{3,2,1,0:T(8,128)(2,1)S(1)} %copy-done.6, ...), custom_call_target="tpu_custom_call" | custom-call | flops 2000000000 | bytes 14000000 | tf_op jit(solution)/shard_map/diagonal_kernel/pallas_call | solution.py:376
  29.7 0.0 collective-permute-done.1.over_core
  29.7 0.0 collective-permute-done.2.over_y
  29.7 0.0 collective-permute-done.3.over_pair
  29.8 0.0 collective-permute-done.4.over_next
  29.8 0.0 copy-done.3
  29.8 0.0 copy-done.5
  29.8 0.0 copy-start.2
  29.8 7.8 %product_kernel.1 = (f32[4,4,320,256]{3,2,1,0:T(8,128)S(1)}, f32[3,3,80,256]{3,2,1,0:T(8,128)S(1)}, f32[3,80,256]{2,1,0:T(8,128)S(1)}) custom-call(s32[12]{0:T(128)S(1)} %concatenate.3.info, bf16[4,4,6,80,256]{4,3,2,1,0:T(8,128)(2,1)S(1)} %get-tuple-element.18.traces, bf16[3,80,256]{2,1,0:T(8,128)(2,1)S(1)} %collective-permute-done.1.over_core, ...), custom_call_target="tpu_custom_call" | custom-call | flops 2000000000 | bytes 20000000 | tf_op jit(solution)/shard_map/product_kernel/pallas_call | solution.py:376
  37.6 0.1 collective-permute-start.5
  37.7 4.3 %collective-permute-start.10 = (f32[3,80,128]{2,1,0:T(8,128)S(1)}, f32[3,80,128]{2,1,0:T(8,128)S(1)}, u32[]{:S(2)}, u32[]{:S(2)}) collective-permute-start(f32[3,80,128]{2,1,0:T(8,128)S(1)} %get-tuple-element.29), channel_id=1, source_target_pairs={{0,128},{64,192},{1,129},{65,193},{2,130},{66,194},{3,131},{67,195... | collective-permute-start | bytes 368648 | tf_op jit(solution)/shard_map/ppermute | solution.py:435
  42.0 1.3 %collective-permute-start.9 = (f32[3,80,128]{2,1,0:T(8,128)S(1)}, f32[3,80,128]{2,1,0:T(8,128)S(1)}, u32[]{:S(2)}, u32[]{:S(2)}) collective-permute-start(f32[3,80,128]{2,1,0:T(8,128)S(1)} %get-tuple-element.29), channel_id=1, source_target_pairs={{0,64},{64,128},{128,192},{1,65},{65,129},{129,193},{2,66},{66,130... | collective-permute-start | bytes 368648 | tf_op jit(solution)/shard_map/ppermute | solution.py:435
  43.3 0.0 collective-permute-done.5.other.below_out
  43.3 0.8 chip_kernel.1
  44.1 1.3 %collective-permute-start.8 = (f32[3,80,128]{2,1,0:T(8,128)S(1)}, f32[3,80,128]{2,1,0:T(8,128)S(1)}, u32[]{:S(2)}, u32[]{:S(2)}) collective-permute-start(f32[3,80,128]{2,1,0:T(8,128)S(1)} %chip_kernel.1), channel_id=1, source_target_pairs={{0,192},{1,193},{2,194},{3,195},{4,196},{5,197},{6,198},{7,199},{8... | collective-permute-start | bytes 368648 | tf_op jit(solution)/shard_map/ppermute | solution.py:435
  45.4 1.3 %collective-permute-start.7 = (f32[3,80,128]{2,1,0:T(8,128)S(1)}, f32[3,80,128]{2,1,0:T(8,128)S(1)}, u32[]{:S(2)}, u32[]{:S(2)}) collective-permute-start(f32[3,80,128]{2,1,0:T(8,128)S(1)} %chip_kernel.1), channel_id=1, source_target_pairs={{0,128},{64,192},{1,129},{65,193},{2,130},{66,194},{3,131},{67,195... | collective-permute-start | bytes 368648 | tf_op jit(solution)/shard_map/ppermute | solution.py:435
  46.7 1.3 %collective-permute-start.6 = (f32[3,80,128]{2,1,0:T(8,128)S(1)}, f32[3,80,128]{2,1,0:T(8,128)S(1)}, u32[]{:S(2)}, u32[]{:S(2)}) collective-permute-start(f32[3,80,128]{2,1,0:T(8,128)S(1)} %chip_kernel.1), channel_id=1, source_target_pairs={{0,64},{64,128},{128,192},{1,65},{65,129},{129,193},{2,66},{66,130... | collective-permute-start | bytes 368648 | tf_op jit(solution)/shard_map/ppermute | solution.py:435
  48.0 0.0 collective-permute-done.10.next_map
  48.0 0.0 collective-permute-done.9.nearest_map
  48.1 3.0 %collective-permute-done.8.three = f32[3,80,128]{2,1,0:T(8,128)S(1)} collective-permute-done((f32[3,80,128]{2,1,0:T(8,128)S(1)}, f32[3,80,128]{2,1,0:T(8,128)S(1)}, u32[]{:S(2)}, u32[]{:S(2)}) %collective-permute-start.8) | collective-permute-done | bytes 122912 | tf_op jit(solution)/shard_map/ppermute | solution.py:435
  51.0 0.0 collective-permute-done.7.two
  51.0 1.7 %collective-permute-done.6.one = f32[3,80,128]{2,1,0:T(8,128)S(1)} collective-permute-done((f32[3,80,128]{2,1,0:T(8,128)S(1)}, f32[3,80,128]{2,1,0:T(8,128)S(1)}, u32[]{:S(2)}, u32[]{:S(2)}) %collective-permute-start.6) | collective-permute-done | bytes 122912 | tf_op jit(solution)/shard_map/ppermute | solution.py:435
  52.7 1.0 %arriving_kernel.1.mine = f32[3,80,128]{2,1,0:T(8,128)S(1)} custom-call(s32[12]{0:T(128)S(1)} %concatenate.3.info, f32[3,80,128]{2,1,0:T(8,128)S(1)} %collective-permute-done.6.one, f32[3,80,128]{2,1,0:T(8,128)S(1)} %collective-permute-done.7.two, f32[3,80,128]{2,1,0:T(8,128)S(1)} %collective-permute-done.8.three, ...), custom_call_target="tpu_custom_call" | custom-call | flops 10000000 | tf_op jit(solution)/shard_map/arriving_kernel/pallas_call | solution.py:376
  53.7 0.9 %collective-permute-start.11 = (f32[3,80,128]{2,1,0:T(8,128)S(1)}, f32[3,80,128]{2,1,0:T(8,128)S(1)}, u32[]{:S(2)}, u32[]{:S(2)}) collective-permute-start(f32[3,80,128]{2,1,0:T(8,128)S(1)} %arriving_kernel.1.mine), channel_id=1, source_target_pairs={{0,32},{32,0},{1,33},{33,1},{2,34},{34,2},{3,35},{35,3},{4,36},{36... | collective-permute-start | bytes 368648 | tf_op jit(solution)/shard_map/ppermute | solution.py:454
  54.6 1.0 %collective-permute-done.11.other = f32[3,80,128]{2,1,0:T(8,128)S(1)} collective-permute-done((f32[3,80,128]{2,1,0:T(8,128)S(1)}, f32[3,80,128]{2,1,0:T(8,128)S(1)}, u32[]{:S(2)}, u32[]{:S(2)}) %collective-permute-start.11) | collective-permute-done | bytes 122912 | tf_op jit(solution)/shard_map/ppermute | solution.py:454
  55.6 0.0 copy-done.2
  55.6 5.4 %eliminate_kernel.1 = (f32[4,4,320,256]{3,2,1,0:T(8,128)S(1)}, f32[32,8,128]{2,1,0:T(8,128)S(1)}) custom-call(s32[12]{0:T(128)S(1)} %concatenate.3.info, bf16[4,4,320,256]{3,2,1,0:T(8,128)(2,1)S(1)} %copy-done, f32[4,4,320,256]{3,2,1,0:T(8,128)S(1)} %get-tuple-element.25.product, bf16[4,4,1,80,320]{4,3,2,1,0:T(8,128)(2,1)S(1)} %copy-done.2, ...), custom_call_target="tpu_custom_call" | custom-call | flops 1000000000 | bytes 10000000 | tf_op jit(solution)/shard_map/eliminate_kernel/pallas_call | solution.py:376
  61.0 13.8 %all_to_all.10.tiles_in = f32[32,8,128]{2,1,0:T(8,128)S(1)} all-to-all(f32[32,8,128]{2,1,0:T(8,128)S(1)} %get-tuple-element.30), channel_id=1, replica_groups=mesh['y'=4,'core'=2,'x'=4,'z'=8] {'x','z'}, dimensions={0} | all-to-all | bytes 262144 | tf_op jit(solution)/shard_map/all_to_all | solution.py:463
  74.8 0.1 merge_kernel.1
  74.9 11.2 %all_to_all.11.tiles = f32[8,8,128]{2,1,0:T(8,128)S(1)} all-to-all(f32[8,8,128]{2,1,0:T(8,128)S(1)} %merge_kernel.1), channel_id=1, replica_groups=mesh['y'=4,'core'=2,'x'=4,'z'=8] {'y','core'}, dimensions={0} | all-to-all | bytes 65536 | tf_op jit(solution)/shard_map/all_to_all | solution.py:465
  86.2 2.9 %finish_kernel.1 = (bf16[4,4,320,256]{3,2,1,0:T(8,128)(2,1)}, f32[2,256]{1,0:T(2,128)}) custom-call(s32[12]{0:T(128)S(1)} %concatenate.3.info, f32[8,8,128]{2,1,0:T(8,128)S(1)} %all_to_all.11.tiles, bf16[4,4,320,256]{3,2,1,0:T(8,128)(2,1)S(1)} %copy-done, f32[4,4,320,256]{3,2,1,0:T(8,128)S(1)} %get-tuple-element.31.eliminated), custom_call_target="tpu_custom_call" | custom-call | tf_op jit(solution)/shard_map/finish_kernel/pallas_call | solution.py:376
  (3 shorter events, 0.0 us)
Async XLA Ops:
  0.6 11.3 %copy-start = (bf16[4,4,320,256]{3,2,1,0:T(8,128)(2,1)S(1)}, bf16[4,4,320,256]{3,2,1,0:T(8,128)(2,1)}, u32[]{:S(2)}) copy-start(bf16[4,4,320,256]{3,2,1,0:T(8,128)(2,1)} %vector.7) | copy-start | bytes 7864324
  3.8 1.2 %copy-start.1 = (bf16[4,4,1,80,320]{4,3,2,1,0:T(8,128)(2,1)S(1)}, bf16[4,4,1,80,320]{4,3,2,1,0:T(8,128)(2,1)}, u32[]{:S(2)}) copy-start(bf16[4,4,1,80,320]{4,3,2,1,0:T(8,128)(2,1)} %slice.3.lifting_below) | copy-start | bytes 2457604
  5.0 1.2 %copy-start.4 = (bf16[4,4,80,320]{3,2,1,0:T(8,128)(2,1)S(1)}, bf16[4,4,80,320]{3,2,1,0:T(8,128)(2,1)}, u32[]{:S(2)}) copy-start(bf16[4,4,80,320]{3,2,1,0:T(8,128)(2,1)} %inverse.3) | copy-start | bytes 2457604
  8.6 21.2 %copy-start.3 = (bf16[4,4,6,80,320]{4,3,2,1,0:T(8,128)(2,1)S(1)}, bf16[4,4,6,80,320]{4,3,2,1,0:T(8,128)(2,1)}, u32[]{:S(2)}) copy-start(bf16[4,4,6,80,320]{4,3,2,1,0:T(8,128)(2,1)} %lifting.1) | copy-start | bytes 14745604
  8.6 21.2 %copy-start.5 = (bf16[4,4,80,320]{3,2,1,0:T(8,128)(2,1)S(1)}, bf16[4,4,80,320]{3,2,1,0:T(8,128)(2,1)}, u32[]{:S(2)}) copy-start(bf16[4,4,80,320]{3,2,1,0:T(8,128)(2,1)} %inverse.3) | copy-start | bytes 2457604
  8.6 14.9 %collective-permute-start = (f32[3,80,128]{2,1,0:T(8,128)S(1)}, f32[3,80,128]{2,1,0:T(8,128)S(1)}, u32[]{:S(2)}, u32[]{:S(2)}) collective-permute-start(f32[3,80,128]{2,1,0:T(8,128)S(1)} %get-tuple-element.17.map_here), channel_id=1, source_target_pairs={{0,32},{32,0},{1,33},{33,1},{2,34},{34,2},{3,35},{35,3},{4,36},{36... | collective-permute-start | bytes 368648 | tf_op jit(solution)/shard_map/ppermute | solution.py:419
  12.8 16.9 %collective-permute-start.1 = (bf16[3,80,256]{2,1,0:T(8,128)(2,1)S(1)}, bf16[3,80,256]{2,1,0:T(8,128)(2,1)S(1)}, u32[]{:S(2)}, u32[]{:S(2)}) collective-permute-start(bf16[3,80,256]{2,1,0:T(8,128)(2,1)S(1)} %get-tuple-element.19), channel_id=1, source_target_pairs={{0,32},{32,0},{1,33},{33,1},{2,34},{34,2},{3,35},{35,3},{4,36},{36... | collective-permute-start | bytes 368648 | tf_op jit(solution)/shard_map/ppermute | solution.py:404
  12.9 16.8 %collective-permute-start.2 = (bf16[3,80,256]{2,1,0:T(8,128)(2,1)S(1)}, bf16[3,80,256]{2,1,0:T(8,128)(2,1)S(1)}, u32[]{:S(2)}, u32[]{:S(2)}) collective-permute-start(bf16[3,80,256]{2,1,0:T(8,128)(2,1)S(1)} %get-tuple-element.20), channel_id=1, source_target_pairs={{32,64},{96,128},{160,192},{64,32},{128,96},{192,160},{33,65},{97,... | collective-permute-start | bytes 368648 | tf_op jit(solution)/shard_map/ppermute | solution.py:406
  14.9 14.9 %collective-permute-start.3 = (bf16[4,80,256]{2,1,0:T(8,128)(2,1)S(1)}, bf16[4,80,256]{2,1,0:T(8,128)(2,1)S(1)}, u32[]{:S(2)}, u32[]{:S(2)}) collective-permute-start(bf16[4,80,256]{2,1,0:T(8,128)(2,1)S(1)} %get-tuple-element.21), channel_id=1, source_target_pairs={{0,1},{1,0},{2,3},{3,2},{4,5},{5,4},{6,7},{7,6},{8,9},{9,8},{10,11... | collective-permute-start | bytes 491528 | tf_op jit(solution)/shard_map/ppermute | solution.py:407
  16.6 13.2 %collective-permute-start.4 = (bf16[4,80,256]{2,1,0:T(8,128)(2,1)S(1)}, bf16[4,80,256]{2,1,0:T(8,128)(2,1)S(1)}, u32[]{:S(2)}, u32[]{:S(2)}) collective-permute-start(bf16[4,80,256]{2,1,0:T(8,128)(2,1)S(1)} %get-tuple-element.22), channel_id=1, source_target_pairs={{1,2},{3,4},{5,6},{7,8},{9,10},{11,12},{13,14},{15,16},{17,18},{19... | collective-permute-start | bytes 491528 | tf_op jit(solution)/shard_map/ppermute | solution.py:409
  23.5 2.1 %copy-start.6 = (bf16[4,4,320,320]{3,2,1,0:T(8,128)(2,1)S(1)}, bf16[4,4,320,320]{3,2,1,0:T(8,128)(2,1)}, u32[]{:S(2)}) copy-start(bf16[4,4,320,320]{3,2,1,0:T(8,128)(2,1)} %diagonal.1) | copy-start | bytes 9830404
  29.8 25.8 %copy-start.2 = (bf16[4,4,1,80,320]{4,3,2,1,0:T(8,128)(2,1)S(1)}, bf16[4,4,1,80,320]{4,3,2,1,0:T(8,128)(2,1)}, u32[]{:S(2)}) copy-start(bf16[4,4,1,80,320]{4,3,2,1,0:T(8,128)(2,1)} %slice.3.lifting_below) | copy-start | bytes 2457604
  37.6 5.7 %collective-permute-start.5 = (f32[3,80,256]{2,1,0:T(8,128)S(1)}, f32[3,80,256]{2,1,0:T(8,128)S(1)}, u32[]{:S(2)}, u32[]{:S(2)}) collective-permute-start(f32[3,80,256]{2,1,0:T(8,128)S(1)} %get-tuple-element.28.mine), channel_id=1, source_target_pairs={{0,32},{32,0},{1,33},{33,1},{2,34},{34,2},{3,35},{35,3},{4,36},{36... | collective-permute-start | bytes 737288 | tf_op jit(solution)/shard_map/ppermute | solution.py:450
  37.7 10.3 %collective-permute-start.10 = (f32[3,80,128]{2,1,0:T(8,128)S(1)}, f32[3,80,128]{2,1,0:T(8,128)S(1)}, u32[]{:S(2)}, u32[]{:S(2)}) collective-permute-start(f32[3,80,128]{2,1,0:T(8,128)S(1)} %get-tuple-element.29), channel_id=1, source_target_pairs={{0,128},{64,192},{1,129},{65,193},{2,130},{66,194},{3,131},{67,195... | collective-permute-start | bytes 368648 | tf_op jit(solution)/shard_map/ppermute | solution.py:435
  42.0 6.1 %collective-permute-start.9 = (f32[3,80,128]{2,1,0:T(8,128)S(1)}, f32[3,80,128]{2,1,0:T(8,128)S(1)}, u32[]{:S(2)}, u32[]{:S(2)}) collective-permute-start(f32[3,80,128]{2,1,0:T(8,128)S(1)} %get-tuple-element.29), channel_id=1, source_target_pairs={{0,64},{64,128},{128,192},{1,65},{65,129},{129,193},{2,66},{66,130... | collective-permute-start | bytes 368648 | tf_op jit(solution)/shard_map/ppermute | solution.py:435
  44.1 6.9 %collective-permute-start.8 = (f32[3,80,128]{2,1,0:T(8,128)S(1)}, f32[3,80,128]{2,1,0:T(8,128)S(1)}, u32[]{:S(2)}, u32[]{:S(2)}) collective-permute-start(f32[3,80,128]{2,1,0:T(8,128)S(1)} %chip_kernel.1), channel_id=1, source_target_pairs={{0,192},{1,193},{2,194},{3,195},{4,196},{5,197},{6,198},{7,199},{8... | collective-permute-start | bytes 368648 | tf_op jit(solution)/shard_map/ppermute | solution.py:435
  45.4 5.6 %collective-permute-start.7 = (f32[3,80,128]{2,1,0:T(8,128)S(1)}, f32[3,80,128]{2,1,0:T(8,128)S(1)}, u32[]{:S(2)}, u32[]{:S(2)}) collective-permute-start(f32[3,80,128]{2,1,0:T(8,128)S(1)} %chip_kernel.1), channel_id=1, source_target_pairs={{0,128},{64,192},{1,129},{65,193},{2,130},{66,194},{3,131},{67,195... | collective-permute-start | bytes 368648 | tf_op jit(solution)/shard_map/ppermute | solution.py:435
  46.7 6.0 %collective-permute-start.6 = (f32[3,80,128]{2,1,0:T(8,128)S(1)}, f32[3,80,128]{2,1,0:T(8,128)S(1)}, u32[]{:S(2)}, u32[]{:S(2)}) collective-permute-start(f32[3,80,128]{2,1,0:T(8,128)S(1)} %chip_kernel.1), channel_id=1, source_target_pairs={{0,64},{64,128},{128,192},{1,65},{65,129},{129,193},{2,66},{66,130... | collective-permute-start | bytes 368648 | tf_op jit(solution)/shard_map/ppermute | solution.py:435
  53.7 1.9 %collective-permute-start.11 = (f32[3,80,128]{2,1,0:T(8,128)S(1)}, f32[3,80,128]{2,1,0:T(8,128)S(1)}, u32[]{:S(2)}, u32[]{:S(2)}) collective-permute-start(f32[3,80,128]{2,1,0:T(8,128)S(1)} %arriving_kernel.1.mine), channel_id=1, source_target_pairs={{0,32},{32,0},{1,33},{33,1},{2,34},{34,2},{3,35},{35,3},{4,36},{36... | collective-permute-start | bytes 368648 | tf_op jit(solution)/shard_map/ppermute | solution.py:454

commit v2 on v1

v2 whole, which is shorter than its diff:
```python
import functools

import jax
import jax.numpy as jnp
from jax import lax
from jax.experimental import pallas as pl
from jax.experimental.pallas import tpu as pltpu
from jax.sharding import Mesh
from jax.sharding import PartitionSpec as P

BLOCK = 320
FACE = 80
LINES_HERE = 4
SEGMENT = 4
MOVING = 3
R = 256
ELEMENTS = LINES_HERE * SEGMENT
HALF = 128
OWN_MAP = slice(R, R + 80)
Y_MAP = slice(R + HALF, R + HALF + 80)
WALL = ("y", "core")
SURF = ("x", "z")
F32 = jnp.float32
BF16 = jnp.bfloat16
EXACT = lax.Precision.HIGHEST
VMEM = pltpu.VMEM
SMEM = pltpu.SMEM


def in_vmem():
    return pl.BlockSpec(memory_space=VMEM)


def in_smem():
    return pl.BlockSpec(memory_space=SMEM)


def wall_here():
    return lax.axis_index("y") * 2 + lax.axis_index("core")


def living_here(lengths, line):
    return jnp.clip(lengths[line] - SEGMENT * wall_here(), 0, SEGMENT)


def shortest_line(lengths):
    at = jnp.int32(3)
    for line in (2, 1, 0):
        at = jnp.where(lengths[line] == 1, line, at)
    return at


def line_in_slot(slot, short):
    return jnp.where(slot == MOVING, short, slot + (slot >= short).astype(jnp.int32))


def list_living(lengths, listed, slots=LINES_HERE, rest_behind=False):
    short = shortest_line(lengths)
    count = jnp.int32(0)
    for slot in range(slots):
        here = living_here(lengths, line_in_slot(slot, short))
        for position in range(SEGMENT):
            entry = slot * SEGMENT + position
            alive = (position < here).astype(jnp.int32)
            listed[count if not rest_behind else jnp.where(alive == 1, count, ELEMENTS - 1 - (entry - count))] = entry
            count = count + alive
    return count


def for_listed(lengths, listed, count, body, together=4, after=None):
    short = shortest_line(lengths)

    @pl.loop(0, (count + together - 1) // together)
    def _(trip):
        for part in range(together):
            entry = listed[jnp.minimum(trip * together + part, count - 1)]
            slot = entry // SEGMENT
            body(slot, line_in_slot(slot, short), entry % SEGMENT)
        if after is not None:
            for part in range(together):
                after(trip * together + part)


def wall_face_rows():
    row = lax.broadcasted_iota(jnp.int32, (2 * FACE, BLOCK), 0)
    column = lax.broadcasted_iota(jnp.int32, (2 * FACE, BLOCK), 1)
    second = (row >= FACE).astype(jnp.int32)
    return (column == 4 * (row - FACE * second) + 3 * second).astype(BF16)


def pick(rows, values):
    return jnp.dot(rows, values, preferred_element_type=F32).astype(BF16)


def a_face(block, end):
    return jnp.concatenate([block[64 * v + 16 * end : 64 * v + 16 * end + 16] for v in range(5)], axis=0)


def split_exactly(values):
    high = values.astype(BF16)
    low = (values - high.astype(F32)).astype(BF16)
    return high, low


def transposed_times(left, right):
    return lax.dot_general(left, right, (((0,), (0,)), ((), ())), preferred_element_type=F32)


def mapped(matrix, state):
    matrix_high, matrix_low = split_exactly(matrix)
    high, low = split_exactly(state)
    rows = matrix.shape[0]
    both = jnp.dot(jnp.concatenate([matrix_high, matrix_low], axis=0), high, preferred_element_type=F32)
    return both[:rows] + (both[rows:] + jnp.dot(matrix_high, low, preferred_element_type=F32))


def edges_kernel(
    lengths_hbm, vector, over_core, over_y, over_pair, over_next, lengths, ends, west, east, sems, run_sems
):
    core, odd = lax.axis_index("core"), lax.axis_index("z") % 2
    copies = [pltpu.make_async_copy(lengths_hbm, lengths, sems.at[0])]
    for end, position in enumerate((0, SEGMENT - 1)):
        copies.append(pltpu.make_async_copy(vector.at[:, position], ends.at[end], sems.at[1 + end]))
    for at, (line, first_row, face) in enumerate(((0, 0, west), (LINES_HERE - 1, 48, east))):
        for run in range(5):
            source = vector.at[line, :, pl.ds(64 * run + first_row, 16)]
            target = face.at[:, pl.ds(16 * run, 16)]
            copies.append(pltpu.make_async_copy(source, target, run_sems.at[at, run]))
    for copy in copies:
        copy.start()
    rows = wall_face_rows()
    for copy in copies:
        copy.wait()
    short = shortest_line(lengths)
    zero = jnp.zeros((FACE, R), BF16)
    for slot in range(MOVING):
        line = line_in_slot(slot, short)
        here = living_here(lengths, line)
        down = jnp.where(here > 0, pick(rows[:FACE], ends[0, line]), zero)
        up = jnp.where(here > SEGMENT - 1, pick(rows[FACE:], ends[1, line]), zero)
        over_core[slot] = jnp.where(core == 0, up, down)
        over_y[slot] = jnp.where(core == 0, down, up)
    first, last = living_here(lengths, 0), living_here(lengths, LINES_HERE - 1)
    for position in range(SEGMENT):
        from_first = jnp.where(position < first, west[position], zero)
        from_last = jnp.where(position < last, east[position], zero)
        over_pair[position] = jnp.where(odd == 0, from_last, from_first)
        over_next[position] = jnp.where(odd == 0, from_first, from_last)


def maps_kernel(
    lengths_hbm,
    after,
    lifting_hbm,
    inverse_hbm,
    diagonal_hbm,
    steps,
    prefixes,
    whole,
    lower,
    inverse,
    diagonal,
    lengths,
    sems,
    lengths_sem,
):
    needed = [pltpu.make_async_copy(lengths_hbm, lengths, lengths_sem)]
    for line in range(LINES_HERE):
        needed.append(pltpu.make_async_copy(inverse_hbm.at[line], inverse.at[line], sems.at[0, line]))
        needed.append(pltpu.make_async_copy(lifting_hbm.at[line, :, 0], lower.at[line], sems.at[1, line]))
    later = [
        pltpu.make_async_copy(diagonal_hbm.at[line], diagonal.at[line], sems.at[2, line]) for line in range(LINES_HERE)
    ]
    for copy in needed + later:
        copy.start()
    for copy in needed:
        copy.wait()
    short = shortest_line(lengths)
    lines = [line_in_slot(slot, short) for slot in range(MOVING)]
    so_far = [None] * MOVING
    for position in range(SEGMENT):
        for slot, line in enumerate(lines):
            step = lax.dot_general(
                inverse[line, position],
                lower[line, position],
                (((1,), (1,)), ((), ())),
                preferred_element_type=F32,
            )
            steps[slot, position] = jnp.where(position < living_here(lengths, line), -step, 0.0)
    for position in range(SEGMENT):
        for slot in range(MOVING):
            step = steps[slot, position]
            so_far[slot] = step if position == 0 else mapped(step, so_far[slot])
            if position < SEGMENT - 1:
                prefixes[slot, position] = so_far[slot]
    for slot in range(MOVING):
        whole[slot] = jnp.concatenate([so_far[slot], jnp.zeros((FACE, HALF - FACE), F32)], axis=1)
    for copy in later:
        copy.wait()


def diagonal_kernel(lengths, vector, diagonal, lifting_hbm, product, traces, lifting, listed, wide, sems):
    copies = [
        pltpu.make_async_copy(lifting_hbm.at[line, :, pl.ds(1, 5)], lifting.at[line], sems.at[line])
        for line in range(LINES_HERE)
    ]
    for copy in copies:
        copy.start()
    for line in range(LINES_HERE):
        here = living_here(lengths, line)
        for position in range(SEGMENT):

            @pl.when(position >= here)
            def _():
                traces[line, position] = jnp.zeros((6, FACE, R), BF16)

    def body(slot, line, position):
        values = vector[line, position]
        product[line, position] = jnp.dot(diagonal[line, position], values, preferred_element_type=F32)
        whole = values.astype(F32)
        for half in range(2):
            columns = slice(half * HALF, (half + 1) * HALF)
            wide[half] = whole[:, columns]
            for face, first in ((0, 0), (1, 3)):
                traces[line, position, face, :, columns] = wide[half, pl.ds(first, FACE, stride=4), :].astype(BF16)
        traces[line, position, 2] = a_face(values, 0)
        traces[line, position, 3] = a_face(values, 3)
        runs = whole.reshape(10, 4, 8, R)
        upper = lax.broadcasted_iota(jnp.int32, (10, 8, R), 1) < 4
        south = jnp.where(upper, runs[:, 0], pltpu.roll(runs[:, 2], 4, axis=1))
        north = jnp.where(upper, pltpu.roll(runs[:, 1], 4, axis=1), runs[:, 3])
        traces[line, position, 4] = south.reshape(FACE, R).astype(BF16)
        traces[line, position, 5] = north.reshape(FACE, R).astype(BF16)

    for_listed(lengths, listed, list_living(lengths, listed), body)
    for copy in copies:
        copy.wait()


def product_kernel(
    lengths,
    norths,
    traces,
    over_core,
    over_y,
    over_pair,
    over_next,
    lower,
    lifting,
    inverse,
    steps,
    map_here,
    map_y,
    product_in,
    product,
    carries,
    outgoing,
    listed,
    driven,
):
    core, odd = lax.axis_index("core"), lax.axis_index("z") % 2
    zero = jnp.zeros((FACE, R), BF16)

    def multiply(slot, line, position):
        wall_slot = jnp.minimum(slot, MOVING - 1)
        moving = slot < MOVING
        from_core = jnp.where(moving, over_core[wall_slot], zero)
        from_y = jnp.where(moving, over_y[wall_slot], zero)
        below_edge = jnp.where(core == 0, from_y, from_core)
        above_edge = jnp.where(core == 0, from_core, from_y)
        below = jnp.where(position == 0, below_edge, traces[line, jnp.maximum(position - 1, 0), 1])
        above = jnp.where(
            position == SEGMENT - 1, above_edge, traces[line, jnp.minimum(position + 1, SEGMENT - 1), 0]
        )
        west_edge = jnp.where(odd == 0, over_next[position], over_pair[position])
        east_edge = jnp.where(odd == 0, over_pair[position], over_next[position])
        west = jnp.where(line == 0, west_edge, traces[jnp.maximum(line - 1, 0), position, 3])
        east = jnp.where(
            line == LINES_HERE - 1, east_edge, traces[jnp.minimum(line + 1, LINES_HERE - 1), position, 2]
        )
        north_line = norths[0, line]
        south_line = jnp.int32(0)
        for other in range(1, LINES_HERE):
            south_line = jnp.where(norths[0, other] == line, other, south_line)
        south = traces[south_line, position, 5]
        north = traces[north_line, position, 4]
        neighbours = jnp.concatenate([below, above, west, east, south, north], axis=0)
        upper_blocks = lifting[line, position].reshape(5 * FACE, BLOCK)
        blocks = jnp.concatenate([lower[line, position], upper_blocks], axis=0)
        product[line, position] = product_in[line, position] + transposed_times(blocks, neighbours)

    count = list_living(lengths, listed)
    for_listed(lengths, listed, count, multiply)

    for slot in range(MOVING):
        for position in range(SEGMENT):

            @pl.when(position >= living_here(lengths, line_in_slot(slot, shortest_line(lengths))))
            def _():
                driven[slot, position] = jnp.zeros((FACE, R), F32)

    def drive(slot, line, position):
        high, low = split_exactly(product[line, position])
        rows = inverse[line, position]
        tail = rows[:, 256:]
        driven[slot, position] = jnp.dot(
            jnp.concatenate([rows[:, :256], rows[:, :256], tail, tail], axis=1),
            jnp.concatenate([high[:256], low[:256], high[256:], low[256:]], axis=0),
            preferred_element_type=F32,
        )

    for_listed(lengths, listed, list_living(lengths, listed, MOVING), drive)
    carried = [driven[slot, 0] for slot in range(MOVING)]
    for position in range(1, SEGMENT):
        for slot in range(MOVING):
            carries[slot, position - 1] = carried[slot]
            carried[slot] = driven[slot, position] + mapped(steps[slot, position], carried[slot])
    for slot in range(MOVING):
        outgoing[slot] = jnp.concatenate([carried[slot], map_here[slot], map_y[slot]], axis=1)


def chip_kernel(mine, other, near, far):
    core, y = lax.axis_index("core"), lax.axis_index("y")
    values = []
    for slot in range(MOVING):
        own, away = mine[slot], other[slot]
        first_value = jnp.where(core == 0, own[:, :HALF], away[:, HALF:R])
        second_value = jnp.where(core == 0, away[:, :HALF], own[:, HALF:R])
        second_map = jnp.where(core == 0, away[:, OWN_MAP], own[:, OWN_MAP])
        values.append(mapped(second_map, first_value) + second_value)
    for slot in range(MOVING):
        near[slot] = values[slot]
        far[slot] = values[slot]

    @pl.when(y == 0)
    def _():
        through_chip(mine, other, values, far)


def through_chip(mine, other, values, results):
    core = lax.axis_index("core")
    moved = []
    for slot, value in enumerate(values):
        own, away = mine[slot][:, Y_MAP], other[slot][:, Y_MAP]
        moved.append(mapped(jnp.where(core == 0, own, away), value))
    for slot, value in enumerate(moved):
        own, away = mine[slot][:, Y_MAP], other[slot][:, Y_MAP]
        results[slot] = mapped(jnp.where(core == 0, away, own), value)


def arriving_kernel(one, two, three, mine, other, arriving):
    y = lax.axis_index("y")
    below = [two[slot] + three[slot] for slot in range(MOVING)]
    for slot in range(MOVING):
        arriving[slot] = below[slot]

    @pl.when(y == 3)
    def _():
        through_chip(mine, other, below, arriving)

    for slot in range(MOVING):
        arriving[slot] = arriving[slot] + one[slot]


def eliminate_kernel(
    lengths,
    vector,
    product,
    lower,
    prefixes,
    carries,
    mine,
    other,
    beside,
    eliminated,
    tiles,
    listed,
    entering,
):
    core = lax.axis_index("core")
    short = shortest_line(lengths)
    entering[...] = jnp.zeros_like(entering)
    values = []
    for slot in range(MOVING):
        left = jnp.where(core == 0, mine[slot], other[slot])
        right = jnp.where(core == 0, other[slot], mine[slot])
        value = jnp.concatenate([left, right], axis=1)
        passed = mapped(beside[slot][:, OWN_MAP], value) + beside[slot][:, :R]
        values.append(jnp.where(core == 0, value, passed))
    for slot, value in enumerate(values):
        entering[slot, 0] = value
        moved = mapped(prefixes[slot].reshape((SEGMENT - 1) * FACE, FACE), value)
        for position in range(1, SEGMENT):
            entering[slot, position] = carries[slot, position - 1] + moved[(position - 1) * FACE : position * FACE]

    count = list_living(lengths, listed)
    nothing = jnp.zeros((8, R), F32)

    def of(trip):
        entry = listed[trip]
        slot = entry // SEGMENT
        return slot, line_in_slot(slot, short), entry % SEGMENT

    def partial(values):
        return values.reshape(BLOCK // 8, 8, R).sum(axis=0)

    def correct(slot, line, position):
        high, low = split_exactly(entering[slot, position])
        block = lower[line, position]
        correction = transposed_times(jnp.concatenate([block, block], axis=0), jnp.concatenate([high, low], axis=0))
        eliminated[line, position] = product[line, position] - correction

    for_listed(lengths, listed, count, correct)

    def products(trip, sums):
        _, line, position = of(trip)
        masked, value = vector[line, position].astype(F32), eliminated[line, position]
        return sums[0] + partial(masked * value), sums[1] + partial(masked * masked)

    cross, square = lax.fori_loop(0, count, products, (nothing, nothing))
    cross = cross.sum(axis=0, keepdims=True)
    square = square.sum(axis=0, keepdims=True)
    share = jnp.where(square > 0, cross / square, 0.0)

    def left_over(trip, total):
        _, line, position = of(trip)
        rest = eliminated[line, position] - share * vector[line, position].astype(F32)
        return total + partial(rest * rest)

    rest = lax.fori_loop(0, count, left_over, nothing).sum(axis=0, keepdims=True)
    pieces = [part[:, at : at + HALF] for part in (cross, square, rest) for at in (0, HALF)]
    tile = jnp.concatenate(pieces + [jnp.zeros((2, HALF), F32)], axis=0)
    for copy in range(tiles.shape[0]):
        tiles[copy] = tile


def merged(tiles):
    cross, square, rest = tiles[:, 0:2], tiles[:, 2:4], tiles[:, 4:6]
    all_cross, all_square = cross.sum(axis=0), square.sum(axis=0)
    own = jnp.where(square > 0, cross / square, 0.0)
    ratio = all_cross / all_square
    away = jnp.where(square > 0, own - ratio[None], 0.0)
    all_rest = (rest + (square * away) * away).sum(axis=0)
    return all_cross, all_square, all_rest, ratio


def merge_kernel(tiles_in, tiles):
    cross, square, rest, _ = merged(tiles_in[...])
    tile = jnp.concatenate([cross, square, rest, jnp.zeros((2, HALF), F32)], axis=0)
    for copy in range(tiles.shape[0]):
        tiles[copy] = tile


def finish_kernel(entries, lengths, tiles, vector, eliminated, basis, coefs, listed, held, sems):
    _, _, rest, ratio = merged(tiles[...])
    spread = jnp.sqrt(rest / entries + 1e-06)
    ratio = jnp.concatenate([ratio[0:1], ratio[1:2]], axis=1)
    spread = jnp.concatenate([spread[0:1], spread[1:2]], axis=1)
    coefs[...] = jnp.concatenate([ratio, spread], axis=0)
    scale = 1.0 / spread
    short = shortest_line(lengths)
    count = list_living(lengths, listed, rest_behind=True)

    def copy_of(trip):
        line, position = line_in_slot(listed[trip] // SEGMENT, short), listed[trip] % SEGMENT
        return pltpu.make_async_copy(held.at[line, position], basis.at[line, position], sems.at[trip])

    @pl.loop(count, ELEMENTS)
    def _(trip):
        line, position = line_in_slot(listed[trip] // SEGMENT, short), listed[trip] % SEGMENT
        held[line, position] = jnp.zeros((BLOCK, R), BF16)
        copy_of(trip).start()

    def body(slot, line, position):
        masked = vector[line, position].astype(F32)
        held[line, position] = ((eliminated[line, position] - ratio * masked) * scale).astype(BF16)

    def after(trip):
        @pl.when(trip < count)
        def _():
            copy_of(trip).start()

    for_listed(lengths, listed, count, body, 2, after)

    @pl.loop(0, ELEMENTS)
    def _(trip):
        copy_of(trip).wait()


def call(kernel, outs, ins, scratch=(), limit=12, flops=0, moved=0, out_specs=None, in_hbm=()):
    return pl.pallas_call(
        kernel,
        out_shape=outs,
        in_specs=[
            pl.BlockSpec(memory_space=pltpu.HBM) if at in in_hbm else in_smem() if arg.dtype == jnp.int32 else in_vmem()
            for at, arg in enumerate(ins)
        ],
        out_specs=out_specs or jax.tree.map(lambda _: in_vmem(), outs),
        scratch_shapes=list(scratch),
        compiler_params=pltpu.CompilerParams(vmem_limit_bytes=limit * 2**20),
        cost_estimate=pl.CostEstimate(flops=flops, bytes_accessed=moved, transcendentals=0),
        name=getattr(kernel, "__name__", "finish_kernel"),
    )(*[pltpu.with_memory_space_constraint(arg, pltpu.HBM) if at in in_hbm else arg for at, arg in enumerate(ins)])


def shaped(*shape, dtype=F32):
    return jax.ShapeDtypeStruct(shape, dtype)


LISTED = pltpu.SMEM((LINES_HERE * SEGMENT + 1,), jnp.int32)


def per_device(vector, lengths, north_of, diagonal, lifting, inverse_rows):
    edge = shaped(MOVING, FACE, R, dtype=BF16)
    side = shaped(SEGMENT, FACE, R, dtype=BF16)
    over_core, over_y, over_pair, over_next = call(
        edges_kernel,
        (edge, edge, side, side),
        (lengths, vector),
        (
            pltpu.SMEM((LINES_HERE,), jnp.int32),
            pltpu.VMEM((2, LINES_HERE, BLOCK, R), BF16),
            pltpu.VMEM((SEGMENT, FACE, R), BF16),
            pltpu.VMEM((SEGMENT, FACE, R), BF16),
            pltpu.SemaphoreType.DMA((3,)),
            pltpu.SemaphoreType.DMA((2, 5)),
        ),
        in_hbm=(0, 1),
    )
    walls, surfs = lax.axis_size(WALL), lax.axis_size(SURF)
    swap = [(0, 1), (1, 0)]
    first_edge = over_core
    over_core = lax.ppermute(over_core, "core", swap)
    rungs = [(i, i + 1) for i in range(1, walls - 1, 2)]
    over_y = lax.ppermute(over_y, WALL, rungs + [(b, a) for a, b in rungs])
    over_pair = lax.ppermute(over_pair, SURF, [(i, i ^ 1) for i in range(surfs)])
    nexts = [(i, (i + 1) % surfs) for i in range(1, surfs, 2)]
    over_next = lax.ppermute(over_next, SURF, nexts + [(b, a) for a, b in nexts])

    blocks = shaped(LINES_HERE, SEGMENT, FACE, BLOCK, dtype=BF16)
    steps, prefixes, whole, lower, inverse, diagonal_here = call(
        maps_kernel,
        (
            shaped(MOVING, SEGMENT, FACE, FACE),
            shaped(MOVING, SEGMENT - 1, FACE, FACE),
            shaped(MOVING, FACE, HALF),
            blocks,
            blocks,
            shaped(LINES_HERE, SEGMENT, BLOCK, BLOCK, dtype=BF16),
        ),
        (lengths, first_edge, lifting, inverse_rows, diagonal),
        (pltpu.SMEM((LINES_HERE,), jnp.int32), pltpu.SemaphoreType.DMA((3, LINES_HERE)), pltpu.SemaphoreType.DMA),
        in_hbm=(0, 2, 3, 4),
    )
    map_y = lax.ppermute(whole, "y", [(1, 0), (2, 3)])
    product, traces, lifting_here = call(
        diagonal_kernel,
        (
            shaped(LINES_HERE, SEGMENT, BLOCK, R),
            shaped(LINES_HERE, SEGMENT, 6, FACE, R, dtype=BF16),
            shaped(LINES_HERE, SEGMENT, 5, FACE, BLOCK, dtype=BF16),
        ),
        (lengths, vector, diagonal_here, lifting),
        (LISTED, pltpu.VMEM((2, BLOCK, HALF), F32), pltpu.SemaphoreType.DMA((LINES_HERE,))),
        in_hbm=(3,),
    )
    product, carries, outgoing = call(
        product_kernel,
        (
            shaped(LINES_HERE, SEGMENT, BLOCK, R),
            shaped(MOVING, SEGMENT - 1, FACE, R),
            shaped(MOVING, FACE, R + 2 * HALF),
        ),
        (
            lengths,
            north_of,
            traces,
            over_core,
            over_y,
            over_pair,
            over_next,
            lower,
            lifting_here,
            inverse,
            steps,
            whole,
            map_y,
            product,
        ),
        (LISTED, pltpu.VMEM((LINES_HERE, SEGMENT, FACE, R), F32)),
    )
    ranks = lax.axis_size("y")

    def up_chips(value, far):
        return lax.ppermute(value, "y", [(i, i + far) for i in range(ranks - far)])

    beside = lax.ppermute(outgoing, "core", swap)
    near, far = call(chip_kernel, (shaped(MOVING, FACE, HALF), shaped(MOVING, FACE, HALF)), (outgoing, beside))
    one, two, three = up_chips(near, 1), up_chips(far, 2), up_chips(far, 3)
    arriving = call(arriving_kernel, shaped(MOVING, FACE, HALF), (one, two, three, outgoing, beside))
    arriving_beside = lax.ppermute(arriving, "core", swap)
    eliminated, tiles = call(
        eliminate_kernel,
        (shaped(LINES_HERE, SEGMENT, BLOCK, R), shaped(surfs, 8, HALF)),
        (lengths, vector, product, lower, prefixes, carries, arriving, arriving_beside, beside),
        (LISTED, pltpu.VMEM((LINES_HERE, SEGMENT, FACE, R), F32)),
        flops=10**9,
        moved=10**7,
    )
    tiles = lax.all_to_all(tiles, SURF, 0, 0, tiled=True)
    tiles = call(merge_kernel, shaped(walls, 8, HALF), (tiles,))
    tiles = lax.all_to_all(tiles, WALL, 0, 0, tiled=True)
    entries = LINES_HERE * SEGMENT * BLOCK * walls * surfs
    return call(
        functools.partial(finish_kernel, entries),
        (shaped(LINES_HERE, SEGMENT, BLOCK, R, dtype=BF16), shaped(2, R)),
        (lengths, tiles, vector, eliminated),
        (LISTED, pltpu.VMEM((LINES_HERE, SEGMENT, BLOCK, R), BF16), pltpu.SemaphoreType.DMA((ELEMENTS,))),
        out_specs=(pl.BlockSpec(memory_space=pl.ANY), in_vmem()),
    )


def solution(mesh):
    split = Mesh(mesh.devices.reshape(4, 2, 4, 8), ("y", "core", "x", "z"))
    placed = (
        P(SURF, WALL, None, None),
        P(SURF),
        P(SURF, None),
        P(SURF, WALL, None, None),
        P(SURF, WALL, None, None, None),
        P(SURF, WALL, None, None),
    )
    return jax.shard_map(
        per_device,
        mesh=split,
        in_specs=placed,
        out_specs=(P(SURF, WALL, None, None), P()),
        check_vma=False,
    )
```

time: 89.4 us -> 76.6 us (0.86)
  local copies, waits for them, and re-layouts: 7.69 us -> 0.02 us
  Pallas kernels: 25.4 us -> 18.4 us
  waiting for transfers between devices: 5.63 us -> 7.72 us
  blocking collectives: 25.1 us -> 26.9 us
  starting transfers between devices: 24.4 us -> 23.1 us
    pallas_call x9, Pallas kernels: 25.4 us -> 18.4 us  [call(): pl.pallas_call(kernel, out_shape=outs, in_specs=[pl.BlockSpec(memory_spac...]
    ppermute x5 -> x3, starting transfers between devices: 9.45 us -> 4.55 us  [up_chips(): return lax.ppermute(value, 'y', [(i, i + far) for i in range(ranks - far)])]
    unnamed x14 -> x6, local copies, waits for them, and re-layouts: 4.54 us -> 0.02 us
    slice x1 -> x0, local copies, waits for them, and re-layouts: 2.4 us -> none  [per_device(): lower = lifting[:, :, 0:1]]
    ppermute x1, starting transfers between devices: 1.96 us -> 4.31 us  [per_device(): over_y = lax.ppermute(over_y, WALL, rungs + [(b, a) for a, b in rungs])]
    ppermute x1, starting transfers between devices: 0.09 us -> 2.37 us  [per_device(): beside = lax.ppermute(outgoing, 'core', swap)]
    ppermute x1, waiting for transfers between devices: 0.01 us -> 2.1 us  [per_device(): map_y = lax.ppermute(whole, 'y', [(1, 0), (2, 3)])]
    ppermute x1, starting transfers between devices: 3.32 us -> 1.29 us  [per_device(): map_y = lax.ppermute(whole, 'y', [(1, 0), (2, 3)])]
  transfers between devices with their start and end apart: 12 -> 10, of which waited for: 3 -> 4; matrix products, arithmetic and copies ran while one was open for 0% -> 0% of each run, Pallas kernels for 7% -> 8%
where the time goes in v2:
time: 76.6 us; the launch traced here: 77 us
  blocking collectives  26.9 us (35%)
  starting transfers between devices  23.1 us (30%)
  Pallas kernels  18.4 us (24%)
  waiting for transfers between devices  7.72 us (10%)
  between operations  0.79 us (1%)
    pallas_call x9, Pallas kernels, call(): pl.pallas_call(kernel, out_shape=outs, in_specs=[pl.BlockSpec(memory_spac...  18.4 us
    all_to_all x1, blocking collectives, per_device(): tiles = lax.all_to_all(tiles, SURF, 0, 0, tiled=True)  15.2 us
    all_to_all x1, blocking collectives, per_device(): tiles = lax.all_to_all(tiles, WALL, 0, 0, tiled=True)  11.7 us
    ppermute x1, starting transfers between devices, per_device(): lax.ppermute(over_next, SURF, nexts + [(b, a) for a, b in nexts])  6.86 us
    ppermute x3, starting transfers between devices, up_chips(): return lax.ppermute(value, 'y', [(i, i + far) for i in range(ranks - far)])  4.55 us
    ppermute x1, starting transfers between devices, per_device(): over_y = lax.ppermute(over_y, WALL, rungs + [(b, a) for a, b in rungs])  4.31 us
    ppermute x3, waiting for transfers between devices, up_chips(): return lax.ppermute(value, 'y', [(i, i + far) for i in range(ranks - far)])  3.15 us
    ppermute x1, starting transfers between devices, per_device(): lax.ppermute(over_pair, SURF, [(i, i ^ 1) for i in range(surfs)])  2.55 us
  transfers between devices with their start and end apart: 10, of which 4 were waited for; matrix products, arithmetic and copies ran while one was open for 0% of the time, Pallas kernels for 8%

profile of v2, /device:TPU:1, one launch (start us, length us, event | category | flops | bytes accessed | tf_op | source)
XLA Modules:
  0.0 77.0 jit_solution(2363532977058969419)
XLA Ops:
  0.6 2.0 %edges_kernel.1 = (bf16[3,80,256]{2,1,0:T(8,128)(2,1)S(1)}, bf16[3,80,256]{2,1,0:T(8,128)(2,1)S(1)}, bf16[4,80,256]{2,1,0:T(8,128)(2,1)S(1)}, bf16[4,80,256]{2,1,0:T(8,128)(2,1)S(1)}) custom-call(s32[4]{0:T(128)} %lengths.7, bf16[4,4,320,256]{3,2,1,0:T(8,128)(2,1)} %vector.7), custom_call_target="tpu_custom_call" | custom-call | tf_op jit(solution)/shard_map/edges_kernel/pallas_call | solution.py:491
  2.6 2.6 %collective-permute-start.2 = (bf16[4,80,256]{2,1,0:T(8,128)(2,1)S(1)}, bf16[4,80,256]{2,1,0:T(8,128)(2,1)S(1)}, u32[]{:S(2)}, u32[]{:S(2)}) collective-permute-start(bf16[4,80,256]{2,1,0:T(8,128)(2,1)S(1)} %get-tuple-element.26), channel_id=1, source_target_pairs={{0,1},{1,0},{2,3},{3,2},{4,5},{5,4},{6,7},{7,6},{8,9},{9,8},{10,11... | collective-permute-start | bytes 491528 | tf_op jit(solution)/shard_map/ppermute | solution.py:536
  5.1 6.9 %collective-permute-start.3 = (bf16[4,80,256]{2,1,0:T(8,128)(2,1)S(1)}, bf16[4,80,256]{2,1,0:T(8,128)(2,1)S(1)}, u32[]{:S(2)}, u32[]{:S(2)}) collective-permute-start(bf16[4,80,256]{2,1,0:T(8,128)(2,1)S(1)} %get-tuple-element.27), channel_id=1, source_target_pairs={{1,2},{3,4},{5,6},{7,8},{9,10},{11,12},{13,14},{15,16},{17,18},{19... | collective-permute-start | bytes 491528 | tf_op jit(solution)/shard_map/ppermute | solution.py:538
  12.0 4.3 %collective-permute-start.1 = (bf16[3,80,256]{2,1,0:T(8,128)(2,1)S(1)}, bf16[3,80,256]{2,1,0:T(8,128)(2,1)S(1)}, u32[]{:S(2)}, u32[]{:S(2)}) collective-permute-start(bf16[3,80,256]{2,1,0:T(8,128)(2,1)S(1)} %get-tuple-element.25), channel_id=1, source_target_pairs={{32,64},{96,128},{160,192},{64,32},{128,96},{192,160},{33,65},{97,... | collective-permute-start | bytes 368648 | tf_op jit(solution)/shard_map/ppermute | solution.py:535
  16.3 0.0 copy-start
  16.3 0.0 copy-start.1
  16.4 0.1 collective-permute-start
  16.5 3.1 %maps_kernel.1 = (f32[3,4,80,80]{3,2,1,0:T(8,128)S(1)}, f32[3,3,80,80]{3,2,1,0:T(8,128)S(1)}, f32[3,80,128]{2,1,0:T(8,128)S(1)}, bf16[4,4,80,320]{3,2,1,0:T(8,12...) custom-call(s32[4]{0:T(128)} %lengths.7, ...), custom_call_target="tpu_custom_call" | custom-call | tf_op jit(solution)/shard_map/maps_kernel/pallas_call | solution.py:491
  19.5 1.3 %collective-permute-start.4 = (f32[3,80,128]{2,1,0:T(8,128)S(1)}, f32[3,80,128]{2,1,0:T(8,128)S(1)}, u32[]{:S(2)}, u32[]{:S(2)}) collective-permute-start(f32[3,80,128]{2,1,0:T(8,128)S(1)} %get-tuple-element.32.map_here), channel_id=1, source_target_pairs={{64,0},{128,192},{65,1},{129,193},{66,2},{130,194},{67,3},{131,195... | collective-permute-start | bytes 368648 | tf_op jit(solution)/shard_map/ppermute | solution.py:555
  20.8 0.0 copy-done
  20.8 0.0 copy-done.1
  20.9 0.0 copy-start.2
  20.9 3.0 %diagonal_kernel.1 = (f32[4,4,320,256]{3,2,1,0:T(8,128)S(1)}, bf16[4,4,6,80,256]{4,3,2,1,0:T(8,128)(2,1)S(1)}, bf16[4,4,5,80,320]{4,3,2,1,0:T(8,128)(2,1)S(1)}) custom-call(s32[4]{0:T(128)S(1)} %copy-done.1, bf16[4,4,320,256]{3,2,1,0:T(8,128)(2,1)S(1)} %copy-done, bf16[4,4,320,320]{3,2,1,0:T(8,128)(2,1)S(1)} %get-tuple-element.23.diagonal, ...), custom_call_target="tpu_custom_call" | custom-call | tf_op jit(solution)/shard_map/diagonal_kernel/pallas_call | solution.py:491
  23.9 0.0 collective-permute-done.1.over_y
  23.9 0.0 collective-permute-done.over_core
  23.9 2.1 %collective-permute-done.4.map_y = f32[3,80,128]{2,1,0:T(8,128)S(1)} collective-permute-done((f32[3,80,128]{2,1,0:T(8,128)S(1)}, f32[3,80,128]{2,1,0:T(8,128)S(1)}, u32[]{:S(2)}, u32[]{:S(2)}) %collective-permute-start.4) | collective-permute-done | bytes 122912 | tf_op jit(solution)/shard_map/ppermute | solution.py:555
  26.0 0.0 collective-permute-done.2.over_pair
  26.0 0.0 collective-permute-done.3.over_next
  26.0 0.0 copy-done.2
  26.0 3.7 %product_kernel.1 = (f32[4,4,320,256]{3,2,1,0:T(8,128)S(1)}, f32[3,3,80,256]{3,2,1,0:T(8,128)S(1)}, f32[3,80,512]{2,1,0:T(8,128)S(1)}) custom-call(s32[4]{0:T(128)S(1)} %copy-done.1, s32[1,4]{1,0:T(1,128)S(1)} %copy-done.2, bf16[4,4,6,80,256]{4,3,2,1,0:T(8,128)(2,1)S(1)} %get-tuple-element.24.traces, bf16[3,80,256]{2,1,0:T(8,128)(2,1)S(1)} %collective-permute-done.over_core, ...), custom_call_target="tpu_custom_call" | custom-call | tf_op jit(solution)/shard_map/product_kernel/pallas_call | solution.py:491
  29.7 2.4 %collective-permute-start.5 = (f32[3,80,512]{2,1,0:T(8,128)S(1)}, f32[3,80,512]{2,1,0:T(8,128)S(1)}, u32[]{:S(2)}, u32[]{:S(2)}) collective-permute-start(f32[3,80,512]{2,1,0:T(8,128)S(1)} %get-tuple-element.37.mine), channel_id=1, source_target_pairs={{0,32},{32,0},{1,33},{33,1},{2,34},{34,2},{3,35},{35,3},{4,36},{36... | collective-permute-start | bytes 1474568 | tf_op jit(solution)/shard_map/ppermute | solution.py:597
  32.0 1.5 %collective-permute-done.5.other.beside = f32[3,80,512]{2,1,0:T(8,128)S(1)} collective-permute-done((f32[3,80,512]{2,1,0:T(8,128)S(1)}, f32[3,80,512]{2,1,0:T(8,128)S(1)}, u32[]{:S(2)}, u32[]{:S(2)}) %collective-permute-start.5) | collective-permute-done | bytes 491552 | tf_op jit(solution)/shard_map/ppermute | solution.py:597
  33.5 0.6 chip_kernel.1
  34.1 1.3 %collective-permute-start.6 = (f32[3,80,128]{2,1,0:T(8,128)S(1)}, f32[3,80,128]{2,1,0:T(8,128)S(1)}, u32[]{:S(2)}, u32[]{:S(2)}) collective-permute-start(f32[3,80,128]{2,1,0:T(8,128)S(1)} %get-tuple-element.38), channel_id=1, source_target_pairs={{0,64},{64,128},{128,192},{1,65},{65,129},{129,193},{2,66},{66,130... | collective-permute-start | bytes 368648 | tf_op jit(solution)/shard_map/ppermute | solution.py:595
  35.4 1.3 %collective-permute-start.8 = (f32[3,80,128]{2,1,0:T(8,128)S(1)}, f32[3,80,128]{2,1,0:T(8,128)S(1)}, u32[]{:S(2)}, u32[]{:S(2)}) collective-permute-start(f32[3,80,128]{2,1,0:T(8,128)S(1)} %get-tuple-element.39), channel_id=1, source_target_pairs={{0,192},{1,193},{2,194},{3,195},{4,196},{5,197},{6,198},{7,199},{8... | collective-permute-start | bytes 368648 | tf_op jit(solution)/shard_map/ppermute | solution.py:595
  36.7 2.0 %collective-permute-start.7 = (f32[3,80,128]{2,1,0:T(8,128)S(1)}, f32[3,80,128]{2,1,0:T(8,128)S(1)}, u32[]{:S(2)}, u32[]{:S(2)}) collective-permute-start(f32[3,80,128]{2,1,0:T(8,128)S(1)} %get-tuple-element.39), channel_id=1, source_target_pairs={{0,128},{64,192},{1,129},{65,193},{2,130},{66,194},{3,131},{67,195... | collective-permute-start | bytes 368648 | tf_op jit(solution)/shard_map/ppermute | solution.py:595
  38.7 0.0 collective-permute-done.6.one
  38.7 3.1 %collective-permute-done.8.three = f32[3,80,128]{2,1,0:T(8,128)S(1)} collective-permute-done((f32[3,80,128]{2,1,0:T(8,128)S(1)}, f32[3,80,128]{2,1,0:T(8,128)S(1)}, u32[]{:S(2)}, u32[]{:S(2)}) %collective-permute-start.8) | collective-permute-done | bytes 122912 | tf_op jit(solution)/shard_map/ppermute | solution.py:595
  41.8 0.0 collective-permute-done.7.two
  41.9 1.1 %collective-permute-start.9 = (f32[3,80,128]{2,1,0:T(8,128)S(1)}, f32[3,80,128]{2,1,0:T(8,128)S(1)}, u32[]{:S(2)}, u32[]{:S(2)}) collective-permute-start(f32[3,80,128]{2,1,0:T(8,128)S(1)} %arriving_kernel.1.mine), channel_id=1, source_target_pairs={{0,32},{32,0},{1,33},{33,1},{2,34},{34,2},{3,35},{35,3},{4,36},{36... | collective-permute-start | bytes 368648 | tf_op jit(solution)/shard_map/ppermute | solution.py:601
  43.0 1.0 %collective-permute-done.9.other = f32[3,80,128]{2,1,0:T(8,128)S(1)} collective-permute-done((f32[3,80,128]{2,1,0:T(8,128)S(1)}, f32[3,80,128]{2,1,0:T(8,128)S(1)}, u32[]{:S(2)}, u32[]{:S(2)}) %collective-permute-start.9) | collective-permute-done | bytes 122912 | tf_op jit(solution)/shard_map/ppermute | solution.py:601
  44.0 3.2 %eliminate_kernel.1 = (f32[4,4,320,256]{3,2,1,0:T(8,128)S(1)}, f32[32,8,128]{2,1,0:T(8,128)S(1)}) custom-call(s32[4]{0:T(128)S(1)} %copy-done.1, bf16[4,4,320,256]{3,2,1,0:T(8,128)(2,1)S(1)} %copy-done, f32[4,4,320,256]{3,2,1,0:T(8,128)S(1)} %get-tuple-element.34.product, bf16[4,4,80,320]{3,2,1,0:T(8,128)(2,1)S(1)} %get-tuple-element.28.lower, ...), custom_call_target="tpu_custom_call" | custom-call | flops 1000000000 | bytes 10000000 | tf_op jit(solution)/shard_map/eliminate_kernel/pallas_call | solution.py:491
  47.2 15.2 %all_to_all.10.tiles_in = f32[32,8,128]{2,1,0:T(8,128)S(1)} all-to-all(f32[32,8,128]{2,1,0:T(8,128)S(1)} %get-tuple-element.40), channel_id=1, replica_groups=mesh['y'=4,'core'=2,'x'=4,'z'=8] {'x','z'}, dimensions={0} | all-to-all | bytes 262144 | tf_op jit(solution)/shard_map/all_to_all | solution.py:610
  62.4 0.1 merge_kernel.1
  62.5 11.7 %all_to_all.11.tiles = f32[8,8,128]{2,1,0:T(8,128)S(1)} all-to-all(f32[8,8,128]{2,1,0:T(8,128)S(1)} %merge_kernel.1), channel_id=1, replica_groups=mesh['y'=4,'core'=2,'x'=4,'z'=8] {'y','core'}, dimensions={0} | all-to-all | bytes 65536 | tf_op jit(solution)/shard_map/all_to_all | solution.py:612
  74.1 2.8 %finish_kernel.1 = (bf16[4,4,320,256]{3,2,1,0:T(8,128)(2,1)}, f32[2,256]{1,0:T(2,128)}) custom-call(s32[4]{0:T(128)S(1)} %copy-done.1, f32[8,8,128]{2,1,0:T(8,128)S(1)} %all_to_all.11.tiles, bf16[4,4,320,256]{3,2,1,0:T(8,128)(2,1)S(1)} %copy-done, f32[4,4,320,256]{3,2,1,0:T(8,128)S(1)} %get-tuple-element.41.eliminated), custom_call_target="tpu_custom_call" | custom-call | tf_op jit(solution)/shard_map/finish_kernel/pallas_call | solution.py:491
  (1 shorter events, 0.0 us)
Async XLA Ops:
  2.6 23.4 %collective-permute-start.2 = (bf16[4,80,256]{2,1,0:T(8,128)(2,1)S(1)}, bf16[4,80,256]{2,1,0:T(8,128)(2,1)S(1)}, u32[]{:S(2)}, u32[]{:S(2)}) collective-permute-start(bf16[4,80,256]{2,1,0:T(8,128)(2,1)S(1)} %get-tuple-element.26), channel_id=1, source_target_pairs={{0,1},{1,0},{2,3},{3,2},{4,5},{5,4},{6,7},{7,6},{8,9},{9,8},{10,11... | collective-permute-start | bytes 491528 | tf_op jit(solution)/shard_map/ppermute | solution.py:536
  5.1 20.8 %collective-permute-start.3 = (bf16[4,80,256]{2,1,0:T(8,128)(2,1)S(1)}, bf16[4,80,256]{2,1,0:T(8,128)(2,1)S(1)}, u32[]{:S(2)}, u32[]{:S(2)}) collective-permute-start(bf16[4,80,256]{2,1,0:T(8,128)(2,1)S(1)} %get-tuple-element.27), channel_id=1, source_target_pairs={{1,2},{3,4},{5,6},{7,8},{9,10},{11,12},{13,14},{15,16},{17,18},{19... | collective-permute-start | bytes 491528 | tf_op jit(solution)/shard_map/ppermute | solution.py:538
  12.0 11.8 %collective-permute-start.1 = (bf16[3,80,256]{2,1,0:T(8,128)(2,1)S(1)}, bf16[3,80,256]{2,1,0:T(8,128)(2,1)S(1)}, u32[]{:S(2)}, u32[]{:S(2)}) collective-permute-start(bf16[3,80,256]{2,1,0:T(8,128)(2,1)S(1)} %get-tuple-element.25), channel_id=1, source_target_pairs={{32,64},{96,128},{160,192},{64,32},{128,96},{192,160},{33,65},{97,... | collective-permute-start | bytes 368648 | tf_op jit(solution)/shard_map/ppermute | solution.py:535
  16.3 4.5 %copy-start = (bf16[4,4,320,256]{3,2,1,0:T(8,128)(2,1)S(1)}, bf16[4,4,320,256]{3,2,1,0:T(8,128)(2,1)}, u32[]{:S(2)}) copy-start(bf16[4,4,320,256]{3,2,1,0:T(8,128)(2,1)} %vector.7) | copy-start | bytes 7864324
  16.3 4.5 %copy-start.1 = (s32[4]{0:T(128)S(1)}, s32[4]{0:T(128)}, u32[]{:S(2)}) copy-start(s32[4]{0:T(128)} %lengths.7) | copy-start | bytes 52
  16.4 7.5 %collective-permute-start = (bf16[3,80,256]{2,1,0:T(8,128)(2,1)S(1)}, bf16[3,80,256]{2,1,0:T(8,128)(2,1)S(1)}, u32[]{:S(2)}, u32[]{:S(2)}) collective-permute-start(bf16[3,80,256]{2,1,0:T(8,128)(2,1)S(1)} %get-tuple-element.22.after), channel_id=1, source_target_pairs={{0,32},{32,0},{1,33},{33,1},{2,34},{34,2},{3,35},{35,3},{4,36},{36... | collective-permute-start | bytes 368648 | tf_op jit(solution)/shard_map/ppermute | solution.py:533
  19.5 6.4 %collective-permute-start.4 = (f32[3,80,128]{2,1,0:T(8,128)S(1)}, f32[3,80,128]{2,1,0:T(8,128)S(1)}, u32[]{:S(2)}, u32[]{:S(2)}) collective-permute-start(f32[3,80,128]{2,1,0:T(8,128)S(1)} %get-tuple-element.32.map_here), channel_id=1, source_target_pairs={{64,0},{128,192},{65,1},{129,193},{66,2},{130,194},{67,3},{131,195... | collective-permute-start | bytes 368648 | tf_op jit(solution)/shard_map/ppermute | solution.py:555
  20.9 5.1 %copy-start.2 = (s32[1,4]{1,0:T(1,128)S(1)}, s32[1,4]{1,0:T(1,128)}, u32[]{:S(2)}) copy-start(s32[1,4]{1,0:T(1,128)} %norths.1) | copy-start | bytes 52
  29.7 3.9 %collective-permute-start.5 = (f32[3,80,512]{2,1,0:T(8,128)S(1)}, f32[3,80,512]{2,1,0:T(8,128)S(1)}, u32[]{:S(2)}, u32[]{:S(2)}) collective-permute-start(f32[3,80,512]{2,1,0:T(8,128)S(1)} %get-tuple-element.37.mine), channel_id=1, source_target_pairs={{0,32},{32,0},{1,33},{33,1},{2,34},{34,2},{3,35},{35,3},{4,36},{36... | collective-permute-start | bytes 1474568 | tf_op jit(solution)/shard_map/ppermute | solution.py:597
  34.1 4.6 %collective-permute-start.6 = (f32[3,80,128]{2,1,0:T(8,128)S(1)}, f32[3,80,128]{2,1,0:T(8,128)S(1)}, u32[]{:S(2)}, u32[]{:S(2)}) collective-permute-start(f32[3,80,128]{2,1,0:T(8,128)S(1)} %get-tuple-element.38), channel_id=1, source_target_pairs={{0,64},{64,128},{128,192},{1,65},{65,129},{129,193},{2,66},{66,130... | collective-permute-start | bytes 368648 | tf_op jit(solution)/shard_map/ppermute | solution.py:595
  35.4 6.4 %collective-permute-start.8 = (f32[3,80,128]{2,1,0:T(8,128)S(1)}, f32[3,80,128]{2,1,0:T(8,128)S(1)}, u32[]{:S(2)}, u32[]{:S(2)}) collective-permute-start(f32[3,80,128]{2,1,0:T(8,128)S(1)} %get-tuple-element.39), channel_id=1, source_target_pairs={{0,192},{1,193},{2,194},{3,195},{4,196},{5,197},{6,198},{7,199},{8... | collective-permute-start | bytes 368648 | tf_op jit(solution)/shard_map/ppermute | solution.py:595
  36.7 5.1 %collective-permute-start.7 = (f32[3,80,128]{2,1,0:T(8,128)S(1)}, f32[3,80,128]{2,1,0:T(8,128)S(1)}, u32[]{:S(2)}, u32[]{:S(2)}) collective-permute-start(f32[3,80,128]{2,1,0:T(8,128)S(1)} %get-tuple-element.39), channel_id=1, source_target_pairs={{0,128},{64,192},{1,129},{65,193},{2,130},{66,194},{3,131},{67,195... | collective-permute-start | bytes 368648 | tf_op jit(solution)/shard_map/ppermute | solution.py:595
  41.9 2.1 %collective-permute-start.9 = (f32[3,80,128]{2,1,0:T(8,128)S(1)}, f32[3,80,128]{2,1,0:T(8,128)S(1)}, u32[]{:S(2)}, u32[]{:S(2)}) collective-permute-start(f32[3,80,128]{2,1,0:T(8,128)S(1)} %arriving_kernel.1.mine), channel_id=1, source_target_pairs={{0,32},{32,0},{1,33},{33,1},{2,34},{34,2},{3,35},{35,3},{4,36},{36... | collective-permute-start | bytes 368648 | tf_op jit(solution)/shard_map/ppermute | solution.py:601

commit v3 on v2

--- a/solution.py
+++ b/solution.py
@@ -16,8 +16,7 @@
 R = 256
 ELEMENTS = LINES_HERE * SEGMENT
 HALF = 128
-OWN_MAP = slice(R, R + 80)
-Y_MAP = slice(R + HALF, R + HALF + 80)
+OWN_MAPS, Y_MAPS = MOVING, MOVING + 1
 WALL = ("y", "core")
 SURF = ("x", "z")
 F32 = jnp.float32
@@ -70,15 +69,27 @@
 def for_listed(lengths, listed, count, body, together=4, after=None):
     short = shortest_line(lengths)
 
-    @pl.loop(0, (count + together - 1) // together)
+    def one(trip):
+        entry = listed[trip]
+        slot = entry // SEGMENT
+        body(slot, line_in_slot(slot, short), entry % SEGMENT)
+
+    def group(first, size):
+        for part in range(size):
+            one(first + part)
+        if after is not None:
+            for part in range(size):
+                after(first + part)
+
+    whole = count // together
+
+    @pl.loop(0, whole)
     def _(trip):
-        for part in range(together):
-            entry = listed[jnp.minimum(trip * together + part, count - 1)]
-            slot = entry // SEGMENT
-            body(slot, line_in_slot(slot, short), entry % SEGMENT)
-        if after is not None:
-            for part in range(together):
-                after(trip * together + part)
+        group(trip * together, together)
+
+    @pl.loop(whole * together, count)
+    def _(trip):
+        group(trip, 1)
 
 
 def wall_face_rows():
@@ -94,6 +105,10 @@
 
 def a_face(block, end):
     return jnp.concatenate([block[64 * v + 16 * end : 64 * v + 16 * end + 16] for v in range(5)], axis=0)
+
+
+def partial(values):
+    return values.reshape(BLOCK // 8, 8, R).sum(axis=0)
 
 
 def split_exactly(values):
@@ -115,7 +130,28 @@
 
 
 def edges_kernel(
-    lengths_hbm, vector, over_core, over_y, over_pair, over_next, lengths, ends, west, east, sems, run_sems
+    lengths_hbm,
+    vector,
+    lifting_hbm,
+    inverse_hbm,
+    diagonal_hbm,
+    over_core,
+    over_y,
+    over_pair,
+    over_next,
+    steps,
+    prefixes,
+    whole,
+    lower,
+    inverse,
+    diagonal,
+    lengths,
+    ends,
+    west,
+    east,
+    sems,
+    run_sems,
+    block_sems,
 ):
     core, odd = lax.axis_index("core"), lax.axis_index("z") % 2
     copies = [pltpu.make_async_copy(lengths_hbm, lengths, sems.at[0])]
@@ -126,7 +162,15 @@
             source = vector.at[line, :, pl.ds(64 * run + first_row, 16)]
             target = face.at[:, pl.ds(16 * run, 16)]
             copies.append(pltpu.make_async_copy(source, target, run_sems.at[at, run]))
-    for copy in copies:
+    needed = []
+    for line in range(LINES_HERE):
+        needed.append(pltpu.make_async_copy(inverse_hbm.at[line], inverse.at[line], block_sems.at[0, line]))
+        needed.append(pltpu.make_async_copy(lifting_hbm.at[line, :, 0], lower.at[line], block_sems.at[1, line]))
+    later = [
+        pltpu.make_async_copy(diagonal_hbm.at[line], diagonal.at[line], block_sems.at[2, line])
+        for line in range(LINES_HERE)
+    ]
+    for copy in copies + needed + later:
         copy.start()
     rows = wall_face_rows()
     for copy in copies:
@@ -146,36 +190,8 @@
         from_last = jnp.where(position < last, east[position], zero)
         over_pair[position] = jnp.where(odd == 0, from_last, from_first)
         over_next[position] = jnp.where(odd == 0, from_first, from_last)
-
-
-def maps_kernel(
-    lengths_hbm,
-    after,
-    lifting_hbm,
-    inverse_hbm,
-    diagonal_hbm,
-    steps,
-    prefixes,
-    whole,
-    lower,
-    inverse,
-    diagonal,
-    lengths,
-    sems,
-    lengths_sem,
-):
-    needed = [pltpu.make_async_copy(lengths_hbm, lengths, lengths_sem)]
-    for line in range(LINES_HERE):
-        needed.append(pltpu.make_async_copy(inverse_hbm.at[line], inverse.at[line], sems.at[0, line]))
-        needed.append(pltpu.make_async_copy(lifting_hbm.at[line, :, 0], lower.at[line], sems.at[1, line]))
-    later = [
-        pltpu.make_async_copy(diagonal_hbm.at[line], diagonal.at[line], sems.at[2, line]) for line in range(LINES_HERE)
-    ]
-    for copy in needed + later:
-        copy.start()
     for copy in needed:
         copy.wait()
-    short = shortest_line(lengths)
     lines = [line_in_slot(slot, short) for slot in range(MOVING)]
     so_far = [None] * MOVING
     for position in range(SEGMENT):
@@ -193,13 +209,12 @@
             so_far[slot] = step if position == 0 else mapped(step, so_far[slot])
             if position < SEGMENT - 1:
                 prefixes[slot, position] = so_far[slot]
-    for slot in range(MOVING):
-        whole[slot] = jnp.concatenate([so_far[slot], jnp.zeros((FACE, HALF - FACE), F32)], axis=1)
+    whole[...] = jnp.concatenate(so_far + [jnp.zeros((FACE, R - MOVING * FACE), F32)], axis=1)
     for copy in later:
         copy.wait()
 
 
-def diagonal_kernel(lengths, vector, diagonal, lifting_hbm, product, traces, lifting, listed, wide, sems):
+def diagonal_kernel(lengths, vector, diagonal, lifting_hbm, product, traces, lifting, squares, listed, wide, sems):
     copies = [
         pltpu.make_async_copy(lifting_hbm.at[line, :, pl.ds(1, 5)], lifting.at[line], sems.at[line])
         for line in range(LINES_HERE)
@@ -214,10 +229,13 @@
             def _():
                 traces[line, position] = jnp.zeros((6, FACE, R), BF16)
 
+    squares[...] = jnp.zeros_like(squares)
+
     def body(slot, line, position):
         values = vector[line, position]
         product[line, position] = jnp.dot(diagonal[line, position], values, preferred_element_type=F32)
         whole = values.astype(F32)
+        squares[...] += partial(whole * whole)
         for half in range(2):
             columns = slice(half * HALF, (half + 1) * HALF)
             wide[half] = whole[:, columns]
@@ -316,18 +334,24 @@
             carries[slot, position - 1] = carried[slot]
             carried[slot] = driven[slot, position] + mapped(steps[slot, position], carried[slot])
     for slot in range(MOVING):
-        outgoing[slot] = jnp.concatenate([carried[slot], map_here[slot], map_y[slot]], axis=1)
+        outgoing[slot] = carried[slot]
+    outgoing[OWN_MAPS] = map_here[...]
+    outgoing[Y_MAPS] = map_y[...]
+
+
+def map_of(maps, slot):
+    return maps[:, slot * FACE : (slot + 1) * FACE]
 
 
 def chip_kernel(mine, other, near, far):
     core, y = lax.axis_index("core"), lax.axis_index("y")
+    second_maps = jnp.where(core == 0, other[OWN_MAPS], mine[OWN_MAPS])
     values = []
     for slot in range(MOVING):
         own, away = mine[slot], other[slot]
-        first_value = jnp.where(core == 0, own[:, :HALF], away[:, HALF:R])
-        second_value = jnp.where(core == 0, away[:, :HALF], own[:, HALF:R])
-        second_map = jnp.where(core == 0, away[:, OWN_MAP], own[:, OWN_MAP])
-        values.append(mapped(second_map, first_value) + second_value)
+        first_value = jnp.where(core == 0, own[:, :HALF], away[:, HALF:])
+        second_value = jnp.where(core == 0, away[:, :HALF], own[:, HALF:])
+        values.append(mapped(map_of(second_maps, slot), first_value) + second_value)
     for slot in range(MOVING):
         near[slot] = values[slot]
         far[slot] = values[slot]
@@ -339,13 +363,11 @@
 
 def through_chip(mine, other, values, results):
     core = lax.axis_index("core")
-    moved = []
-    for slot, value in enumerate(values):
-        own, away = mine[slot][:, Y_MAP], other[slot][:, Y_MAP]
-        moved.append(mapped(jnp.where(core == 0, own, away), value))
+    first_maps = jnp.where(core == 0, mine[Y_MAPS], other[Y_MAPS])
+    second_maps = jnp.where(core == 0, other[Y_MAPS], mine[Y_MAPS])
+    moved = [mapped(map_of(first_maps, slot), value) for slot, value in enumerate(values)]
     for slot, value in enumerate(moved):
-        own, away = mine[slot][:, Y_MAP], other[slot][:, Y_MAP]
-        results[slot] = mapped(jnp.where(core == 0, away, own), value)
+        results[slot] = mapped(map_of(second_maps, slot), value)
 
 
 def arriving_kernel(one, two, three, mine, other, arriving):
@@ -365,6 +387,7 @@
 def eliminate_kernel(
     lengths,
     vector,
+    squares,
     product,
     lower,
     prefixes,
@@ -376,6 +399,7 @@
     tiles,
     listed,
     entering,
+    sums,
 ):
     core = lax.axis_index("core")
     short = shortest_line(lengths)
@@ -385,7 +409,7 @@
         left = jnp.where(core == 0, mine[slot], other[slot])
         right = jnp.where(core == 0, other[slot], mine[slot])
         value = jnp.concatenate([left, right], axis=1)
-        passed = mapped(beside[slot][:, OWN_MAP], value) + beside[slot][:, :R]
+        passed = mapped(map_of(beside[OWN_MAPS], slot), value) + beside[slot]
         values.append(jnp.where(core == 0, value, passed))
     for slot, value in enumerate(values):
         entering[slot, 0] = value
@@ -394,40 +418,28 @@
             entering[slot, position] = carries[slot, position - 1] + moved[(position - 1) * FACE : position * FACE]
 
     count = list_living(lengths, listed)
-    nothing = jnp.zeros((8, R), F32)
-
-    def of(trip):
-        entry = listed[trip]
-        slot = entry // SEGMENT
-        return slot, line_in_slot(slot, short), entry % SEGMENT
-
-    def partial(values):
-        return values.reshape(BLOCK // 8, 8, R).sum(axis=0)
+    sums[...] = jnp.zeros_like(sums)
 
     def correct(slot, line, position):
         high, low = split_exactly(entering[slot, position])
         block = lower[line, position]
         correction = transposed_times(jnp.concatenate([block, block], axis=0), jnp.concatenate([high, low], axis=0))
-        eliminated[line, position] = product[line, position] - correction
+        value = product[line, position] - correction
+        eliminated[line, position] = value
+        masked = vector[line, position].astype(F32)
+        sums[0] += partial(masked * value)
 
     for_listed(lengths, listed, count, correct)
-
-    def products(trip, sums):
-        _, line, position = of(trip)
-        masked, value = vector[line, position].astype(F32), eliminated[line, position]
-        return sums[0] + partial(masked * value), sums[1] + partial(masked * masked)
-
-    cross, square = lax.fori_loop(0, count, products, (nothing, nothing))
-    cross = cross.sum(axis=0, keepdims=True)
-    square = square.sum(axis=0, keepdims=True)
+    cross = sums[0].sum(axis=0, keepdims=True)
+    square = squares[...].sum(axis=0, keepdims=True)
     share = jnp.where(square > 0, cross / square, 0.0)
 
-    def left_over(trip, total):
-        _, line, position = of(trip)
+    def leave(slot, line, position):
         rest = eliminated[line, position] - share * vector[line, position].astype(F32)
-        return total + partial(rest * rest)
-
-    rest = lax.fori_loop(0, count, left_over, nothing).sum(axis=0, keepdims=True)
+        sums[1] += partial(rest * rest)
+
+    for_listed(lengths, listed, count, leave)
+    rest = sums[1].sum(axis=0, keepdims=True)
     pieces = [part[:, at : at + HALF] for part in (cross, square, rest) for at in (0, HALF)]
     tile = jnp.concatenate(pieces + [jnp.zeros((2, HALF), F32)], axis=0)
     for copy in range(tiles.shape[0]):
@@ -476,11 +488,9 @@
         held[line, position] = ((eliminated[line, position] - ratio * masked) * scale).astype(BF16)
 
     def after(trip):
-        @pl.when(trip < count)
-        def _():
-            copy_of(trip).start()
-
-    for_listed(lengths, listed, count, body, 2, after)
+        copy_of(trip).start()
+
+    for_listed(lengths, listed, count, body, 4, after)
 
     @pl.loop(0, ELEMENTS)
     def _(trip):
@@ -513,10 +523,22 @@
 def per_device(vector, lengths, north_of, diagonal, lifting, inverse_rows):
     edge = shaped(MOVING, FACE, R, dtype=BF16)
     side = shaped(SEGMENT, FACE, R, dtype=BF16)
-    over_core, over_y, over_pair, over_next = call(
+    blocks = shaped(LINES_HERE, SEGMENT, FACE, BLOCK, dtype=BF16)
+    over_core, over_y, over_pair, over_next, steps, prefixes, whole, lower, inverse, diagonal_here = call(
         edges_kernel,
-        (edge, edge, side, side),
-        (lengths, vector),
+        (
+            edge,
+            edge,
+            side,
+            side,
+            shaped(MOVING, SEGMENT, FACE, FACE),
+            shaped(MOVING, SEGMENT - 1, FACE, FACE),
+            shaped(FACE, R),
+            blocks,
+            blocks,
+            shaped(LINES_HERE, SEGMENT, BLOCK, BLOCK, dtype=BF16),
+        ),
+        (lengths, vector, lifting, inverse_rows, diagonal),
         (
             pltpu.SMEM((LINES_HERE,), jnp.int32),
             pltpu.VMEM((2, LINES_HERE, BLOCK, R), BF16),
@@ -524,12 +546,12 @@
             pltpu.VMEM((SEGMENT, FACE, R), BF16),
             pltpu.SemaphoreType.DMA((3,)),
             pltpu.SemaphoreType.DMA((2, 5)),
+            pltpu.SemaphoreType.DMA((3, LINES_HERE)),
         ),
-        in_hbm=(0, 1),
+        in_hbm=(0, 1, 2, 3, 4),
     )
     walls, surfs = lax.axis_size(WALL), lax.axis_size(SURF)
     swap = [(0, 1), (1, 0)]
-    first_edge = over_core
     over_core = lax.ppermute(over_core, "core", swap)
     rungs = [(i, i + 1) for i in range(1, walls - 1, 2)]
     over_y = lax.ppermute(over_y, WALL, rungs + [(b, a) for a, b in rungs])
@@ -537,28 +559,14 @@
     nexts = [(i, (i + 1) % surfs) for i in range(1, surfs, 2)]
     over_next = lax.ppermute(over_next, SURF, nexts + [(b, a) for a, b in nexts])
 
-    blocks = shaped(LINES_HERE, SEGMENT, FACE, BLOCK, dtype=BF16)
-    steps, prefixes, whole, lower, inverse, diagonal_here = call(
-        maps_kernel,
-        (
-            shaped(MOVING, SEGMENT, FACE, FACE),
-            shaped(MOVING, SEGMENT - 1, FACE, FACE),
-            shaped(MOVING, FACE, HALF),
-            blocks,
-            blocks,
-            shaped(LINES_HERE, SEGMENT, BLOCK, BLOCK, dtype=BF16),
-        ),
-        (lengths, first_edge, lifting, inverse_rows, diagonal),
-        (pltpu.SMEM((LINES_HERE,), jnp.int32), pltpu.SemaphoreType.DMA((3, LINES_HERE)), pltpu.SemaphoreType.DMA),
-        in_hbm=(0, 2, 3, 4),
-    )
     map_y = lax.ppermute(whole, "y", [(1, 0), (2, 3)])
-    product, traces, lifting_here = call(
+    product, traces, lifting_here, squares = call(
         diagonal_kernel,
         (
             shaped(LINES_HERE, SEGMENT, BLOCK, R),
             shaped(LINES_HERE, SEGMENT, 6, FACE, R, dtype=BF16),
             shaped(LINES_HERE, SEGMENT, 5, FACE, BLOCK, dtype=BF16),
+            shaped(8, R),
         ),
         (lengths, vector, diagonal_here, lifting),
         (LISTED, pltpu.VMEM((2, BLOCK, HALF), F32), pltpu.SemaphoreType.DMA((LINES_HERE,))),
@@ -569,7 +577,7 @@
         (
             shaped(LINES_HERE, SEGMENT, BLOCK, R),
             shaped(MOVING, SEGMENT - 1, FACE, R),
-            shaped(MOVING, FACE, R + 2 * HALF),
+            shaped(MOVING + 2, FACE, R),
         ),
         (
             lengths,
@@ -602,8 +610,8 @@
     eliminated, tiles = call(
         eliminate_kernel,
         (shaped(LINES_HERE, SEGMENT, BLOCK, R), shaped(surfs, 8, HALF)),
-        (lengths, vector, product, lower, prefixes, carries, arriving, arriving_beside, beside),
-        (LISTED, pltpu.VMEM((LINES_HERE, SEGMENT, FACE, R), F32)),
+        (lengths, vector, squares, product, lower, prefixes, carries, arriving, arriving_beside, beside),
+        (LISTED, pltpu.VMEM((LINES_HERE, SEGMENT, FACE, R), F32), pltpu.VMEM((2, 8, R), F32)),
         flops=10**9,
         moved=10**7,
     )

time: 76.6 us -> 74.9 us (0.978); the launches traced: 77 us -> 74.2 us
  blocking collectives: 26.9 us -> 23.8 us
  waiting for transfers between devices: 7.72 us -> 5.88 us
  starting transfers between devices: 23.1 us -> 24.3 us
  Pallas kernels: 18.4 us -> 19.4 us
    ppermute x3, starting transfers between devices: 4.55 us -> 7.87 us  [up_chips(): return lax.ppermute(value, 'y', [(i, i + far) for i in range(ranks - far)])]
    all_to_all x1, blocking collectives: 15.2 us -> 12.1 us  [per_device(): tiles = lax.all_to_all(tiles, SURF, 0, 0, tiled=True)]
    ppermute x1, starting transfers between devices: 2.37 us -> 0.09 us  [per_device(): beside = lax.ppermute(outgoing, 'core', swap)]
    ppermute x1, starting transfers between devices: 4.31 us -> 3.07 us  [per_device(): over_y = lax.ppermute(over_y, WALL, rungs + [(b, a) for a, b in rungs])]
    ppermute x1, waiting for transfers between devices: 2.1 us -> 0.87 us  [per_device(): map_y = lax.ppermute(whole, 'y', [(1, 0), (2, 3)])]
    ppermute x1, starting transfers between devices: 0.09 us -> 1.23 us  [per_device(): over_core = lax.ppermute(over_core, 'core', swap)]
    pallas_call x9 -> x8, Pallas kernels: 18.4 us -> 19.4 us  [call(): pl.pallas_call(kernel, out_shape=outs, in_specs=[pl.BlockSpec(memory_spac...]
    ppermute x3, waiting for transfers between devices: 3.15 us -> 2.29 us  [up_chips(): return lax.ppermute(value, 'y', [(i, i + far) for i in range(ranks - far)])]
  transfers between devices with their start and end apart: 10 -> 10, of which waited for: 4 -> 4; matrix products, arithmetic and copies ran while one was open for 0% -> 0% of each run, Pallas kernels for 8% -> 4%
where the time goes in v3:
time: 74.9 us; the launch traced here: 74.2 us
  starting transfers between devices  24.3 us (32%)
  blocking collectives  23.8 us (32%)
  Pallas kernels  19.4 us (26%)
  waiting for transfers between devices  5.88 us (8%)
  between operations  0.8 us (1%)
    pallas_call x8, Pallas kernels, call(): pl.pallas_call(kernel, out_shape=outs, in_specs=[pl.BlockSpec(memory_spac...  19.4 us
    all_to_all x1, blocking collectives, per_device(): tiles = lax.all_to_all(tiles, SURF, 0, 0, tiled=True)  12.1 us
    all_to_all x1, blocking collectives, per_device(): tiles = lax.all_to_all(tiles, WALL, 0, 0, tiled=True)  11.7 us
    ppermute x3, starting transfers between devices, up_chips(): return lax.ppermute(value, 'y', [(i, i + far) for i in range(ranks - far)])  7.87 us
    ppermute x1, starting transfers between devices, per_device(): lax.ppermute(over_next, SURF, nexts + [(b, a) for a, b in nexts])  6.86 us
    ppermute x1, starting transfers between devices, per_device(): over_y = lax.ppermute(over_y, WALL, rungs + [(b, a) for a, b in rungs])  3.07 us
    ppermute x1, starting transfers between devices, per_device(): lax.ppermute(over_pair, SURF, [(i, i ^ 1) for i in range(surfs)])  2.55 us
    ppermute x3, waiting for transfers between devices, up_chips(): return lax.ppermute(value, 'y', [(i, i + far) for i in range(ranks - far)])  2.29 us
  transfers between devices with their start and end apart: 10, of which 4 were waited for; matrix products, arithmetic and copies ran while one was open for 0% of the time, Pallas kernels for 4%

profile of v3, /device:TPU:1, one launch (start us, length us, event | category | flops | bytes accessed | tf_op | source)
XLA Modules:
  0.0 74.2 jit_solution(3184179569203511615)
XLA Ops:
  0.6 0.0 copy-start.1
  0.6 0.0 copy-start
  0.7 4.6 %edges_kernel.1 = (bf16[3,80,256]{2,1,0:T(8,128)(2,1)S(1)}, bf16[3,80,256]{2,1,0:T(8,128)(2,1)S(1)}, bf16[4,80,256]{2,1,0:T(8,128)(2,1)S(1)}, bf16[4,80,256]{2,1...) custom-call(s32[4]{0:T(128)} %lengths.7, ...), custom_call_target="tpu_custom_call" | custom-call | tf_op jit(solution)/shard_map/edges_kernel/pallas_call | solution.py:501
  5.3 2.6 %collective-permute-start.2 = (bf16[4,80,256]{2,1,0:T(8,128)(2,1)S(1)}, bf16[4,80,256]{2,1,0:T(8,128)(2,1)S(1)}, u32[]{:S(2)}, u32[]{:S(2)}) collective-permute-start(bf16[4,80,256]{2,1,0:T(8,128)(2,1)S(1)} %get-tuple-element.28), channel_id=1, source_target_pairs={{0,1},{1,0},{2,3},{3,2},{4,5},{5,4},{6,7},{7,6},{8,9},{9,8},{10,11... | collective-permute-start | bytes 491528 | tf_op jit(solution)/shard_map/ppermute | solution.py:558
  7.8 6.9 %collective-permute-start.3 = (bf16[4,80,256]{2,1,0:T(8,128)(2,1)S(1)}, bf16[4,80,256]{2,1,0:T(8,128)(2,1)S(1)}, u32[]{:S(2)}, u32[]{:S(2)}) collective-permute-start(bf16[4,80,256]{2,1,0:T(8,128)(2,1)S(1)} %get-tuple-element.29), channel_id=1, source_target_pairs={{1,2},{3,4},{5,6},{7,8},{9,10},{11,12},{13,14},{15,16},{17,18},{19... | collective-permute-start | bytes 491528 | tf_op jit(solution)/shard_map/ppermute | solution.py:560
  14.7 1.2 %collective-permute-start = (bf16[3,80,256]{2,1,0:T(8,128)(2,1)S(1)}, bf16[3,80,256]{2,1,0:T(8,128)(2,1)S(1)}, u32[]{:S(2)}, u32[]{:S(2)}) collective-permute-start(bf16[3,80,256]{2,1,0:T(8,128)(2,1)S(1)} %get-tuple-element.26), channel_id=1, source_target_pairs={{0,32},{32,0},{1,33},{33,1},{2,34},{34,2},{3,35},{35,3},{4,36},{36... | collective-permute-start | bytes 368648 | tf_op jit(solution)/shard_map/ppermute | solution.py:555
  15.9 3.1 %collective-permute-start.1 = (bf16[3,80,256]{2,1,0:T(8,128)(2,1)S(1)}, bf16[3,80,256]{2,1,0:T(8,128)(2,1)S(1)}, u32[]{:S(2)}, u32[]{:S(2)}) collective-permute-start(bf16[3,80,256]{2,1,0:T(8,128)(2,1)S(1)} %get-tuple-element.27), channel_id=1, source_target_pairs={{32,64},{96,128},{160,192},{64,32},{128,96},{192,160},{33,65},{97,... | collective-permute-start | bytes 368648 | tf_op jit(solution)/shard_map/ppermute | solution.py:557
  19.0 1.3 %collective-permute-start.4 = (f32[80,256]{1,0:T(8,128)S(1)}, f32[80,256]{1,0:T(8,128)S(1)}, u32[]{:S(2)}, u32[]{:S(2)}) collective-permute-start(f32[80,256]{1,0:T(8,128)S(1)} %get-tuple-element.34.map_here), channel_id=1, source_target_pairs={{64,0},{128,192},{65,1},{129,193},{66,2},{130,194},{67,3},{131,195... | collective-permute-start | bytes 245768 | tf_op jit(solution)/shard_map/ppermute | solution.py:562
  20.3 0.0 copy-done.1
  20.3 0.0 copy-done
  20.3 0.0 copy-start.2
  20.3 3.0 %diagonal_kernel.1 = (f32[4,4,320,256]{3,2,1,0:T(8,128)S(1)}, bf16[4,4,6,80,256]{4,3,2,1,0:T(8,128)(2,1)S(1)}, bf16[4,4,5,80,320]{4,3,2,1,0:T(8,128)(2,1)S(1)}, f32[8,256]{1,0:T(8,128)S(1)}) custom-call(s32[4]{0:T(128)S(1)} %copy-done.1, bf16[4,4,320,256]{3,2,1,0:T(8,128)(2,1)S(1)} %copy-done, bf16[4,4,320,320]{3,2,1,0:T(8,128)(2,1)S(1)} %get-tuple-element.23.diagonal, ...), custom_call_target="tpu_custom_call" | custom-call | tf_op jit(solution)/shard_map/diagonal_kernel/pallas_call | solution.py:501
  23.3 0.9 %collective-permute-done.4.map_y = f32[80,256]{1,0:T(8,128)S(1)} collective-permute-done((f32[80,256]{1,0:T(8,128)S(1)}, f32[80,256]{1,0:T(8,128)S(1)}, u32[]{:S(2)}, u32[]{:S(2)}) %collective-permute-start.4) | collective-permute-done | bytes 81952 | tf_op jit(solution)/shard_map/ppermute | solution.py:562
  24.2 0.0 collective-permute-done.over_core
  24.2 0.0 collective-permute-done.1.over_y
  24.2 0.0 collective-permute-done.2.over_pair
  24.2 0.0 collective-permute-done.3.over_next
  24.2 0.0 copy-done.2
  24.2 4.8 %product_kernel.1 = (f32[4,4,320,256]{3,2,1,0:T(8,128)S(1)}, f32[3,3,80,256]{3,2,1,0:T(8,128)S(1)}, f32[5,80,256]{2,1,0:T(8,128)S(1)}) custom-call(s32[4]{0:T(128)S(1)} %copy-done.1, s32[1,4]{1,0:T(1,128)S(1)} %copy-done.2, bf16[4,4,6,80,256]{4,3,2,1,0:T(8,128)(2,1)S(1)} %get-tuple-element.25.traces, bf16[3,80,256]{2,1,0:T(8,128)(2,1)S(1)} %collective-permute-done.over_core, ...), custom_call_target="tpu_custom_call" | custom-call | tf_op jit(solution)/shard_map/product_kernel/pallas_call | solution.py:501
  29.0 0.1 collective-permute-start.5
  29.1 1.7 %collective-permute-done.5.other.beside = f32[5,80,256]{2,1,0:T(8,128)S(1)} collective-permute-done((f32[5,80,256]{2,1,0:T(8,128)S(1)}, f32[5,80,256]{2,1,0:T(8,128)S(1)}, u32[]{:S(2)}, u32[]{:S(2)}) %collective-permute-start.5) | collective-permute-done | bytes 409632 | tf_op jit(solution)/shard_map/ppermute | solution.py:605
  30.8 0.7 chip_kernel.1
  31.5 2.7 %collective-permute-start.6 = (f32[3,80,128]{2,1,0:T(8,128)S(1)}, f32[3,80,128]{2,1,0:T(8,128)S(1)}, u32[]{:S(2)}, u32[]{:S(2)}) collective-permute-start(f32[3,80,128]{2,1,0:T(8,128)S(1)} %get-tuple-element.40), channel_id=1, source_target_pairs={{0,64},{64,128},{128,192},{1,65},{65,129},{129,193},{2,66},{66,130... | collective-permute-start | bytes 368648 | tf_op jit(solution)/shard_map/ppermute | solution.py:603
  34.2 2.2 %collective-permute-start.8 = (f32[3,80,128]{2,1,0:T(8,128)S(1)}, f32[3,80,128]{2,1,0:T(8,128)S(1)}, u32[]{:S(2)}, u32[]{:S(2)}) collective-permute-start(f32[3,80,128]{2,1,0:T(8,128)S(1)} %get-tuple-element.41), channel_id=1, source_target_pairs={{0,192},{1,193},{2,194},{3,195},{4,196},{5,197},{6,198},{7,199},{8... | collective-permute-start | bytes 368648 | tf_op jit(solution)/shard_map/ppermute | solution.py:603
  36.4 3.0 %collective-permute-start.7 = (f32[3,80,128]{2,1,0:T(8,128)S(1)}, f32[3,80,128]{2,1,0:T(8,128)S(1)}, u32[]{:S(2)}, u32[]{:S(2)}) collective-permute-start(f32[3,80,128]{2,1,0:T(8,128)S(1)} %get-tuple-element.41), channel_id=1, source_target_pairs={{0,128},{64,192},{1,129},{65,193},{2,130},{66,194},{3,131},{67,195... | collective-permute-start | bytes 368648 | tf_op jit(solution)/shard_map/ppermute | solution.py:603
  39.4 0.0 collective-permute-done.6.one
  39.4 0.0 collective-permute-done.8.three
  39.4 2.3 %collective-permute-done.7.two = f32[3,80,128]{2,1,0:T(8,128)S(1)} collective-permute-done((f32[3,80,128]{2,1,0:T(8,128)S(1)}, f32[3,80,128]{2,1,0:T(8,128)S(1)}, u32[]{:S(2)}, u32[]{:S(2)}) %collective-permute-start.7) | collective-permute-done | bytes 122912 | tf_op jit(solution)/shard_map/ppermute | solution.py:603
  41.7 1.3 %collective-permute-start.9 = (f32[3,80,128]{2,1,0:T(8,128)S(1)}, f32[3,80,128]{2,1,0:T(8,128)S(1)}, u32[]{:S(2)}, u32[]{:S(2)}) collective-permute-start(f32[3,80,128]{2,1,0:T(8,128)S(1)} %arriving_kernel.1.mine), channel_id=1, source_target_pairs={{0,32},{32,0},{1,33},{33,1},{2,34},{34,2},{3,35},{35,3},{4,36},{36... | collective-permute-start | bytes 368648 | tf_op jit(solution)/shard_map/ppermute | solution.py:609
  43.0 1.0 %collective-permute-done.9.other = f32[3,80,128]{2,1,0:T(8,128)S(1)} collective-permute-done((f32[3,80,128]{2,1,0:T(8,128)S(1)}, f32[3,80,128]{2,1,0:T(8,128)S(1)}, u32[]{:S(2)}, u32[]{:S(2)}) %collective-permute-start.9) | collective-permute-done | bytes 122912 | tf_op jit(solution)/shard_map/ppermute | solution.py:609
  44.0 3.3 %eliminate_kernel.1 = (f32[4,4,320,256]{3,2,1,0:T(8,128)S(1)}, f32[32,8,128]{2,1,0:T(8,128)S(1)}) custom-call(s32[4]{0:T(128)S(1)} %copy-done.1, bf16[4,4,320,256]{3,2,1,0:T(8,128)(2,1)S(1)} %copy-done, f32[8,256]{1,0:T(8,128)S(1)} %get-tuple-element.24.squares, f32[4,4,320,256]{3,2,1,0:T(8,128)S(1)} %get-tuple-element.36.product, ...), custom_call_target="tpu_custom_call" | custom-call | flops 1000000000 | bytes 10000000 | tf_op jit(solution)/shard_map/eliminate_kernel/pallas_call | solution.py:501
  47.3 12.1 %all_to_all.10.tiles_in = f32[32,8,128]{2,1,0:T(8,128)S(1)} all-to-all(f32[32,8,128]{2,1,0:T(8,128)S(1)} %get-tuple-element.42), channel_id=1, replica_groups=mesh['y'=4,'core'=2,'x'=4,'z'=8] {'x','z'}, dimensions={0} | all-to-all | bytes 262144 | tf_op jit(solution)/shard_map/all_to_all | solution.py:618
  59.4 0.1 merge_kernel.1
  59.5 11.7 %all_to_all.11.tiles = f32[8,8,128]{2,1,0:T(8,128)S(1)} all-to-all(f32[8,8,128]{2,1,0:T(8,128)S(1)} %merge_kernel.1), channel_id=1, replica_groups=mesh['y'=4,'core'=2,'x'=4,'z'=8] {'y','core'}, dimensions={0} | all-to-all | bytes 65536 | tf_op jit(solution)/shard_map/all_to_all | solution.py:620
  71.2 3.0 %finish_kernel.1 = (bf16[4,4,320,256]{3,2,1,0:T(8,128)(2,1)}, f32[2,256]{1,0:T(2,128)}) custom-call(s32[4]{0:T(128)S(1)} %copy-done.1, f32[8,8,128]{2,1,0:T(8,128)S(1)} %all_to_all.11.tiles, bf16[4,4,320,256]{3,2,1,0:T(8,128)(2,1)S(1)} %copy-done, f32[4,4,320,256]{3,2,1,0:T(8,128)S(1)} %get-tuple-element.43.eliminated), custom_call_target="tpu_custom_call" | custom-call | tf_op jit(solution)/shard_map/finish_kernel/pallas_call | solution.py:501
  (1 shorter events, 0.0 us)
Async XLA Ops:
  0.6 19.7 %copy-start.1 = (s32[4]{0:T(128)S(1)}, s32[4]{0:T(128)}, u32[]{:S(2)}) copy-start(s32[4]{0:T(128)} %lengths.7) | copy-start | bytes 52
  0.6 19.7 %copy-start = (bf16[4,4,320,256]{3,2,1,0:T(8,128)(2,1)S(1)}, bf16[4,4,320,256]{3,2,1,0:T(8,128)(2,1)}, u32[]{:S(2)}) copy-start(bf16[4,4,320,256]{3,2,1,0:T(8,128)(2,1)} %vector.7) | copy-start | bytes 7864324
  5.3 18.9 %collective-permute-start.2 = (bf16[4,80,256]{2,1,0:T(8,128)(2,1)S(1)}, bf16[4,80,256]{2,1,0:T(8,128)(2,1)S(1)}, u32[]{:S(2)}, u32[]{:S(2)}) collective-permute-start(bf16[4,80,256]{2,1,0:T(8,128)(2,1)S(1)} %get-tuple-element.28), channel_id=1, source_target_pairs={{0,1},{1,0},{2,3},{3,2},{4,5},{5,4},{6,7},{7,6},{8,9},{9,8},{10,11... | collective-permute-start | bytes 491528 | tf_op jit(solution)/shard_map/ppermute | solution.py:558
  7.8 16.4 %collective-permute-start.3 = (bf16[4,80,256]{2,1,0:T(8,128)(2,1)S(1)}, bf16[4,80,256]{2,1,0:T(8,128)(2,1)S(1)}, u32[]{:S(2)}, u32[]{:S(2)}) collective-permute-start(bf16[4,80,256]{2,1,0:T(8,128)(2,1)S(1)} %get-tuple-element.29), channel_id=1, source_target_pairs={{1,2},{3,4},{5,6},{7,8},{9,10},{11,12},{13,14},{15,16},{17,18},{19... | collective-permute-start | bytes 491528 | tf_op jit(solution)/shard_map/ppermute | solution.py:560
  14.7 9.5 %collective-permute-start = (bf16[3,80,256]{2,1,0:T(8,128)(2,1)S(1)}, bf16[3,80,256]{2,1,0:T(8,128)(2,1)S(1)}, u32[]{:S(2)}, u32[]{:S(2)}) collective-permute-start(bf16[3,80,256]{2,1,0:T(8,128)(2,1)S(1)} %get-tuple-element.26), channel_id=1, source_target_pairs={{0,32},{32,0},{1,33},{33,1},{2,34},{34,2},{3,35},{35,3},{4,36},{36... | collective-permute-start | bytes 368648 | tf_op jit(solution)/shard_map/ppermute | solution.py:555
  15.9 8.3 %collective-permute-start.1 = (bf16[3,80,256]{2,1,0:T(8,128)(2,1)S(1)}, bf16[3,80,256]{2,1,0:T(8,128)(2,1)S(1)}, u32[]{:S(2)}, u32[]{:S(2)}) collective-permute-start(bf16[3,80,256]{2,1,0:T(8,128)(2,1)S(1)} %get-tuple-element.27), channel_id=1, source_target_pairs={{32,64},{96,128},{160,192},{64,32},{128,96},{192,160},{33,65},{97,... | collective-permute-start | bytes 368648 | tf_op jit(solution)/shard_map/ppermute | solution.py:557
  19.0 5.2 %collective-permute-start.4 = (f32[80,256]{1,0:T(8,128)S(1)}, f32[80,256]{1,0:T(8,128)S(1)}, u32[]{:S(2)}, u32[]{:S(2)}) collective-permute-start(f32[80,256]{1,0:T(8,128)S(1)} %get-tuple-element.34.map_here), channel_id=1, source_target_pairs={{64,0},{128,192},{65,1},{129,193},{66,2},{130,194},{67,3},{131,195... | collective-permute-start | bytes 245768 | tf_op jit(solution)/shard_map/ppermute | solution.py:562
  20.3 3.9 %copy-start.2 = (s32[1,4]{1,0:T(1,128)S(1)}, s32[1,4]{1,0:T(1,128)}, u32[]{:S(2)}) copy-start(s32[1,4]{1,0:T(1,128)} %norths.1) | copy-start | bytes 52
  29.0 1.8 %collective-permute-start.5 = (f32[5,80,256]{2,1,0:T(8,128)S(1)}, f32[5,80,256]{2,1,0:T(8,128)S(1)}, u32[]{:S(2)}, u32[]{:S(2)}) collective-permute-start(f32[5,80,256]{2,1,0:T(8,128)S(1)} %get-tuple-element.39.mine), channel_id=1, source_target_pairs={{0,32},{32,0},{1,33},{33,1},{2,34},{34,2},{3,35},{35,3},{4,36},{36... | collective-permute-start | bytes 1228808 | tf_op jit(solution)/shard_map/ppermute | solution.py:605
  31.5 7.9 %collective-permute-start.6 = (f32[3,80,128]{2,1,0:T(8,128)S(1)}, f32[3,80,128]{2,1,0:T(8,128)S(1)}, u32[]{:S(2)}, u32[]{:S(2)}) collective-permute-start(f32[3,80,128]{2,1,0:T(8,128)S(1)} %get-tuple-element.40), channel_id=1, source_target_pairs={{0,64},{64,128},{128,192},{1,65},{65,129},{129,193},{2,66},{66,130... | collective-permute-start | bytes 368648 | tf_op jit(solution)/shard_map/ppermute | solution.py:603
  34.2 5.2 %collective-permute-start.8 = (f32[3,80,128]{2,1,0:T(8,128)S(1)}, f32[3,80,128]{2,1,0:T(8,128)S(1)}, u32[]{:S(2)}, u32[]{:S(2)}) collective-permute-start(f32[3,80,128]{2,1,0:T(8,128)S(1)} %get-tuple-element.41), channel_id=1, source_target_pairs={{0,192},{1,193},{2,194},{3,195},{4,196},{5,197},{6,198},{7,199},{8... | collective-permute-start | bytes 368648 | tf_op jit(solution)/shard_map/ppermute | solution.py:603
  36.4 5.3 %collective-permute-start.7 = (f32[3,80,128]{2,1,0:T(8,128)S(1)}, f32[3,80,128]{2,1,0:T(8,128)S(1)}, u32[]{:S(2)}, u32[]{:S(2)}) collective-permute-start(f32[3,80,128]{2,1,0:T(8,128)S(1)} %get-tuple-element.41), channel_id=1, source_target_pairs={{0,128},{64,192},{1,129},{65,193},{2,130},{66,194},{3,131},{67,195... | collective-permute-start | bytes 368648 | tf_op jit(solution)/shard_map/ppermute | solution.py:603
  41.7 2.3 %collective-permute-start.9 = (f32[3,80,128]{2,1,0:T(8,128)S(1)}, f32[3,80,128]{2,1,0:T(8,128)S(1)}, u32[]{:S(2)}, u32[]{:S(2)}) collective-permute-start(f32[3,80,128]{2,1,0:T(8,128)S(1)} %arriving_kernel.1.mine), channel_id=1, source_target_pairs={{0,32},{32,0},{1,33},{33,1},{2,34},{34,2},{3,35},{35,3},{4,36},{36... | collective-permute-start | bytes 368648 | tf_op jit(solution)/shard_map/ppermute | solution.py:609

commit v4 on v3

--- a/solution.py
+++ b/solution.py
@@ -14,7 +14,6 @@
 SEGMENT = 4
 MOVING = 3
 R = 256
-ELEMENTS = LINES_HERE * SEGMENT
 HALF = 128
 OWN_MAPS, Y_MAPS = MOVING, MOVING + 1
 WALL = ("y", "core")
@@ -23,15 +22,22 @@
 BF16 = jnp.bfloat16
 EXACT = lax.Precision.HIGHEST
 VMEM = pltpu.VMEM
-SMEM = pltpu.SMEM
 
 
 def in_vmem():
     return pl.BlockSpec(memory_space=VMEM)
 
 
-def in_smem():
-    return pl.BlockSpec(memory_space=SMEM)
+class Digits:
+    def __init__(self, number, bits):
+        self.number, self.bits = number, bits
+
+    def __getitem__(self, at):
+        return (self.number >> (self.bits * at)) & ((1 << self.bits) - 1)
+
+
+def lengths_and_norths(tile):
+    return Digits(jnp.max(tile[0:8]).astype(jnp.int32), 6), Digits(jnp.max(tile[8:16]).astype(jnp.int32), 2)
 
 
 def wall_here():
@@ -53,20 +59,18 @@
     return jnp.where(slot == MOVING, short, slot + (slot >= short).astype(jnp.int32))
 
 
-def list_living(lengths, listed, slots=LINES_HERE, rest_behind=False):
+def list_living(lengths, listed, slots=LINES_HERE):
     short = shortest_line(lengths)
     count = jnp.int32(0)
     for slot in range(slots):
         here = living_here(lengths, line_in_slot(slot, short))
         for position in range(SEGMENT):
-            entry = slot * SEGMENT + position
-            alive = (position < here).astype(jnp.int32)
-            listed[count if not rest_behind else jnp.where(alive == 1, count, ELEMENTS - 1 - (entry - count))] = entry
-            count = count + alive
+            listed[count] = slot * SEGMENT + position
+            count = count + (position < here).astype(jnp.int32)
     return count
 
 
-def for_listed(lengths, listed, count, body, together=4, after=None):
+def for_listed(lengths, listed, count, body, together=4):
     short = shortest_line(lengths)
 
     def one(trip):
@@ -77,9 +81,6 @@
     def group(first, size):
         for part in range(size):
             one(first + part)
-        if after is not None:
-            for part in range(size):
-                after(first + part)
 
     whole = count // together
 
@@ -131,10 +132,10 @@
 
 def edges_kernel(
     lengths_hbm,
-    vector,
+    norths_hbm,
+    vector_hbm,
     lifting_hbm,
     inverse_hbm,
-    diagonal_hbm,
     over_core,
     over_y,
     over_pair,
@@ -144,50 +145,48 @@
     whole,
     lower,
     inverse,
-    diagonal,
+    vector,
+    tile,
     lengths,
-    ends,
-    west,
-    east,
+    norths,
     sems,
-    run_sems,
     block_sems,
 ):
     core, odd = lax.axis_index("core"), lax.axis_index("z") % 2
-    copies = [pltpu.make_async_copy(lengths_hbm, lengths, sems.at[0])]
-    for end, position in enumerate((0, SEGMENT - 1)):
-        copies.append(pltpu.make_async_copy(vector.at[:, position], ends.at[end], sems.at[1 + end]))
-    for at, (line, first_row, face) in enumerate(((0, 0, west), (LINES_HERE - 1, 48, east))):
-        for run in range(5):
-            source = vector.at[line, :, pl.ds(64 * run + first_row, 16)]
-            target = face.at[:, pl.ds(16 * run, 16)]
-            copies.append(pltpu.make_async_copy(source, target, run_sems.at[at, run]))
+    copies = [
+        pltpu.make_async_copy(lengths_hbm, lengths, sems.at[0]),
+        pltpu.make_async_copy(norths_hbm, norths, sems.at[1]),
+    ]
+    for line in range(LINES_HERE):
+        copies.append(pltpu.make_async_copy(vector_hbm.at[line], vector.at[line], block_sems.at[2, line]))
     needed = []
     for line in range(LINES_HERE):
         needed.append(pltpu.make_async_copy(inverse_hbm.at[line], inverse.at[line], block_sems.at[0, line]))
         needed.append(pltpu.make_async_copy(lifting_hbm.at[line, :, 0], lower.at[line], block_sems.at[1, line]))
-    later = [
-        pltpu.make_async_copy(diagonal_hbm.at[line], diagonal.at[line], block_sems.at[2, line])
-        for line in range(LINES_HERE)
-    ]
-    for copy in copies + needed + later:
+    for copy in copies + needed:
         copy.start()
     rows = wall_face_rows()
     for copy in copies:
         copy.wait()
+    length_digits, north_digits = jnp.int32(0), jnp.int32(0)
+    for line in range(LINES_HERE):
+        length_digits = length_digits + (lengths[line] << (6 * line))
+        north_digits = north_digits + (norths[0, line] << (2 * line))
+    tile[0:8] = jnp.full((8, HALF), length_digits.astype(F32))
+    tile[8:16] = jnp.full((8, HALF), north_digits.astype(F32))
     short = shortest_line(lengths)
     zero = jnp.zeros((FACE, R), BF16)
     for slot in range(MOVING):
         line = line_in_slot(slot, short)
         here = living_here(lengths, line)
-        down = jnp.where(here > 0, pick(rows[:FACE], ends[0, line]), zero)
-        up = jnp.where(here > SEGMENT - 1, pick(rows[FACE:], ends[1, line]), zero)
+        down = jnp.where(here > 0, pick(rows[:FACE], vector[line, 0]), zero)
+        up = jnp.where(here > SEGMENT - 1, pick(rows[FACE:], vector[line, SEGMENT - 1]), zero)
         over_core[slot] = jnp.where(core == 0, up, down)
         over_y[slot] = jnp.where(core == 0, down, up)
     first, last = living_here(lengths, 0), living_here(lengths, LINES_HERE - 1)
     for position in range(SEGMENT):
-        from_first = jnp.where(position < first, west[position], zero)
-        from_last = jnp.where(position < last, east[position], zero)
+        from_first = jnp.where(position < first, a_face(vector[0, position], 0), zero)
+        from_last = jnp.where(position < last, a_face(vector[LINES_HERE - 1, position], 3), zero)
         over_pair[position] = jnp.where(odd == 0, from_last, from_first)
         over_next[position] = jnp.where(odd == 0, from_first, from_last)
     for copy in needed:
@@ -210,11 +209,10 @@
             if position < SEGMENT - 1:
                 prefixes[slot, position] = so_far[slot]
     whole[...] = jnp.concatenate(so_far + [jnp.zeros((FACE, R - MOVING * FACE), F32)], axis=1)
-    for copy in later:
-        copy.wait()
-
-
-def diagonal_kernel(lengths, vector, diagonal, lifting_hbm, product, traces, lifting, squares, listed, wide, sems):
+
+
+def diagonal_kernel(tile, vector, diagonal, lifting_hbm, product, traces, lifting, squares, listed, wide, sems):
+    lengths, _ = lengths_and_norths(tile)
     copies = [
         pltpu.make_async_copy(lifting_hbm.at[line, :, pl.ds(1, 5)], lifting.at[line], sems.at[line])
         for line in range(LINES_HERE)
@@ -256,8 +254,7 @@
 
 
 def product_kernel(
-    lengths,
-    norths,
+    tile,
     traces,
     over_core,
     over_y,
@@ -277,6 +274,7 @@
     driven,
 ):
     core, odd = lax.axis_index("core"), lax.axis_index("z") % 2
+    lengths, norths = lengths_and_norths(tile)
     zero = jnp.zeros((FACE, R), BF16)
 
     def multiply(slot, line, position):
@@ -296,10 +294,10 @@
         east = jnp.where(
             line == LINES_HERE - 1, east_edge, traces[jnp.minimum(line + 1, LINES_HERE - 1), position, 2]
         )
-        north_line = norths[0, line]
+        north_line = norths[line]
         south_line = jnp.int32(0)
         for other in range(1, LINES_HERE):
-            south_line = jnp.where(norths[0, other] == line, other, south_line)
+            south_line = jnp.where(norths[other] == line, other, south_line)
         south = traces[south_line, position, 5]
         north = traces[north_line, position, 4]
         neighbours = jnp.concatenate([below, above, west, east, south, north], axis=0)
@@ -385,7 +383,7 @@
 
 
 def eliminate_kernel(
-    lengths,
+    tile,
     vector,
     squares,
     product,
@@ -402,7 +400,7 @@
     sums,
 ):
     core = lax.axis_index("core")
-    short = shortest_line(lengths)
+    lengths, _ = lengths_and_norths(tile)
     entering[...] = jnp.zeros_like(entering)
     values = []
     for slot in range(MOVING):
@@ -441,9 +439,9 @@
     for_listed(lengths, listed, count, leave)
     rest = sums[1].sum(axis=0, keepdims=True)
     pieces = [part[:, at : at + HALF] for part in (cross, square, rest) for at in (0, HALF)]
-    tile = jnp.concatenate(pieces + [jnp.zeros((2, HALF), F32)], axis=0)
+    sums_tile = jnp.concatenate(pieces + [jnp.zeros((2, HALF), F32)], axis=0)
     for copy in range(tiles.shape[0]):
-        tiles[copy] = tile
+        tiles[copy] = sums_tile
 
 
 def merged(tiles):
@@ -463,38 +461,26 @@
         tiles[copy] = tile
 
 
-def finish_kernel(entries, lengths, tiles, vector, eliminated, basis, coefs, listed, held, sems):
+def finish_kernel(entries, tile, tiles, vector, eliminated, basis, coefs, held, sems):
+    lengths, _ = lengths_and_norths(tile)
     _, _, rest, ratio = merged(tiles[...])
     spread = jnp.sqrt(rest / entries + 1e-06)
     ratio = jnp.concatenate([ratio[0:1], ratio[1:2]], axis=1)
     spread = jnp.concatenate([spread[0:1], spread[1:2]], axis=1)
     coefs[...] = jnp.concatenate([ratio, spread], axis=0)
     scale = 1.0 / spread
-    short = shortest_line(lengths)
-    count = list_living(lengths, listed, rest_behind=True)
-
-    def copy_of(trip):
-        line, position = line_in_slot(listed[trip] // SEGMENT, short), listed[trip] % SEGMENT
-        return pltpu.make_async_copy(held.at[line, position], basis.at[line, position], sems.at[trip])
-
-    @pl.loop(count, ELEMENTS)
-    def _(trip):
-        line, position = line_in_slot(listed[trip] // SEGMENT, short), listed[trip] % SEGMENT
-        held[line, position] = jnp.zeros((BLOCK, R), BF16)
-        copy_of(trip).start()
-
-    def body(slot, line, position):
-        masked = vector[line, position].astype(F32)
-        held[line, position] = ((eliminated[line, position] - ratio * masked) * scale).astype(BF16)
-
-    def after(trip):
-        copy_of(trip).start()
-
-    for_listed(lengths, listed, count, body, 4, after)
-
-    @pl.loop(0, ELEMENTS)
-    def _(trip):
-        copy_of(trip).wait()
+    copies = []
+    for line in range(LINES_HERE):
+        here = living_here(lengths, line)
+        for position in range(SEGMENT):
+            masked = vector[line, position].astype(F32)
+            value = (eliminated[line, position] - ratio * masked) * scale
+            held[line, position] = jnp.where(position < here, value, 0.0).astype(BF16)
+        copy = pltpu.make_async_copy(held.at[line], basis.at[line], sems.at[line])
+        copy.start()
+        copies.append(copy)
+    for copy in copies:
+        copy.wait()
 
 
 def call(kernel, outs, ins, scratch=(), limit=12, flops=0, moved=0, out_specs=None, in_hbm=()):
@@ -502,7 +488,7 @@
         kernel,
         out_shape=outs,
         in_specs=[
-            pl.BlockSpec(memory_space=pltpu.HBM) if at in in_hbm else in_smem() if arg.dtype == jnp.int32 else in_vmem()
+            pl.BlockSpec(memory_space=pltpu.HBM) if at in in_hbm else in_vmem()
             for at, arg in enumerate(ins)
         ],
         out_specs=out_specs or jax.tree.map(lambda _: in_vmem(), outs),
@@ -524,7 +510,7 @@
     edge = shaped(MOVING, FACE, R, dtype=BF16)
     side = shaped(SEGMENT, FACE, R, dtype=BF16)
     blocks = shaped(LINES_HERE, SEGMENT, FACE, BLOCK, dtype=BF16)
-    over_core, over_y, over_pair, over_next, steps, prefixes, whole, lower, inverse, diagonal_here = call(
+    over_core, over_y, over_pair, over_next, steps, prefixes, whole, lower, inverse, vector, tile = call(
         edges_kernel,
         (
             edge,
@@ -536,16 +522,14 @@
             shaped(FACE, R),
             blocks,
             blocks,
-            shaped(LINES_HERE, SEGMENT, BLOCK, BLOCK, dtype=BF16),
+            shaped(LINES_HERE, SEGMENT, BLOCK, R, dtype=BF16),
+            shaped(16, HALF),
         ),
-        (lengths, vector, lifting, inverse_rows, diagonal),
+        (lengths, north_of, vector, lifting, inverse_rows),
         (
             pltpu.SMEM((LINES_HERE,), jnp.int32),
-            pltpu.VMEM((2, LINES_HERE, BLOCK, R), BF16),
-            pltpu.VMEM((SEGMENT, FACE, R), BF16),
-            pltpu.VMEM((SEGMENT, FACE, R), BF16),
-            pltpu.SemaphoreType.DMA((3,)),
-            pltpu.SemaphoreType.DMA((2, 5)),
+            pltpu.SMEM((1, LINES_HERE), jnp.int32),
+            pltpu.SemaphoreType.DMA((2,)),
             pltpu.SemaphoreType.DMA((3, LINES_HERE)),
         ),
         in_hbm=(0, 1, 2, 3, 4),
@@ -568,7 +552,7 @@
             shaped(LINES_HERE, SEGMENT, 5, FACE, BLOCK, dtype=BF16),
             shaped(8, R),
         ),
-        (lengths, vector, diagonal_here, lifting),
+        (tile, vector, diagonal, lifting),
         (LISTED, pltpu.VMEM((2, BLOCK, HALF), F32), pltpu.SemaphoreType.DMA((LINES_HERE,))),
         in_hbm=(3,),
     )
@@ -580,8 +564,7 @@
             shaped(MOVING + 2, FACE, R),
         ),
         (
-            lengths,
-            north_of,
+            tile,
             traces,
             over_core,
             over_y,
@@ -610,7 +593,7 @@
     eliminated, tiles = call(
         eliminate_kernel,
         (shaped(LINES_HERE, SEGMENT, BLOCK, R), shaped(surfs, 8, HALF)),
-        (lengths, vector, squares, product, lower, prefixes, carries, arriving, arriving_beside, beside),
+        (tile, vector, squares, product, lower, prefixes, carries, arriving, arriving_beside, beside),
         (LISTED, pltpu.VMEM((LINES_HERE, SEGMENT, FACE, R), F32), pltpu.VMEM((2, 8, R), F32)),
         flops=10**9,
         moved=10**7,
@@ -622,8 +605,8 @@
     return call(
         functools.partial(finish_kernel, entries),
         (shaped(LINES_HERE, SEGMENT, BLOCK, R, dtype=BF16), shaped(2, R)),
-        (lengths, tiles, vector, eliminated),
-        (LISTED, pltpu.VMEM((LINES_HERE, SEGMENT, BLOCK, R), BF16), pltpu.SemaphoreType.DMA((ELEMENTS,))),
+        (tile, tiles, vector, eliminated),
+        (pltpu.VMEM((LINES_HERE, SEGMENT, BLOCK, R), BF16), pltpu.SemaphoreType.DMA((LINES_HERE,))),
         out_specs=(pl.BlockSpec(memory_space=pl.ANY), in_vmem()),
     )
 

time: 74.9 us -> 72.4 us (0.967)
  Pallas kernels: 19.4 us -> 14.6 us
  blocking collectives: 23.8 us -> 25.5 us
  starting transfers between devices: 24.3 us -> 25.3 us
    pallas_call x8, Pallas kernels: 19.4 us -> 14.6 us  [call(): pl.pallas_call(kernel, out_shape=outs, in_specs=[pl.BlockSpec(memory_spac...]
    all_to_all x1, blocking collectives: 12.1 us -> 13.8 us  [per_device(): tiles = lax.all_to_all(tiles, SURF, 0, 0, tiled=True)]
  transfers between devices with their start and end apart: 10 -> 10, of which waited for: 4 -> 4; matrix products, arithmetic and copies ran while one was open for 0% -> 0% of each run, Pallas kernels for 4% -> 3%
where the time goes in v4:
time: 72.4 us; the launch traced here: 71.9 us
  blocking collectives  25.5 us (35%)
  starting transfers between devices  25.3 us (35%)
  Pallas kernels  14.6 us (20%)
  waiting for transfers between devices  5.68 us (8%)
  between operations  0.76 us (1%)
    pallas_call x8, Pallas kernels, call(): pl.pallas_call(kernel, out_shape=outs, in_specs=[pl.BlockSpec(memory_spac...  14.6 us
    all_to_all x1, blocking collectives, per_device(): tiles = lax.all_to_all(tiles, SURF, 0, 0, tiled=True)  13.8 us
    all_to_all x1, blocking collectives, per_device(): tiles = lax.all_to_all(tiles, WALL, 0, 0, tiled=True)  11.7 us
    ppermute x3, starting transfers between devices, up_chips(): return lax.ppermute(value, 'y', [(i, i + far) for i in range(ranks - far)])  7.89 us
    ppermute x1, starting transfers between devices, per_device(): lax.ppermute(over_next, SURF, nexts + [(b, a) for a, b in nexts])  6.87 us
    ppermute x1, starting transfers between devices, per_device(): over_y = lax.ppermute(over_y, WALL, rungs + [(b, a) for a, b in rungs])  3.08 us
    ppermute x1, starting transfers between devices, per_device(): lax.ppermute(over_pair, SURF, [(i, i ^ 1) for i in range(surfs)])  2.55 us
    ppermute x1, starting transfers between devices, per_device(): arriving_beside = lax.ppermute(arriving, 'core', swap)  1.95 us
  transfers between devices with their start and end apart: 10, of which 4 were waited for; matrix products, arithmetic and copies ran while one was open for 0% of the time, Pallas kernels for 3%

profile of v4, /device:TPU:1, one launch (start us, length us, event | category | flops | bytes accessed | tf_op | source)
XLA Modules:
  0.0 71.9 jit_solution(874513274707038773)
XLA Ops:
  0.6 0.0 copy-start
  0.6 3.4 %edges_kernel.1 = (bf16[3,80,256]{2,1,0:T(8,128)(2,1)S(1)}, bf16[3,80,256]{2,1,0:T(8,128)(2,1)S(1)}, bf16[4,80,256]{2,1,0:T(8,128)(2,1)S(1)}, bf16[4,80,256]{2,1...) custom-call(s32[4]{0:T(128)} %lengths_hbm.1, ...), custom_call_target="tpu_custom_call" | custom-call | tf_op jit(solution)/shard_map/edges_kernel/pallas_call | solution.py:487
  4.1 2.5 %collective-permute-start.2 = (bf16[4,80,256]{2,1,0:T(8,128)(2,1)S(1)}, bf16[4,80,256]{2,1,0:T(8,128)(2,1)S(1)}, u32[]{:S(2)}, u32[]{:S(2)}) collective-permute-start(bf16[4,80,256]{2,1,0:T(8,128)(2,1)S(1)} %get-tuple-element.30), channel_id=1, source_target_pairs={{0,1},{1,0},{2,3},{3,2},{4,5},{5,4},{6,7},{7,6},{8,9},{9,8},{10,11... | collective-permute-start | bytes 491528 | tf_op jit(solution)/shard_map/ppermute | solution.py:542
  6.6 6.9 %collective-permute-start.3 = (bf16[4,80,256]{2,1,0:T(8,128)(2,1)S(1)}, bf16[4,80,256]{2,1,0:T(8,128)(2,1)S(1)}, u32[]{:S(2)}, u32[]{:S(2)}) collective-permute-start(bf16[4,80,256]{2,1,0:T(8,128)(2,1)S(1)} %get-tuple-element.31), channel_id=1, source_target_pairs={{1,2},{3,4},{5,6},{7,8},{9,10},{11,12},{13,14},{15,16},{17,18},{19... | collective-permute-start | bytes 491528 | tf_op jit(solution)/shard_map/ppermute | solution.py:544
  13.5 1.2 %collective-permute-start = (bf16[3,80,256]{2,1,0:T(8,128)(2,1)S(1)}, bf16[3,80,256]{2,1,0:T(8,128)(2,1)S(1)}, u32[]{:S(2)}, u32[]{:S(2)}) collective-permute-start(bf16[3,80,256]{2,1,0:T(8,128)(2,1)S(1)} %get-tuple-element.28), channel_id=1, source_target_pairs={{0,32},{32,0},{1,33},{33,1},{2,34},{34,2},{3,35},{35,3},{4,36},{36... | collective-permute-start | bytes 368648 | tf_op jit(solution)/shard_map/ppermute | solution.py:539
  14.7 3.1 %collective-permute-start.1 = (bf16[3,80,256]{2,1,0:T(8,128)(2,1)S(1)}, bf16[3,80,256]{2,1,0:T(8,128)(2,1)S(1)}, u32[]{:S(2)}, u32[]{:S(2)}) collective-permute-start(bf16[3,80,256]{2,1,0:T(8,128)(2,1)S(1)} %get-tuple-element.29), channel_id=1, source_target_pairs={{32,64},{96,128},{160,192},{64,32},{128,96},{192,160},{33,65},{97,... | collective-permute-start | bytes 368648 | tf_op jit(solution)/shard_map/ppermute | solution.py:541
  17.8 1.3 %collective-permute-start.4 = (f32[80,256]{1,0:T(8,128)S(1)}, f32[80,256]{1,0:T(8,128)S(1)}, u32[]{:S(2)}, u32[]{:S(2)}) collective-permute-start(f32[80,256]{1,0:T(8,128)S(1)} %get-tuple-element.36.map_here), channel_id=1, source_target_pairs={{64,0},{128,192},{65,1},{129,193},{66,2},{130,194},{67,3},{131,195... | collective-permute-start | bytes 245768 | tf_op jit(solution)/shard_map/ppermute | solution.py:546
  19.1 0.0 copy-done
  19.1 2.4 %diagonal_kernel.1 = (f32[4,4,320,256]{3,2,1,0:T(8,128)S(1)}, bf16[4,4,6,80,256]{4,3,2,1,0:T(8,128)(2,1)S(1)}, bf16[4,4,5,80,320]{4,3,2,1,0:T(8,128)(2,1)S(1)}, f32[8,256]{1,0:T(8,128)S(1)}) custom-call(f32[16,128]{1,0:T(8,128)S(1)} %get-tuple-element.24.tile, bf16[4,4,320,256]{3,2,1,0:T(8,128)(2,1)S(1)} %get-tuple-element.25.vector, ...), custom_call_target="tpu_custom_call" | custom-call | tf_op jit(solution)/shard_map/diagonal_kernel/pallas_call | solution.py:487
  21.6 1.4 %collective-permute-done.4.map_y = f32[80,256]{1,0:T(8,128)S(1)} collective-permute-done((f32[80,256]{1,0:T(8,128)S(1)}, f32[80,256]{1,0:T(8,128)S(1)}, u32[]{:S(2)}, u32[]{:S(2)}) %collective-permute-start.4) | collective-permute-done | bytes 81952 | tf_op jit(solution)/shard_map/ppermute | solution.py:546
  23.0 0.0 collective-permute-done.over_core
  23.0 0.0 collective-permute-done.1.over_y
  23.0 0.0 collective-permute-done.2.over_pair
  23.0 0.0 collective-permute-done.3.over_next
  23.0 3.1 %product_kernel.1 = (f32[4,4,320,256]{3,2,1,0:T(8,128)S(1)}, f32[3,3,80,256]{3,2,1,0:T(8,128)S(1)}, f32[5,80,256]{2,1,0:T(8,128)S(1)}) custom-call(f32[16,128]{1,0:T(8,128)S(1)} %get-tuple-element.24.tile, bf16[4,4,6,80,256]{4,3,2,1,0:T(8,128)(2,1)S(1)} %get-tuple-element.27.traces, bf16[3,80,256]{2,1,0:T(8,128)(2,1)S(1)} %collective-permute-done.over_core, ...), custom_call_target="tpu_custom_call" | custom-call | tf_op jit(solution)/shard_map/product_kernel/pallas_call | solution.py:487
  26.1 0.4 collective-permute-start.5
  26.5 1.4 %collective-permute-done.5.other.beside = f32[5,80,256]{2,1,0:T(8,128)S(1)} collective-permute-done((f32[5,80,256]{2,1,0:T(8,128)S(1)}, f32[5,80,256]{2,1,0:T(8,128)S(1)}, u32[]{:S(2)}, u32[]{:S(2)}) %collective-permute-start.5) | collective-permute-done | bytes 409632 | tf_op jit(solution)/shard_map/ppermute | solution.py:588
  27.9 0.7 chip_kernel.1
  28.6 2.2 %collective-permute-start.6 = (f32[3,80,128]{2,1,0:T(8,128)S(1)}, f32[3,80,128]{2,1,0:T(8,128)S(1)}, u32[]{:S(2)}, u32[]{:S(2)}) collective-permute-start(f32[3,80,128]{2,1,0:T(8,128)S(1)} %get-tuple-element.42), channel_id=1, source_target_pairs={{0,64},{64,128},{128,192},{1,65},{65,129},{129,193},{2,66},{66,130... | collective-permute-start | bytes 368648 | tf_op jit(solution)/shard_map/ppermute | solution.py:586
  30.8 3.2 %collective-permute-start.8 = (f32[3,80,128]{2,1,0:T(8,128)S(1)}, f32[3,80,128]{2,1,0:T(8,128)S(1)}, u32[]{:S(2)}, u32[]{:S(2)}) collective-permute-start(f32[3,80,128]{2,1,0:T(8,128)S(1)} %get-tuple-element.43), channel_id=1, source_target_pairs={{0,192},{1,193},{2,194},{3,195},{4,196},{5,197},{6,198},{7,199},{8... | collective-permute-start | bytes 368648 | tf_op jit(solution)/shard_map/ppermute | solution.py:586
  34.0 2.5 %collective-permute-start.7 = (f32[3,80,128]{2,1,0:T(8,128)S(1)}, f32[3,80,128]{2,1,0:T(8,128)S(1)}, u32[]{:S(2)}, u32[]{:S(2)}) collective-permute-start(f32[3,80,128]{2,1,0:T(8,128)S(1)} %get-tuple-element.43), channel_id=1, source_target_pairs={{0,128},{64,192},{1,129},{65,193},{2,130},{66,194},{3,131},{67,195... | collective-permute-start | bytes 368648 | tf_op jit(solution)/shard_map/ppermute | solution.py:586
  36.5 0.0 collective-permute-done.6.one
  36.5 0.0 collective-permute-done.8.three
  36.5 1.8 %collective-permute-done.7.two = f32[3,80,128]{2,1,0:T(8,128)S(1)} collective-permute-done((f32[3,80,128]{2,1,0:T(8,128)S(1)}, f32[3,80,128]{2,1,0:T(8,128)S(1)}, u32[]{:S(2)}, u32[]{:S(2)}) %collective-permute-start.7) | collective-permute-done | bytes 122912 | tf_op jit(solution)/shard_map/ppermute | solution.py:586
  38.4 1.9 %collective-permute-start.9 = (f32[3,80,128]{2,1,0:T(8,128)S(1)}, f32[3,80,128]{2,1,0:T(8,128)S(1)}, u32[]{:S(2)}, u32[]{:S(2)}) collective-permute-start(f32[3,80,128]{2,1,0:T(8,128)S(1)} %arriving_kernel.1.mine), channel_id=1, source_target_pairs={{0,32},{32,0},{1,33},{33,1},{2,34},{34,2},{3,35},{35,3},{4,36},{36... | collective-permute-start | bytes 368648 | tf_op jit(solution)/shard_map/ppermute | solution.py:592
  40.3 1.0 %collective-permute-done.9.other = f32[3,80,128]{2,1,0:T(8,128)S(1)} collective-permute-done((f32[3,80,128]{2,1,0:T(8,128)S(1)}, f32[3,80,128]{2,1,0:T(8,128)S(1)}, u32[]{:S(2)}, u32[]{:S(2)}) %collective-permute-start.9) | collective-permute-done | bytes 122912 | tf_op jit(solution)/shard_map/ppermute | solution.py:592
  41.3 2.1 %eliminate_kernel.1 = (f32[4,4,320,256]{3,2,1,0:T(8,128)S(1)}, f32[32,8,128]{2,1,0:T(8,128)S(1)}) custom-call(f32[16,128]{1,0:T(8,128)S(1)} %get-tuple-element.24.tile, bf16[4,4,320,256]{3,2,1,0:T(8,128)(2,1)S(1)} %get-tuple-element.25.vector, f32[8,256]{1,0:T(8,128)S(1)} %get-tuple-element.26.squares, f32[4,4,320,256]{3,2,1,0:T(8,128)S(1)} %get-tuple-element.38.product, ...), custom_call_target="tpu_custom_call" | custom-call | flops 1000000000 | bytes 10000000 | tf_op jit(solution)/shard_map/eliminate_kernel/pallas_call | solution.py:487
  43.4 13.8 %all_to_all.10.tiles_in = f32[32,8,128]{2,1,0:T(8,128)S(1)} all-to-all(f32[32,8,128]{2,1,0:T(8,128)S(1)} %get-tuple-element.44), channel_id=1, replica_groups=mesh['y'=4,'core'=2,'x'=4,'z'=8] {'x','z'}, dimensions={0} | all-to-all | bytes 262144 | tf_op jit(solution)/shard_map/all_to_all | solution.py:601
  57.2 0.1 merge_kernel.1
  57.3 11.7 %all_to_all.11.tiles = f32[8,8,128]{2,1,0:T(8,128)S(1)} all-to-all(f32[8,8,128]{2,1,0:T(8,128)S(1)} %merge_kernel.1), channel_id=1, replica_groups=mesh['y'=4,'core'=2,'x'=4,'z'=8] {'y','core'}, dimensions={0} | all-to-all | bytes 65536 | tf_op jit(solution)/shard_map/all_to_all | solution.py:603
  69.0 2.8 %finish_kernel.1 = (bf16[4,4,320,256]{3,2,1,0:T(8,128)(2,1)}, f32[2,256]{1,0:T(2,128)}) custom-call(f32[16,128]{1,0:T(8,128)S(1)} %get-tuple-element.24.tile, f32[8,8,128]{2,1,0:T(8,128)S(1)} %all_to_all.11.tiles, bf16[4,4,320,256]{3,2,1,0:T(8,128)(2,1)S(1)} %get-tuple-element.25.vector, f32[4,4,320,256]{3,2,1,0:T(8,128)S(1)} %get-tuple-element.45.eliminated), custom_call_target="tpu_custom_call" | custom-call | tf_op jit(solution)/shard_map/finish_kernel/pallas_call | solution.py:487
  (1 shorter events, 0.0 us)
Async XLA Ops:
  0.6 18.5 %copy-start = (bf16[4,4,320,320]{3,2,1,0:T(8,128)(2,1)S(1)}, bf16[4,4,320,320]{3,2,1,0:T(8,128)(2,1)}, u32[]{:S(2)}) copy-start(bf16[4,4,320,320]{3,2,1,0:T(8,128)(2,1)} %diagonal.1) | copy-start | bytes 9830404
  4.1 18.9 %collective-permute-start.2 = (bf16[4,80,256]{2,1,0:T(8,128)(2,1)S(1)}, bf16[4,80,256]{2,1,0:T(8,128)(2,1)S(1)}, u32[]{:S(2)}, u32[]{:S(2)}) collective-permute-start(bf16[4,80,256]{2,1,0:T(8,128)(2,1)S(1)} %get-tuple-element.30), channel_id=1, source_target_pairs={{0,1},{1,0},{2,3},{3,2},{4,5},{5,4},{6,7},{7,6},{8,9},{9,8},{10,11... | collective-permute-start | bytes 491528 | tf_op jit(solution)/shard_map/ppermute | solution.py:542
  6.6 16.4 %collective-permute-start.3 = (bf16[4,80,256]{2,1,0:T(8,128)(2,1)S(1)}, bf16[4,80,256]{2,1,0:T(8,128)(2,1)S(1)}, u32[]{:S(2)}, u32[]{:S(2)}) collective-permute-start(bf16[4,80,256]{2,1,0:T(8,128)(2,1)S(1)} %get-tuple-element.31), channel_id=1, source_target_pairs={{1,2},{3,4},{5,6},{7,8},{9,10},{11,12},{13,14},{15,16},{17,18},{19... | collective-permute-start | bytes 491528 | tf_op jit(solution)/shard_map/ppermute | solution.py:544
  13.5 9.5 %collective-permute-start = (bf16[3,80,256]{2,1,0:T(8,128)(2,1)S(1)}, bf16[3,80,256]{2,1,0:T(8,128)(2,1)S(1)}, u32[]{:S(2)}, u32[]{:S(2)}) collective-permute-start(bf16[3,80,256]{2,1,0:T(8,128)(2,1)S(1)} %get-tuple-element.28), channel_id=1, source_target_pairs={{0,32},{32,0},{1,33},{33,1},{2,34},{34,2},{3,35},{35,3},{4,36},{36... | collective-permute-start | bytes 368648 | tf_op jit(solution)/shard_map/ppermute | solution.py:539
  14.7 8.3 %collective-permute-start.1 = (bf16[3,80,256]{2,1,0:T(8,128)(2,1)S(1)}, bf16[3,80,256]{2,1,0:T(8,128)(2,1)S(1)}, u32[]{:S(2)}, u32[]{:S(2)}) collective-permute-start(bf16[3,80,256]{2,1,0:T(8,128)(2,1)S(1)} %get-tuple-element.29), channel_id=1, source_target_pairs={{32,64},{96,128},{160,192},{64,32},{128,96},{192,160},{33,65},{97,... | collective-permute-start | bytes 368648 | tf_op jit(solution)/shard_map/ppermute | solution.py:541
  17.8 5.2 %collective-permute-start.4 = (f32[80,256]{1,0:T(8,128)S(1)}, f32[80,256]{1,0:T(8,128)S(1)}, u32[]{:S(2)}, u32[]{:S(2)}) collective-permute-start(f32[80,256]{1,0:T(8,128)S(1)} %get-tuple-element.36.map_here), channel_id=1, source_target_pairs={{64,0},{128,192},{65,1},{129,193},{66,2},{130,194},{67,3},{131,195... | collective-permute-start | bytes 245768 | tf_op jit(solution)/shard_map/ppermute | solution.py:546
  26.1 1.8 %collective-permute-start.5 = (f32[5,80,256]{2,1,0:T(8,128)S(1)}, f32[5,80,256]{2,1,0:T(8,128)S(1)}, u32[]{:S(2)}, u32[]{:S(2)}) collective-permute-start(f32[5,80,256]{2,1,0:T(8,128)S(1)} %get-tuple-element.41.mine), channel_id=1, source_target_pairs={{0,32},{32,0},{1,33},{33,1},{2,34},{34,2},{3,35},{35,3},{4,36},{36... | collective-permute-start | bytes 1228808 | tf_op jit(solution)/shard_map/ppermute | solution.py:588
  28.6 7.9 %collective-permute-start.6 = (f32[3,80,128]{2,1,0:T(8,128)S(1)}, f32[3,80,128]{2,1,0:T(8,128)S(1)}, u32[]{:S(2)}, u32[]{:S(2)}) collective-permute-start(f32[3,80,128]{2,1,0:T(8,128)S(1)} %get-tuple-element.42), channel_id=1, source_target_pairs={{0,64},{64,128},{128,192},{1,65},{65,129},{129,193},{2,66},{66,130... | collective-permute-start | bytes 368648 | tf_op jit(solution)/shard_map/ppermute | solution.py:586
  30.8 5.7 %collective-permute-start.8 = (f32[3,80,128]{2,1,0:T(8,128)S(1)}, f32[3,80,128]{2,1,0:T(8,128)S(1)}, u32[]{:S(2)}, u32[]{:S(2)}) collective-permute-start(f32[3,80,128]{2,1,0:T(8,128)S(1)} %get-tuple-element.43), channel_id=1, source_target_pairs={{0,192},{1,193},{2,194},{3,195},{4,196},{5,197},{6,198},{7,199},{8... | collective-permute-start | bytes 368648 | tf_op jit(solution)/shard_map/ppermute | solution.py:586
  34.0 4.3 %collective-permute-start.7 = (f32[3,80,128]{2,1,0:T(8,128)S(1)}, f32[3,80,128]{2,1,0:T(8,128)S(1)}, u32[]{:S(2)}, u32[]{:S(2)}) collective-permute-start(f32[3,80,128]{2,1,0:T(8,128)S(1)} %get-tuple-element.43), channel_id=1, source_target_pairs={{0,128},{64,192},{1,129},{65,193},{2,130},{66,194},{3,131},{67,195... | collective-permute-start | bytes 368648 | tf_op jit(solution)/shard_map/ppermute | solution.py:586
  38.4 2.9 %collective-permute-start.9 = (f32[3,80,128]{2,1,0:T(8,128)S(1)}, f32[3,80,128]{2,1,0:T(8,128)S(1)}, u32[]{:S(2)}, u32[]{:S(2)}) collective-permute-start(f32[3,80,128]{2,1,0:T(8,128)S(1)} %arriving_kernel.1.mine), channel_id=1, source_target_pairs={{0,32},{32,0},{1,33},{33,1},{2,34},{34,2},{3,35},{35,3},{4,36},{36... | collective-permute-start | bytes 368648 | tf_op jit(solution)/shard_map/ppermute | solution.py:592

commit v5 on v4

--- a/solution.py
+++ b/solution.py
@@ -147,6 +147,7 @@
     inverse,
     vector,
     tile,
+    alive,
     lengths,
     norths,
     sems,
@@ -174,6 +175,10 @@
         north_digits = north_digits + (norths[0, line] << (2 * line))
     tile[0:8] = jnp.full((8, HALF), length_digits.astype(F32))
     tile[8:16] = jnp.full((8, HALF), north_digits.astype(F32))
+    for line in range(LINES_HERE):
+        here = living_here(lengths, line)
+        for position in range(SEGMENT):
+            alive[line, position] = jnp.full((8, HALF), (position < here).astype(jnp.int32).astype(F32))
     short = shortest_line(lengths)
     zero = jnp.zeros((FACE, R), BF16)
     for slot in range(MOVING):
@@ -211,14 +216,8 @@
     whole[...] = jnp.concatenate(so_far + [jnp.zeros((FACE, R - MOVING * FACE), F32)], axis=1)
 
 
-def diagonal_kernel(tile, vector, diagonal, lifting_hbm, product, traces, lifting, squares, listed, wide, sems):
+def diagonal_kernel(tile, vector, diagonal, product, traces, squares, listed, wide):
     lengths, _ = lengths_and_norths(tile)
-    copies = [
-        pltpu.make_async_copy(lifting_hbm.at[line, :, pl.ds(1, 5)], lifting.at[line], sems.at[line])
-        for line in range(LINES_HERE)
-    ]
-    for copy in copies:
-        copy.start()
     for line in range(LINES_HERE):
         here = living_here(lengths, line)
         for position in range(SEGMENT):
@@ -249,8 +248,6 @@
         traces[line, position, 5] = north.reshape(FACE, R).astype(BF16)
 
     for_listed(lengths, listed, list_living(lengths, listed), body)
-    for copy in copies:
-        copy.wait()
 
 
 def product_kernel(
@@ -260,7 +257,6 @@
     over_y,
     over_pair,
     over_next,
-    lower,
     lifting,
     inverse,
     steps,
@@ -301,8 +297,7 @@
         south = traces[south_line, position, 5]
         north = traces[north_line, position, 4]
         neighbours = jnp.concatenate([below, above, west, east, south, north], axis=0)
-        upper_blocks = lifting[line, position].reshape(5 * FACE, BLOCK)
-        blocks = jnp.concatenate([lower[line, position], upper_blocks], axis=0)
+        blocks = lifting[line, position].reshape(6 * FACE, BLOCK)
         product[line, position] = product_in[line, position] + transposed_times(blocks, neighbours)
 
     count = list_living(lengths, listed)
@@ -461,8 +456,7 @@
         tiles[copy] = tile
 
 
-def finish_kernel(entries, tile, tiles, vector, eliminated, basis, coefs, held, sems):
-    lengths, _ = lengths_and_norths(tile)
+def finish_kernel(entries, alive, tiles, vector, eliminated, basis, coefs, held, sems):
     _, _, rest, ratio = merged(tiles[...])
     spread = jnp.sqrt(rest / entries + 1e-06)
     ratio = jnp.concatenate([ratio[0:1], ratio[1:2]], axis=1)
@@ -471,11 +465,13 @@
     scale = 1.0 / spread
     copies = []
     for line in range(LINES_HERE):
-        here = living_here(lengths, line)
         for position in range(SEGMENT):
             masked = vector[line, position].astype(F32)
             value = (eliminated[line, position] - ratio * masked) * scale
-            held[line, position] = jnp.where(position < here, value, 0.0).astype(BF16)
+            flags = alive[line, position]
+            flags = jnp.concatenate([flags, flags], axis=1) > 0
+            value = jnp.where(flags[None], value.reshape(BLOCK // 8, 8, R), 0.0)
+            held[line, position] = value.reshape(BLOCK, R).astype(BF16)
         copy = pltpu.make_async_copy(held.at[line], basis.at[line], sems.at[line])
         copy.start()
         copies.append(copy)
@@ -510,7 +506,7 @@
     edge = shaped(MOVING, FACE, R, dtype=BF16)
     side = shaped(SEGMENT, FACE, R, dtype=BF16)
     blocks = shaped(LINES_HERE, SEGMENT, FACE, BLOCK, dtype=BF16)
-    over_core, over_y, over_pair, over_next, steps, prefixes, whole, lower, inverse, vector, tile = call(
+    over_core, over_y, over_pair, over_next, steps, prefixes, whole, lower, inverse, vector, tile, alive = call(
         edges_kernel,
         (
             edge,
@@ -524,6 +520,7 @@
             blocks,
             shaped(LINES_HERE, SEGMENT, BLOCK, R, dtype=BF16),
             shaped(16, HALF),
+            shaped(LINES_HERE, SEGMENT, 8, HALF),
         ),
         (lengths, north_of, vector, lifting, inverse_rows),
         (
@@ -544,17 +541,15 @@
     over_next = lax.ppermute(over_next, SURF, nexts + [(b, a) for a, b in nexts])
 
     map_y = lax.ppermute(whole, "y", [(1, 0), (2, 3)])
-    product, traces, lifting_here, squares = call(
+    product, traces, squares = call(
         diagonal_kernel,
         (
             shaped(LINES_HERE, SEGMENT, BLOCK, R),
             shaped(LINES_HERE, SEGMENT, 6, FACE, R, dtype=BF16),
-            shaped(LINES_HERE, SEGMENT, 5, FACE, BLOCK, dtype=BF16),
             shaped(8, R),
         ),
-        (tile, vector, diagonal, lifting),
-        (LISTED, pltpu.VMEM((2, BLOCK, HALF), F32), pltpu.SemaphoreType.DMA((LINES_HERE,))),
-        in_hbm=(3,),
+        (tile, vector, diagonal),
+        (LISTED, pltpu.VMEM((2, BLOCK, HALF), F32)),
     )
     product, carries, outgoing = call(
         product_kernel,
@@ -570,8 +565,7 @@
             over_y,
             over_pair,
             over_next,
-            lower,
-            lifting_here,
+            lifting,
             inverse,
             steps,
             whole,
@@ -605,7 +599,7 @@
     return call(
         functools.partial(finish_kernel, entries),
         (shaped(LINES_HERE, SEGMENT, BLOCK, R, dtype=BF16), shaped(2, R)),
-        (tile, tiles, vector, eliminated),
+        (alive, tiles, vector, eliminated),
         (pltpu.VMEM((LINES_HERE, SEGMENT, BLOCK, R), BF16), pltpu.SemaphoreType.DMA((LINES_HERE,))),
         out_specs=(pl.BlockSpec(memory_space=pl.ANY), in_vmem()),
     )

time: 72.4 us -> 72.2 us (level)
  Pallas kernels: 14.6 us -> 13.5 us
    all_to_all x1, blocking collectives: 13.8 us -> 15.1 us  [per_device(): tiles = lax.all_to_all(tiles, SURF, 0, 0, tiled=True)]
    pallas_call x8, Pallas kernels: 14.6 us -> 13.5 us  [call(): pl.pallas_call(kernel, out_shape=outs, in_specs=[pl.BlockSpec(memory_spac...]
    ppermute x3, starting transfers between devices: 7.89 us -> 6.97 us  [up_chips(): return lax.ppermute(value, 'y', [(i, i + far) for i in range(ranks - far)])]
    all_to_all x1, blocking collectives: 11.7 us -> 10.9 us  [per_device(): tiles = lax.all_to_all(tiles, WALL, 0, 0, tiled=True)]
    ppermute x1, waiting for transfers between devices: 1.43 us -> 2.18 us  [per_device(): map_y = lax.ppermute(whole, 'y', [(1, 0), (2, 3)])]
  transfers between devices with their start and end apart: 10 -> 10, of which waited for: 4 -> 4; matrix products, arithmetic and copies ran while one was open for 0% -> 0% of each run, Pallas kernels for 3% -> 2%
where the time goes in v5:
time: 72.2 us; the launch traced here: 71.4 us
  blocking collectives  26 us (36%)
  starting transfers between devices  24.8 us (34%)
  Pallas kernels  13.5 us (19%)
  waiting for transfers between devices  6.37 us (9%)
  between operations  0.77 us (1%)
    all_to_all x1, blocking collectives, per_device(): tiles = lax.all_to_all(tiles, SURF, 0, 0, tiled=True)  15.1 us
    pallas_call x8, Pallas kernels, call(): pl.pallas_call(kernel, out_shape=outs, in_specs=[pl.BlockSpec(memory_spac...  13.5 us
    all_to_all x1, blocking collectives, per_device(): tiles = lax.all_to_all(tiles, WALL, 0, 0, tiled=True)  10.9 us
    ppermute x3, starting transfers between devices, up_chips(): return lax.ppermute(value, 'y', [(i, i + far) for i in range(ranks - far)])  6.97 us
    ppermute x1, starting transfers between devices, per_device(): lax.ppermute(over_next, SURF, nexts + [(b, a) for a, b in nexts])  6.87 us
    ppermute x1, starting transfers between devices, per_device(): over_y = lax.ppermute(over_y, WALL, rungs + [(b, a) for a, b in rungs])  3.08 us
    ppermute x1, starting transfers between devices, per_device(): lax.ppermute(over_pair, SURF, [(i, i ^ 1) for i in range(surfs)])  2.54 us
    ppermute x1, waiting for transfers between devices, per_device(): map_y = lax.ppermute(whole, 'y', [(1, 0), (2, 3)])  2.18 us
  transfers between devices with their start and end apart: 10, of which 4 were waited for; matrix products, arithmetic and copies ran while one was open for 0% of the time, Pallas kernels for 2%

profile of v5, /device:TPU:1, one launch (start us, length us, event | category | flops | bytes accessed | tf_op | source)
XLA Modules:
  0.0 71.4 jit_solution(8333558976620576961)
XLA Ops:
  0.6 0.0 copy-start.1
  0.6 3.4 %edges_kernel.1 = (bf16[3,80,256]{2,1,0:T(8,128)(2,1)S(1)}, bf16[3,80,256]{2,1,0:T(8,128)(2,1)S(1)}, bf16[4,80,256]{2,1,0:T(8,128)(2,1)S(1)}, bf16[4,80,256]{2,1...) custom-call(s32[4]{0:T(128)} %lengths_hbm.1, ...), custom_call_target="tpu_custom_call" | custom-call | tf_op jit(solution)/shard_map/edges_kernel/pallas_call | solution.py:483
  4.1 0.0 copy-start
  4.1 2.5 %collective-permute-start.2 = (bf16[4,80,256]{2,1,0:T(8,128)(2,1)S(1)}, bf16[4,80,256]{2,1,0:T(8,128)(2,1)S(1)}, u32[]{:S(2)}, u32[]{:S(2)}) collective-permute-start(bf16[4,80,256]{2,1,0:T(8,128)(2,1)S(1)} %get-tuple-element.31), channel_id=1, source_target_pairs={{0,1},{1,0},{2,3},{3,2},{4,5},{5,4},{6,7},{7,6},{8,9},{9,8},{10,11... | collective-permute-start | bytes 491528 | tf_op jit(solution)/shard_map/ppermute | solution.py:539
  6.6 6.9 %collective-permute-start.3 = (bf16[4,80,256]{2,1,0:T(8,128)(2,1)S(1)}, bf16[4,80,256]{2,1,0:T(8,128)(2,1)S(1)}, u32[]{:S(2)}, u32[]{:S(2)}) collective-permute-start(bf16[4,80,256]{2,1,0:T(8,128)(2,1)S(1)} %get-tuple-element.32), channel_id=1, source_target_pairs={{1,2},{3,4},{5,6},{7,8},{9,10},{11,12},{13,14},{15,16},{17,18},{19... | collective-permute-start | bytes 491528 | tf_op jit(solution)/shard_map/ppermute | solution.py:541
  13.5 1.2 %collective-permute-start = (bf16[3,80,256]{2,1,0:T(8,128)(2,1)S(1)}, bf16[3,80,256]{2,1,0:T(8,128)(2,1)S(1)}, u32[]{:S(2)}, u32[]{:S(2)}) collective-permute-start(bf16[3,80,256]{2,1,0:T(8,128)(2,1)S(1)} %get-tuple-element.29), channel_id=1, source_target_pairs={{0,32},{32,0},{1,33},{33,1},{2,34},{34,2},{3,35},{35,3},{4,36},{36... | collective-permute-start | bytes 368648 | tf_op jit(solution)/shard_map/ppermute | solution.py:536
  14.7 3.1 %collective-permute-start.1 = (bf16[3,80,256]{2,1,0:T(8,128)(2,1)S(1)}, bf16[3,80,256]{2,1,0:T(8,128)(2,1)S(1)}, u32[]{:S(2)}, u32[]{:S(2)}) collective-permute-start(bf16[3,80,256]{2,1,0:T(8,128)(2,1)S(1)} %get-tuple-element.30), channel_id=1, source_target_pairs={{32,64},{96,128},{160,192},{64,32},{128,96},{192,160},{33,65},{97,... | collective-permute-start | bytes 368648 | tf_op jit(solution)/shard_map/ppermute | solution.py:538
  17.8 1.3 %collective-permute-start.4 = (f32[80,256]{1,0:T(8,128)S(1)}, f32[80,256]{1,0:T(8,128)S(1)}, u32[]{:S(2)}, u32[]{:S(2)}) collective-permute-start(f32[80,256]{1,0:T(8,128)S(1)} %get-tuple-element.35.map_here), channel_id=1, source_target_pairs={{64,0},{128,192},{65,1},{129,193},{66,2},{130,194},{67,3},{131,195... | collective-permute-start | bytes 245768 | tf_op jit(solution)/shard_map/ppermute | solution.py:543
  19.1 0.0 copy-done.1
  19.1 1.7 %diagonal_kernel.1 = (f32[4,4,320,256]{3,2,1,0:T(8,128)S(1)}, bf16[4,4,6,80,256]{4,3,2,1,0:T(8,128)(2,1)S(1)}, f32[8,256]{1,0:T(8,128)S(1)}) custom-call(f32[16,128]{1,0:T(8,128)S(1)} %get-tuple-element.25.tile, bf16[4,4,320,256]{3,2,1,0:T(8,128)(2,1)S(1)} %get-tuple-element.26.vector, bf16[4,4,320,320]{3,2,1,0:T(8,128)(2,1)S(1)} %copy-done.1), custom_call_target="tpu_custom_call" | custom-call | tf_op jit(solution)/shard_map/diagonal_kernel/pallas_call | solution.py:483
  20.8 2.2 %collective-permute-done.4.map_y = f32[80,256]{1,0:T(8,128)S(1)} collective-permute-done((f32[80,256]{1,0:T(8,128)S(1)}, f32[80,256]{1,0:T(8,128)S(1)}, u32[]{:S(2)}, u32[]{:S(2)}) %collective-permute-start.4) | collective-permute-done | bytes 81952 | tf_op jit(solution)/shard_map/ppermute | solution.py:543
  23.0 0.0 collective-permute-done.over_core
  23.0 0.0 collective-permute-done.1.over_y
  23.0 0.0 collective-permute-done.2.over_pair
  23.0 0.0 collective-permute-done.3.over_next
  23.0 0.0 copy-done
  23.0 3.1 %product_kernel.1 = (f32[4,4,320,256]{3,2,1,0:T(8,128)S(1)}, f32[3,3,80,256]{3,2,1,0:T(8,128)S(1)}, f32[5,80,256]{2,1,0:T(8,128)S(1)}) custom-call(f32[16,128]{1,0:T(8,128)S(1)} %get-tuple-element.25.tile, bf16[4,4,6,80,256]{4,3,2,1,0:T(8,128)(2,1)S(1)} %get-tuple-element.28.traces, bf16[3,80,256]{2,1,0:T(8,128)(2,1)S(1)} %collective-permute-done.over_core, ...), custom_call_target="tpu_custom_call" | custom-call | tf_op jit(solution)/shard_map/product_kernel/pallas_call | solution.py:483
  26.1 0.9 %collective-permute-start.5 = (f32[5,80,256]{2,1,0:T(8,128)S(1)}, f32[5,80,256]{2,1,0:T(8,128)S(1)}, u32[]{:S(2)}, u32[]{:S(2)}) collective-permute-start(f32[5,80,256]{2,1,0:T(8,128)S(1)} %get-tuple-element.41.mine), channel_id=1, source_target_pairs={{0,32},{32,0},{1,33},{33,1},{2,34},{34,2},{3,35},{35,3},{4,36},{36... | collective-permute-start | bytes 1228808 | tf_op jit(solution)/shard_map/ppermute | solution.py:582
  27.0 1.4 %collective-permute-done.5.other.beside = f32[5,80,256]{2,1,0:T(8,128)S(1)} collective-permute-done((f32[5,80,256]{2,1,0:T(8,128)S(1)}, f32[5,80,256]{2,1,0:T(8,128)S(1)}, u32[]{:S(2)}, u32[]{:S(2)}) %collective-permute-start.5) | collective-permute-done | bytes 409632 | tf_op jit(solution)/shard_map/ppermute | solution.py:582
  28.3 0.7 chip_kernel.1
  29.0 1.3 %collective-permute-start.6 = (f32[3,80,128]{2,1,0:T(8,128)S(1)}, f32[3,80,128]{2,1,0:T(8,128)S(1)}, u32[]{:S(2)}, u32[]{:S(2)}) collective-permute-start(f32[3,80,128]{2,1,0:T(8,128)S(1)} %get-tuple-element.42), channel_id=1, source_target_pairs={{0,64},{64,128},{128,192},{1,65},{65,129},{129,193},{2,66},{66,130... | collective-permute-start | bytes 368648 | tf_op jit(solution)/shard_map/ppermute | solution.py:580
  30.3 3.2 %collective-permute-start.8 = (f32[3,80,128]{2,1,0:T(8,128)S(1)}, f32[3,80,128]{2,1,0:T(8,128)S(1)}, u32[]{:S(2)}, u32[]{:S(2)}) collective-permute-start(f32[3,80,128]{2,1,0:T(8,128)S(1)} %get-tuple-element.43), channel_id=1, source_target_pairs={{0,192},{1,193},{2,194},{3,195},{4,196},{5,197},{6,198},{7,199},{8... | collective-permute-start | bytes 368648 | tf_op jit(solution)/shard_map/ppermute | solution.py:580
  33.5 2.5 %collective-permute-start.7 = (f32[3,80,128]{2,1,0:T(8,128)S(1)}, f32[3,80,128]{2,1,0:T(8,128)S(1)}, u32[]{:S(2)}, u32[]{:S(2)}) collective-permute-start(f32[3,80,128]{2,1,0:T(8,128)S(1)} %get-tuple-element.43), channel_id=1, source_target_pairs={{0,128},{64,192},{1,129},{65,193},{2,130},{66,194},{3,131},{67,195... | collective-permute-start | bytes 368648 | tf_op jit(solution)/shard_map/ppermute | solution.py:580
  36.0 0.0 collective-permute-done.6.one
  36.0 0.0 collective-permute-done.8.three
  36.0 1.8 %collective-permute-done.7.two = f32[3,80,128]{2,1,0:T(8,128)S(1)} collective-permute-done((f32[3,80,128]{2,1,0:T(8,128)S(1)}, f32[3,80,128]{2,1,0:T(8,128)S(1)}, u32[]{:S(2)}, u32[]{:S(2)}) %collective-permute-start.7) | collective-permute-done | bytes 122912 | tf_op jit(solution)/shard_map/ppermute | solution.py:580
  37.9 1.9 %collective-permute-start.9 = (f32[3,80,128]{2,1,0:T(8,128)S(1)}, f32[3,80,128]{2,1,0:T(8,128)S(1)}, u32[]{:S(2)}, u32[]{:S(2)}) collective-permute-start(f32[3,80,128]{2,1,0:T(8,128)S(1)} %arriving_kernel.1.mine), channel_id=1, source_target_pairs={{0,32},{32,0},{1,33},{33,1},{2,34},{34,2},{3,35},{35,3},{4,36},{36... | collective-permute-start | bytes 368648 | tf_op jit(solution)/shard_map/ppermute | solution.py:586
  39.8 1.0 %collective-permute-done.9.other = f32[3,80,128]{2,1,0:T(8,128)S(1)} collective-permute-done((f32[3,80,128]{2,1,0:T(8,128)S(1)}, f32[3,80,128]{2,1,0:T(8,128)S(1)}, u32[]{:S(2)}, u32[]{:S(2)}) %collective-permute-start.9) | collective-permute-done | bytes 122912 | tf_op jit(solution)/shard_map/ppermute | solution.py:586
  40.8 2.1 %eliminate_kernel.1 = (f32[4,4,320,256]{3,2,1,0:T(8,128)S(1)}, f32[32,8,128]{2,1,0:T(8,128)S(1)}) custom-call(f32[16,128]{1,0:T(8,128)S(1)} %get-tuple-element.25.tile, bf16[4,4,320,256]{3,2,1,0:T(8,128)(2,1)S(1)} %get-tuple-element.26.vector, f32[8,256]{1,0:T(8,128)S(1)} %get-tuple-element.27.squares, f32[4,4,320,256]{3,2,1,0:T(8,128)S(1)} %get-tuple-element.37.product, ...), custom_call_target="tpu_custom_call" | custom-call | flops 1000000000 | bytes 10000000 | tf_op jit(solution)/shard_map/eliminate_kernel/pallas_call | solution.py:483
  42.9 15.1 %all_to_all.10.tiles_in = f32[32,8,128]{2,1,0:T(8,128)S(1)} all-to-all(f32[32,8,128]{2,1,0:T(8,128)S(1)} %get-tuple-element.44), channel_id=1, replica_groups=mesh['y'=4,'core'=2,'x'=4,'z'=8] {'x','z'}, dimensions={0} | all-to-all | bytes 262144 | tf_op jit(solution)/shard_map/all_to_all | solution.py:595
  58.0 0.1 merge_kernel.1
  58.1 10.9 %all_to_all.11.tiles = f32[8,8,128]{2,1,0:T(8,128)S(1)} all-to-all(f32[8,8,128]{2,1,0:T(8,128)S(1)} %merge_kernel.1), channel_id=1, replica_groups=mesh['y'=4,'core'=2,'x'=4,'z'=8] {'y','core'}, dimensions={0} | all-to-all | bytes 65536 | tf_op jit(solution)/shard_map/all_to_all | solution.py:597
  69.0 2.4 %finish_kernel.1 = (bf16[4,4,320,256]{3,2,1,0:T(8,128)(2,1)}, f32[2,256]{1,0:T(2,128)}) custom-call(f32[4,4,8,128]{3,2,1,0:T(8,128)S(1)} %get-tuple-element.24.alive, f32[8,8,128]{2,1,0:T(8,128)S(1)} %all_to_all.11.tiles, bf16[4,4,320,256]{3,2,1,0:T(8,128)(2,1)S(1)} %get-tuple-element.26.vector, f32[4,4,320,256]{3,2,1,0:T(8,128)S(1)} %get-tuple-element.45.eliminated), custom_call_target="tpu_custom_call" | custom-call | tf_op jit(solution)/shard_map/finish_kernel/pallas_call | solution.py:483
  (1 shorter events, 0.0 us)
Async XLA Ops:
  0.6 18.5 %copy-start.1 = (bf16[4,4,320,320]{3,2,1,0:T(8,128)(2,1)S(1)}, bf16[4,4,320,320]{3,2,1,0:T(8,128)(2,1)}, u32[]{:S(2)}) copy-start(bf16[4,4,320,320]{3,2,1,0:T(8,128)(2,1)} %diagonal.1) | copy-start | bytes 9830404
  4.1 19.0 %copy-start = (bf16[4,4,6,80,320]{4,3,2,1,0:T(8,128)(2,1)S(1)}, bf16[4,4,6,80,320]{4,3,2,1,0:T(8,128)(2,1)}, u32[]{:S(2)}) copy-start(bf16[4,4,6,80,320]{4,3,2,1,0:T(8,128)(2,1)} %lifting.1) | copy-start | bytes 14745604
  4.1 18.9 %collective-permute-start.2 = (bf16[4,80,256]{2,1,0:T(8,128)(2,1)S(1)}, bf16[4,80,256]{2,1,0:T(8,128)(2,1)S(1)}, u32[]{:S(2)}, u32[]{:S(2)}) collective-permute-start(bf16[4,80,256]{2,1,0:T(8,128)(2,1)S(1)} %get-tuple-element.31), channel_id=1, source_target_pairs={{0,1},{1,0},{2,3},{3,2},{4,5},{5,4},{6,7},{7,6},{8,9},{9,8},{10,11... | collective-permute-start | bytes 491528 | tf_op jit(solution)/shard_map/ppermute | solution.py:539
  6.6 16.4 %collective-permute-start.3 = (bf16[4,80,256]{2,1,0:T(8,128)(2,1)S(1)}, bf16[4,80,256]{2,1,0:T(8,128)(2,1)S(1)}, u32[]{:S(2)}, u32[]{:S(2)}) collective-permute-start(bf16[4,80,256]{2,1,0:T(8,128)(2,1)S(1)} %get-tuple-element.32), channel_id=1, source_target_pairs={{1,2},{3,4},{5,6},{7,8},{9,10},{11,12},{13,14},{15,16},{17,18},{19... | collective-permute-start | bytes 491528 | tf_op jit(solution)/shard_map/ppermute | solution.py:541
  13.5 9.5 %collective-permute-start = (bf16[3,80,256]{2,1,0:T(8,128)(2,1)S(1)}, bf16[3,80,256]{2,1,0:T(8,128)(2,1)S(1)}, u32[]{:S(2)}, u32[]{:S(2)}) collective-permute-start(bf16[3,80,256]{2,1,0:T(8,128)(2,1)S(1)} %get-tuple-element.29), channel_id=1, source_target_pairs={{0,32},{32,0},{1,33},{33,1},{2,34},{34,2},{3,35},{35,3},{4,36},{36... | collective-permute-start | bytes 368648 | tf_op jit(solution)/shard_map/ppermute | solution.py:536
  14.7 8.3 %collective-permute-start.1 = (bf16[3,80,256]{2,1,0:T(8,128)(2,1)S(1)}, bf16[3,80,256]{2,1,0:T(8,128)(2,1)S(1)}, u32[]{:S(2)}, u32[]{:S(2)}) collective-permute-start(bf16[3,80,256]{2,1,0:T(8,128)(2,1)S(1)} %get-tuple-element.30), channel_id=1, source_target_pairs={{32,64},{96,128},{160,192},{64,32},{128,96},{192,160},{33,65},{97,... | collective-permute-start | bytes 368648 | tf_op jit(solution)/shard_map/ppermute | solution.py:538
  17.8 5.2 %collective-permute-start.4 = (f32[80,256]{1,0:T(8,128)S(1)}, f32[80,256]{1,0:T(8,128)S(1)}, u32[]{:S(2)}, u32[]{:S(2)}) collective-permute-start(f32[80,256]{1,0:T(8,128)S(1)} %get-tuple-element.35.map_here), channel_id=1, source_target_pairs={{64,0},{128,192},{65,1},{129,193},{66,2},{130,194},{67,3},{131,195... | collective-permute-start | bytes 245768 | tf_op jit(solution)/shard_map/ppermute | solution.py:543
  26.1 2.2 %collective-permute-start.5 = (f32[5,80,256]{2,1,0:T(8,128)S(1)}, f32[5,80,256]{2,1,0:T(8,128)S(1)}, u32[]{:S(2)}, u32[]{:S(2)}) collective-permute-start(f32[5,80,256]{2,1,0:T(8,128)S(1)} %get-tuple-element.41.mine), channel_id=1, source_target_pairs={{0,32},{32,0},{1,33},{33,1},{2,34},{34,2},{3,35},{35,3},{4,36},{36... | collective-permute-start | bytes 1228808 | tf_op jit(solution)/shard_map/ppermute | solution.py:582
  29.0 7.0 %collective-permute-start.6 = (f32[3,80,128]{2,1,0:T(8,128)S(1)}, f32[3,80,128]{2,1,0:T(8,128)S(1)}, u32[]{:S(2)}, u32[]{:S(2)}) collective-permute-start(f32[3,80,128]{2,1,0:T(8,128)S(1)} %get-tuple-element.42), channel_id=1, source_target_pairs={{0,64},{64,128},{128,192},{1,65},{65,129},{129,193},{2,66},{66,130... | collective-permute-start | bytes 368648 | tf_op jit(solution)/shard_map/ppermute | solution.py:580
  30.3 5.7 %collective-permute-start.8 = (f32[3,80,128]{2,1,0:T(8,128)S(1)}, f32[3,80,128]{2,1,0:T(8,128)S(1)}, u32[]{:S(2)}, u32[]{:S(2)}) collective-permute-start(f32[3,80,128]{2,1,0:T(8,128)S(1)} %get-tuple-element.43), channel_id=1, source_target_pairs={{0,192},{1,193},{2,194},{3,195},{4,196},{5,197},{6,198},{7,199},{8... | collective-permute-start | bytes 368648 | tf_op jit(solution)/shard_map/ppermute | solution.py:580
  33.5 4.3 %collective-permute-start.7 = (f32[3,80,128]{2,1,0:T(8,128)S(1)}, f32[3,80,128]{2,1,0:T(8,128)S(1)}, u32[]{:S(2)}, u32[]{:S(2)}) collective-permute-start(f32[3,80,128]{2,1,0:T(8,128)S(1)} %get-tuple-element.43), channel_id=1, source_target_pairs={{0,128},{64,192},{1,129},{65,193},{2,130},{66,194},{3,131},{67,195... | collective-permute-start | bytes 368648 | tf_op jit(solution)/shard_map/ppermute | solution.py:580
  37.9 2.9 %collective-permute-start.9 = (f32[3,80,128]{2,1,0:T(8,128)S(1)}, f32[3,80,128]{2,1,0:T(8,128)S(1)}, u32[]{:S(2)}, u32[]{:S(2)}) collective-permute-start(f32[3,80,128]{2,1,0:T(8,128)S(1)} %arriving_kernel.1.mine), channel_id=1, source_target_pairs={{0,32},{32,0},{1,33},{33,1},{2,34},{34,2},{3,35},{35,3},{4,36},{36... | collective-permute-start | bytes 368648 | tf_op jit(solution)/shard_map/ppermute | solution.py:586

commit v6 on v5

--- a/solution.py
+++ b/solution.py
@@ -158,13 +158,18 @@
         pltpu.make_async_copy(lengths_hbm, lengths, sems.at[0]),
         pltpu.make_async_copy(norths_hbm, norths, sems.at[1]),
     ]
-    for line in range(LINES_HERE):
-        copies.append(pltpu.make_async_copy(vector_hbm.at[line], vector.at[line], block_sems.at[2, line]))
+    for at, position in enumerate((0, SEGMENT - 1)):
+        copies.append(
+            pltpu.make_async_copy(vector_hbm.at[:, position], vector.at[:, position], block_sems.at[2, at])
+        )
+    inner = pltpu.make_async_copy(
+        vector_hbm.at[:, pl.ds(1, SEGMENT - 2)], vector.at[:, pl.ds(1, SEGMENT - 2)], block_sems.at[2, 2]
+    )
     needed = []
     for line in range(LINES_HERE):
         needed.append(pltpu.make_async_copy(inverse_hbm.at[line], inverse.at[line], block_sems.at[0, line]))
         needed.append(pltpu.make_async_copy(lifting_hbm.at[line, :, 0], lower.at[line], block_sems.at[1, line]))
-    for copy in copies + needed:
+    for copy in copies + [inner] + needed:
         copy.start()
     rows = wall_face_rows()
     for copy in copies:
@@ -189,6 +194,7 @@
         over_core[slot] = jnp.where(core == 0, up, down)
         over_y[slot] = jnp.where(core == 0, down, up)
     first, last = living_here(lengths, 0), living_here(lengths, LINES_HERE - 1)
+    inner.wait()
     for position in range(SEGMENT):
         from_first = jnp.where(position < first, a_face(vector[0, position], 0), zero)
         from_last = jnp.where(position < last, a_face(vector[LINES_HERE - 1, position], 3), zero)
@@ -216,7 +222,12 @@
     whole[...] = jnp.concatenate(so_far + [jnp.zeros((FACE, R - MOVING * FACE), F32)], axis=1)
 
 
-def diagonal_kernel(tile, vector, diagonal, product, traces, squares, listed, wide):
+def diagonal_kernel(tile, vector, diagonal_hbm, product, traces, squares, diagonal, sems, wide):
+    def block_copy(line):
+        return pltpu.make_async_copy(diagonal_hbm.at[line], diagonal.at[line], sems.at[line])
+
+    for line in range(LINES_HERE):
+        block_copy(line).start()
     lengths, _ = lengths_and_norths(tile)
     for line in range(LINES_HERE):
         here = living_here(lengths, line)
@@ -228,7 +239,7 @@
 
     squares[...] = jnp.zeros_like(squares)
 
-    def body(slot, line, position):
+    def body(line, position):
         values = vector[line, position]
         product[line, position] = jnp.dot(diagonal[line, position], values, preferred_element_type=F32)
         whole = values.astype(F32)
@@ -247,7 +258,21 @@
         traces[line, position, 4] = south.reshape(FACE, R).astype(BF16)
         traces[line, position, 5] = north.reshape(FACE, R).astype(BF16)
 
-    for_listed(lengths, listed, list_living(lengths, listed), body)
+    @pl.loop(0, LINES_HERE)
+    def _(line):
+        here = living_here(lengths, line)
+        block_copy(line).wait()
+
+        @pl.when(here == SEGMENT)
+        def _():
+            for position in range(SEGMENT):
+                body(line, position)
+
+        @pl.when(here < SEGMENT)
+        def _():
+            @pl.loop(0, here)
+            def _(position):
+                body(line, position)
 
 
 def product_kernel(
@@ -549,7 +574,12 @@
             shaped(8, R),
         ),
         (tile, vector, diagonal),
-        (LISTED, pltpu.VMEM((2, BLOCK, HALF), F32)),
+        (
+            pltpu.VMEM((LINES_HERE, SEGMENT, BLOCK, BLOCK), BF16),
+            pltpu.SemaphoreType.DMA((LINES_HERE,)),
+            pltpu.VMEM((2, BLOCK, HALF), F32),
+        ),
+        in_hbm=(2,),
     )
     product, carries, outgoing = call(
         product_kernel,

time: 72.2 us -> 72.1 us (level)
  Pallas kernels: 13.5 us -> 16.5 us
  starting transfers between devices: 24.8 us -> 23.3 us
  waiting for transfers between devices: 6.37 us -> 5.36 us
    pallas_call x8, Pallas kernels: 13.5 us -> 16.5 us  [call(): pl.pallas_call(kernel, out_shape=outs, in_specs=[pl.BlockSpec(memory_spac...]
    ppermute x1, waiting for transfers between devices: 2.18 us -> 0.81 us  [per_device(): map_y = lax.ppermute(whole, 'y', [(1, 0), (2, 3)])]
    all_to_all x1, blocking collectives: 10.9 us -> 11.9 us  [per_device(): tiles = lax.all_to_all(tiles, WALL, 0, 0, tiled=True)]
    all_to_all x1, blocking collectives: 15.1 us -> 14.2 us  [per_device(): tiles = lax.all_to_all(tiles, SURF, 0, 0, tiled=True)]
    ppermute x1, starting transfers between devices: 0.85 us -> 0.09 us  [per_device(): beside = lax.ppermute(outgoing, 'core', swap)]
  transfers between devices with their start and end apart: 10 -> 10, of which waited for: 4 -> 4; matrix products, arithmetic and copies ran while one was open for 0% -> 0% of each run, Pallas kernels for 2% -> 4%
where the time goes in v6:
time: 72.1 us; the launch traced here: 72 us
  blocking collectives  26.1 us (36%)
  starting transfers between devices  23.3 us (32%)
  Pallas kernels  16.5 us (23%)
  waiting for transfers between devices  5.36 us (7%)
  between operations  0.76 us (1%)
    pallas_call x8, Pallas kernels, call(): pl.pallas_call(kernel, out_shape=outs, in_specs=[pl.BlockSpec(memory_spac...  16.5 us
    all_to_all x1, blocking collectives, per_device(): tiles = lax.all_to_all(tiles, SURF, 0, 0, tiled=True)  14.2 us
    all_to_all x1, blocking collectives, per_device(): tiles = lax.all_to_all(tiles, WALL, 0, 0, tiled=True)  11.9 us
    ppermute x1, starting transfers between devices, per_device(): lax.ppermute(over_next, SURF, nexts + [(b, a) for a, b in nexts])  6.87 us
    ppermute x3, starting transfers between devices, up_chips(): return lax.ppermute(value, 'y', [(i, i + far) for i in range(ranks - far)])  6.25 us
    ppermute x1, starting transfers between devices, per_device(): over_y = lax.ppermute(over_y, WALL, rungs + [(b, a) for a, b in rungs])  3.08 us
    ppermute x1, starting transfers between devices, per_device(): lax.ppermute(over_pair, SURF, [(i, i ^ 1) for i in range(surfs)])  2.55 us
    ppermute x1, starting transfers between devices, per_device(): arriving_beside = lax.ppermute(arriving, 'core', swap)  1.95 us
  transfers between devices with their start and end apart: 10, of which 4 were waited for; matrix products, arithmetic and copies ran while one was open for 0% of the time, Pallas kernels for 4%

profile of v6, /device:TPU:1, one launch (start us, length us, event | category | flops | bytes accessed | tf_op | source)
XLA Modules:
  0.0 72.0 jit_solution(18157701178817128327)
XLA Ops:
  0.6 3.3 %edges_kernel.1 = (bf16[3,80,256]{2,1,0:T(8,128)(2,1)S(1)}, bf16[3,80,256]{2,1,0:T(8,128)(2,1)S(1)}, bf16[4,80,256]{2,1,0:T(8,128)(2,1)S(1)}, bf16[4,80,256]{2,1...) custom-call(s32[4]{0:T(128)} %lengths_hbm.1, ...), custom_call_target="tpu_custom_call" | custom-call | tf_op jit(solution)/shard_map/edges_kernel/pallas_call | solution.py:508
  3.9 0.0 copy-start
  3.9 2.5 %collective-permute-start.2 = (bf16[4,80,256]{2,1,0:T(8,128)(2,1)S(1)}, bf16[4,80,256]{2,1,0:T(8,128)(2,1)S(1)}, u32[]{:S(2)}, u32[]{:S(2)}) collective-permute-start(bf16[4,80,256]{2,1,0:T(8,128)(2,1)S(1)} %get-tuple-element.31), channel_id=1, source_target_pairs={{0,1},{1,0},{2,3},{3,2},{4,5},{5,4},{6,7},{7,6},{8,9},{9,8},{10,11... | collective-permute-start | bytes 491528 | tf_op jit(solution)/shard_map/ppermute | solution.py:564
  6.5 6.9 %collective-permute-start.3 = (bf16[4,80,256]{2,1,0:T(8,128)(2,1)S(1)}, bf16[4,80,256]{2,1,0:T(8,128)(2,1)S(1)}, u32[]{:S(2)}, u32[]{:S(2)}) collective-permute-start(bf16[4,80,256]{2,1,0:T(8,128)(2,1)S(1)} %get-tuple-element.32), channel_id=1, source_target_pairs={{1,2},{3,4},{5,6},{7,8},{9,10},{11,12},{13,14},{15,16},{17,18},{19... | collective-permute-start | bytes 491528 | tf_op jit(solution)/shard_map/ppermute | solution.py:566
  13.3 1.2 %collective-permute-start = (bf16[3,80,256]{2,1,0:T(8,128)(2,1)S(1)}, bf16[3,80,256]{2,1,0:T(8,128)(2,1)S(1)}, u32[]{:S(2)}, u32[]{:S(2)}) collective-permute-start(bf16[3,80,256]{2,1,0:T(8,128)(2,1)S(1)} %get-tuple-element.29), channel_id=1, source_target_pairs={{0,32},{32,0},{1,33},{33,1},{2,34},{34,2},{3,35},{35,3},{4,36},{36... | collective-permute-start | bytes 368648 | tf_op jit(solution)/shard_map/ppermute | solution.py:561
  14.6 3.1 %collective-permute-start.1 = (bf16[3,80,256]{2,1,0:T(8,128)(2,1)S(1)}, bf16[3,80,256]{2,1,0:T(8,128)(2,1)S(1)}, u32[]{:S(2)}, u32[]{:S(2)}) collective-permute-start(bf16[3,80,256]{2,1,0:T(8,128)(2,1)S(1)} %get-tuple-element.30), channel_id=1, source_target_pairs={{32,64},{96,128},{160,192},{64,32},{128,96},{192,160},{33,65},{97,... | collective-permute-start | bytes 368648 | tf_op jit(solution)/shard_map/ppermute | solution.py:563
  17.7 1.3 %collective-permute-start.4 = (f32[80,256]{1,0:T(8,128)S(1)}, f32[80,256]{1,0:T(8,128)S(1)}, u32[]{:S(2)}, u32[]{:S(2)}) collective-permute-start(f32[80,256]{1,0:T(8,128)S(1)} %get-tuple-element.35.map_here), channel_id=1, source_target_pairs={{64,0},{128,192},{65,1},{129,193},{66,2},{130,194},{67,3},{131,195... | collective-permute-start | bytes 245768 | tf_op jit(solution)/shard_map/ppermute | solution.py:568
  19.0 3.1 %diagonal_kernel.1 = (f32[4,4,320,256]{3,2,1,0:T(8,128)S(1)}, bf16[4,4,6,80,256]{4,3,2,1,0:T(8,128)(2,1)S(1)}, f32[8,256]{1,0:T(8,128)S(1)}) custom-call(f32[16,128]{1,0:T(8,128)S(1)} %get-tuple-element.25.tile, bf16[4,4,320,256]{3,2,1,0:T(8,128)(2,1)S(1)} %get-tuple-element.26.vector, bf16[4,4,320,320]{3,2,1,0:T(8,128)(2,1)} %diagonal_hbm.1), custom_call_target="tpu_custom_call" | custom-call | tf_op jit(solution)/shard_map/diagonal_kernel/pallas_call | solution.py:508
  22.0 0.8 %collective-permute-done.4.map_y = f32[80,256]{1,0:T(8,128)S(1)} collective-permute-done((f32[80,256]{1,0:T(8,128)S(1)}, f32[80,256]{1,0:T(8,128)S(1)}, u32[]{:S(2)}, u32[]{:S(2)}) %collective-permute-start.4) | collective-permute-done | bytes 81952 | tf_op jit(solution)/shard_map/ppermute | solution.py:568
  22.9 0.0 collective-permute-done.over_core
  22.9 0.0 collective-permute-done.1.over_y
  22.9 0.0 collective-permute-done.2.over_pair
  22.9 0.0 collective-permute-done.3.over_next
  22.9 0.0 copy-done
  22.9 4.2 %product_kernel.1 = (f32[4,4,320,256]{3,2,1,0:T(8,128)S(1)}, f32[3,3,80,256]{3,2,1,0:T(8,128)S(1)}, f32[5,80,256]{2,1,0:T(8,128)S(1)}) custom-call(f32[16,128]{1,0:T(8,128)S(1)} %get-tuple-element.25.tile, bf16[4,4,6,80,256]{4,3,2,1,0:T(8,128)(2,1)S(1)} %get-tuple-element.28.traces, bf16[3,80,256]{2,1,0:T(8,128)(2,1)S(1)} %collective-permute-done.over_core, ...), custom_call_target="tpu_custom_call" | custom-call | tf_op jit(solution)/shard_map/product_kernel/pallas_call | solution.py:508
  27.0 0.1 collective-permute-start.5
  27.1 1.7 %collective-permute-done.5.other.beside = f32[5,80,256]{2,1,0:T(8,128)S(1)} collective-permute-done((f32[5,80,256]{2,1,0:T(8,128)S(1)}, f32[5,80,256]{2,1,0:T(8,128)S(1)}, u32[]{:S(2)}, u32[]{:S(2)}) %collective-permute-start.5) | collective-permute-done | bytes 409632 | tf_op jit(solution)/shard_map/ppermute | solution.py:612
  28.9 0.7 chip_kernel.1
  29.6 1.8 %collective-permute-start.6 = (f32[3,80,128]{2,1,0:T(8,128)S(1)}, f32[3,80,128]{2,1,0:T(8,128)S(1)}, u32[]{:S(2)}, u32[]{:S(2)}) collective-permute-start(f32[3,80,128]{2,1,0:T(8,128)S(1)} %get-tuple-element.42), channel_id=1, source_target_pairs={{0,64},{64,128},{128,192},{1,65},{65,129},{129,193},{2,66},{66,130... | collective-permute-start | bytes 368648 | tf_op jit(solution)/shard_map/ppermute | solution.py:610
  31.4 2.0 %collective-permute-start.8 = (f32[3,80,128]{2,1,0:T(8,128)S(1)}, f32[3,80,128]{2,1,0:T(8,128)S(1)}, u32[]{:S(2)}, u32[]{:S(2)}) collective-permute-start(f32[3,80,128]{2,1,0:T(8,128)S(1)} %get-tuple-element.43), channel_id=1, source_target_pairs={{0,192},{1,193},{2,194},{3,195},{4,196},{5,197},{6,198},{7,199},{8... | collective-permute-start | bytes 368648 | tf_op jit(solution)/shard_map/ppermute | solution.py:610
  33.4 2.5 %collective-permute-start.7 = (f32[3,80,128]{2,1,0:T(8,128)S(1)}, f32[3,80,128]{2,1,0:T(8,128)S(1)}, u32[]{:S(2)}, u32[]{:S(2)}) collective-permute-start(f32[3,80,128]{2,1,0:T(8,128)S(1)} %get-tuple-element.43), channel_id=1, source_target_pairs={{0,128},{64,192},{1,129},{65,193},{2,130},{66,194},{3,131},{67,195... | collective-permute-start | bytes 368648 | tf_op jit(solution)/shard_map/ppermute | solution.py:610
  35.8 0.0 collective-permute-done.6.one
  35.8 0.0 collective-permute-done.8.three
  35.9 1.8 %collective-permute-done.7.two = f32[3,80,128]{2,1,0:T(8,128)S(1)} collective-permute-done((f32[3,80,128]{2,1,0:T(8,128)S(1)}, f32[3,80,128]{2,1,0:T(8,128)S(1)}, u32[]{:S(2)}, u32[]{:S(2)}) %collective-permute-start.7) | collective-permute-done | bytes 122912 | tf_op jit(solution)/shard_map/ppermute | solution.py:610
  37.7 1.9 %collective-permute-start.9 = (f32[3,80,128]{2,1,0:T(8,128)S(1)}, f32[3,80,128]{2,1,0:T(8,128)S(1)}, u32[]{:S(2)}, u32[]{:S(2)}) collective-permute-start(f32[3,80,128]{2,1,0:T(8,128)S(1)} %arriving_kernel.1.mine), channel_id=1, source_target_pairs={{0,32},{32,0},{1,33},{33,1},{2,34},{34,2},{3,35},{35,3},{4,36},{36... | collective-permute-start | bytes 368648 | tf_op jit(solution)/shard_map/ppermute | solution.py:616
  39.7 1.0 %collective-permute-done.9.other = f32[3,80,128]{2,1,0:T(8,128)S(1)} collective-permute-done((f32[3,80,128]{2,1,0:T(8,128)S(1)}, f32[3,80,128]{2,1,0:T(8,128)S(1)}, u32[]{:S(2)}, u32[]{:S(2)}) %collective-permute-start.9) | collective-permute-done | bytes 122912 | tf_op jit(solution)/shard_map/ppermute | solution.py:616
  40.6 2.8 %eliminate_kernel.1 = (f32[4,4,320,256]{3,2,1,0:T(8,128)S(1)}, f32[32,8,128]{2,1,0:T(8,128)S(1)}) custom-call(f32[16,128]{1,0:T(8,128)S(1)} %get-tuple-element.25.tile, bf16[4,4,320,256]{3,2,1,0:T(8,128)(2,1)S(1)} %get-tuple-element.26.vector, f32[8,256]{1,0:T(8,128)S(1)} %get-tuple-element.27.squares, f32[4,4,320,256]{3,2,1,0:T(8,128)S(1)} %get-tuple-element.37.product, ...), custom_call_target="tpu_custom_call" | custom-call | flops 1000000000 | bytes 10000000 | tf_op jit(solution)/shard_map/eliminate_kernel/pallas_call | solution.py:508
  43.4 14.2 %all_to_all.10.tiles_in = f32[32,8,128]{2,1,0:T(8,128)S(1)} all-to-all(f32[32,8,128]{2,1,0:T(8,128)S(1)} %get-tuple-element.44), channel_id=1, replica_groups=mesh['y'=4,'core'=2,'x'=4,'z'=8] {'x','z'}, dimensions={0} | all-to-all | bytes 262144 | tf_op jit(solution)/shard_map/all_to_all | solution.py:625
  57.6 0.1 merge_kernel.1
  57.7 11.9 %all_to_all.11.tiles = f32[8,8,128]{2,1,0:T(8,128)S(1)} all-to-all(f32[8,8,128]{2,1,0:T(8,128)S(1)} %merge_kernel.1), channel_id=1, replica_groups=mesh['y'=4,'core'=2,'x'=4,'z'=8] {'y','core'}, dimensions={0} | all-to-all | bytes 65536 | tf_op jit(solution)/shard_map/all_to_all | solution.py:627
  69.6 2.4 %finish_kernel.1 = (bf16[4,4,320,256]{3,2,1,0:T(8,128)(2,1)}, f32[2,256]{1,0:T(2,128)}) custom-call(f32[4,4,8,128]{3,2,1,0:T(8,128)S(1)} %get-tuple-element.24.alive, f32[8,8,128]{2,1,0:T(8,128)S(1)} %all_to_all.11.tiles, bf16[4,4,320,256]{3,2,1,0:T(8,128)(2,1)S(1)} %get-tuple-element.26.vector, f32[4,4,320,256]{3,2,1,0:T(8,128)S(1)} %get-tuple-element.45.eliminated), custom_call_target="tpu_custom_call" | custom-call | tf_op jit(solution)/shard_map/finish_kernel/pallas_call | solution.py:508
  (1 shorter events, 0.0 us)
Async XLA Ops:
  3.9 19.0 %copy-start = (bf16[4,4,6,80,320]{4,3,2,1,0:T(8,128)(2,1)S(1)}, bf16[4,4,6,80,320]{4,3,2,1,0:T(8,128)(2,1)}, u32[]{:S(2)}) copy-start(bf16[4,4,6,80,320]{4,3,2,1,0:T(8,128)(2,1)} %lifting.1) | copy-start | bytes 14745604
  3.9 18.9 %collective-permute-start.2 = (bf16[4,80,256]{2,1,0:T(8,128)(2,1)S(1)}, bf16[4,80,256]{2,1,0:T(8,128)(2,1)S(1)}, u32[]{:S(2)}, u32[]{:S(2)}) collective-permute-start(bf16[4,80,256]{2,1,0:T(8,128)(2,1)S(1)} %get-tuple-element.31), channel_id=1, source_target_pairs={{0,1},{1,0},{2,3},{3,2},{4,5},{5,4},{6,7},{7,6},{8,9},{9,8},{10,11... | collective-permute-start | bytes 491528 | tf_op jit(solution)/shard_map/ppermute | solution.py:564
  6.5 16.4 %collective-permute-start.3 = (bf16[4,80,256]{2,1,0:T(8,128)(2,1)S(1)}, bf16[4,80,256]{2,1,0:T(8,128)(2,1)S(1)}, u32[]{:S(2)}, u32[]{:S(2)}) collective-permute-start(bf16[4,80,256]{2,1,0:T(8,128)(2,1)S(1)} %get-tuple-element.32), channel_id=1, source_target_pairs={{1,2},{3,4},{5,6},{7,8},{9,10},{11,12},{13,14},{15,16},{17,18},{19... | collective-permute-start | bytes 491528 | tf_op jit(solution)/shard_map/ppermute | solution.py:566
  13.3 9.5 %collective-permute-start = (bf16[3,80,256]{2,1,0:T(8,128)(2,1)S(1)}, bf16[3,80,256]{2,1,0:T(8,128)(2,1)S(1)}, u32[]{:S(2)}, u32[]{:S(2)}) collective-permute-start(bf16[3,80,256]{2,1,0:T(8,128)(2,1)S(1)} %get-tuple-element.29), channel_id=1, source_target_pairs={{0,32},{32,0},{1,33},{33,1},{2,34},{34,2},{3,35},{35,3},{4,36},{36... | collective-permute-start | bytes 368648 | tf_op jit(solution)/shard_map/ppermute | solution.py:561
  14.6 8.3 %collective-permute-start.1 = (bf16[3,80,256]{2,1,0:T(8,128)(2,1)S(1)}, bf16[3,80,256]{2,1,0:T(8,128)(2,1)S(1)}, u32[]{:S(2)}, u32[]{:S(2)}) collective-permute-start(bf16[3,80,256]{2,1,0:T(8,128)(2,1)S(1)} %get-tuple-element.30), channel_id=1, source_target_pairs={{32,64},{96,128},{160,192},{64,32},{128,96},{192,160},{33,65},{97,... | collective-permute-start | bytes 368648 | tf_op jit(solution)/shard_map/ppermute | solution.py:563
  17.7 5.2 %collective-permute-start.4 = (f32[80,256]{1,0:T(8,128)S(1)}, f32[80,256]{1,0:T(8,128)S(1)}, u32[]{:S(2)}, u32[]{:S(2)}) collective-permute-start(f32[80,256]{1,0:T(8,128)S(1)} %get-tuple-element.35.map_here), channel_id=1, source_target_pairs={{64,0},{128,192},{65,1},{129,193},{66,2},{130,194},{67,3},{131,195... | collective-permute-start | bytes 245768 | tf_op jit(solution)/shard_map/ppermute | solution.py:568
  27.0 1.8 %collective-permute-start.5 = (f32[5,80,256]{2,1,0:T(8,128)S(1)}, f32[5,80,256]{2,1,0:T(8,128)S(1)}, u32[]{:S(2)}, u32[]{:S(2)}) collective-permute-start(f32[5,80,256]{2,1,0:T(8,128)S(1)} %get-tuple-element.41.mine), channel_id=1, source_target_pairs={{0,32},{32,0},{1,33},{33,1},{2,34},{34,2},{3,35},{35,3},{4,36},{36... | collective-permute-start | bytes 1228808 | tf_op jit(solution)/shard_map/ppermute | solution.py:612
  29.6 6.3 %collective-permute-start.6 = (f32[3,80,128]{2,1,0:T(8,128)S(1)}, f32[3,80,128]{2,1,0:T(8,128)S(1)}, u32[]{:S(2)}, u32[]{:S(2)}) collective-permute-start(f32[3,80,128]{2,1,0:T(8,128)S(1)} %get-tuple-element.42), channel_id=1, source_target_pairs={{0,64},{64,128},{128,192},{1,65},{65,129},{129,193},{2,66},{66,130... | collective-permute-start | bytes 368648 | tf_op jit(solution)/shard_map/ppermute | solution.py:610
  31.4 4.5 %collective-permute-start.8 = (f32[3,80,128]{2,1,0:T(8,128)S(1)}, f32[3,80,128]{2,1,0:T(8,128)S(1)}, u32[]{:S(2)}, u32[]{:S(2)}) collective-permute-start(f32[3,80,128]{2,1,0:T(8,128)S(1)} %get-tuple-element.43), channel_id=1, source_target_pairs={{0,192},{1,193},{2,194},{3,195},{4,196},{5,197},{6,198},{7,199},{8... | collective-permute-start | bytes 368648 | tf_op jit(solution)/shard_map/ppermute | solution.py:610
  33.4 4.3 %collective-permute-start.7 = (f32[3,80,128]{2,1,0:T(8,128)S(1)}, f32[3,80,128]{2,1,0:T(8,128)S(1)}, u32[]{:S(2)}, u32[]{:S(2)}) collective-permute-start(f32[3,80,128]{2,1,0:T(8,128)S(1)} %get-tuple-element.43), channel_id=1, source_target_pairs={{0,128},{64,192},{1,129},{65,193},{2,130},{66,194},{3,131},{67,195... | collective-permute-start | bytes 368648 | tf_op jit(solution)/shard_map/ppermute | solution.py:610
  37.7 2.9 %collective-permute-start.9 = (f32[3,80,128]{2,1,0:T(8,128)S(1)}, f32[3,80,128]{2,1,0:T(8,128)S(1)}, u32[]{:S(2)}, u32[]{:S(2)}) collective-permute-start(f32[3,80,128]{2,1,0:T(8,128)S(1)} %arriving_kernel.1.mine), channel_id=1, source_target_pairs={{0,32},{32,0},{1,33},{33,1},{2,34},{34,2},{3,35},{35,3},{4,36},{36... | collective-permute-start | bytes 368648 | tf_op jit(solution)/shard_map/ppermute | solution.py:616

commit v7 on v5

--- a/solution.py
+++ b/solution.py
@@ -142,6 +142,7 @@
     over_next,
     steps,
     prefixes,
+    last_two,
     whole,
     lower,
     inverse,
@@ -158,13 +159,18 @@
         pltpu.make_async_copy(lengths_hbm, lengths, sems.at[0]),
         pltpu.make_async_copy(norths_hbm, norths, sems.at[1]),
     ]
-    for line in range(LINES_HERE):
-        copies.append(pltpu.make_async_copy(vector_hbm.at[line], vector.at[line], block_sems.at[2, line]))
+    for at, position in enumerate((0, SEGMENT - 1)):
+        copies.append(
+            pltpu.make_async_copy(vector_hbm.at[:, position], vector.at[:, position], block_sems.at[2, at])
+        )
+    inner = pltpu.make_async_copy(
+        vector_hbm.at[:, pl.ds(1, SEGMENT - 2)], vector.at[:, pl.ds(1, SEGMENT - 2)], block_sems.at[2, 2]
+    )
     needed = []
     for line in range(LINES_HERE):
         needed.append(pltpu.make_async_copy(inverse_hbm.at[line], inverse.at[line], block_sems.at[0, line]))
         needed.append(pltpu.make_async_copy(lifting_hbm.at[line, :, 0], lower.at[line], block_sems.at[1, line]))
-    for copy in copies + needed:
+    for copy in copies + [inner] + needed:
         copy.start()
     rows = wall_face_rows()
     for copy in copies:
@@ -189,6 +195,7 @@
         over_core[slot] = jnp.where(core == 0, up, down)
         over_y[slot] = jnp.where(core == 0, down, up)
     first, last = living_here(lengths, 0), living_here(lengths, LINES_HERE - 1)
+    inner.wait()
     for position in range(SEGMENT):
         from_first = jnp.where(position < first, a_face(vector[0, position], 0), zero)
         from_last = jnp.where(position < last, a_face(vector[LINES_HERE - 1, position], 3), zero)
@@ -197,7 +204,6 @@
     for copy in needed:
         copy.wait()
     lines = [line_in_slot(slot, short) for slot in range(MOVING)]
-    so_far = [None] * MOVING
     for position in range(SEGMENT):
         for slot, line in enumerate(lines):
             step = lax.dot_general(
@@ -207,12 +213,14 @@
                 preferred_element_type=F32,
             )
             steps[slot, position] = jnp.where(position < living_here(lengths, line), -step, 0.0)
-    for position in range(SEGMENT):
-        for slot in range(MOVING):
-            step = steps[slot, position]
-            so_far[slot] = step if position == 0 else mapped(step, so_far[slot])
-            if position < SEGMENT - 1:
-                prefixes[slot, position] = so_far[slot]
+    for slot in range(MOVING):
+        prefixes[slot, 0] = steps[slot, 0]
+        prefixes[slot, 1] = mapped(steps[slot, 1], steps[slot, 0])
+        last_two[slot] = mapped(steps[slot, 3], steps[slot, 2])
+    so_far = []
+    for slot in range(MOVING):
+        prefixes[slot, 2] = mapped(steps[slot, 2], prefixes[slot, 1])
+        so_far.append(mapped(last_two[slot], prefixes[slot, 1]))
     whole[...] = jnp.concatenate(so_far + [jnp.zeros((FACE, R - MOVING * FACE), F32)], axis=1)
 
 
@@ -260,6 +268,7 @@
     lifting,
     inverse,
     steps,
+    last_two,
     map_here,
     map_y,
     product_in,
@@ -321,13 +330,13 @@
         )
 
     for_listed(lengths, listed, list_living(lengths, listed, MOVING), drive)
-    carried = [driven[slot, 0] for slot in range(MOVING)]
-    for position in range(1, SEGMENT):
-        for slot in range(MOVING):
-            carries[slot, position - 1] = carried[slot]
-            carried[slot] = driven[slot, position] + mapped(steps[slot, position], carried[slot])
-    for slot in range(MOVING):
-        outgoing[slot] = carried[slot]
+    for slot in range(MOVING):
+        carries[slot, 0] = driven[slot, 0]
+        carries[slot, 1] = driven[slot, 1] + mapped(steps[slot, 1], driven[slot, 0])
+        outgoing[slot] = driven[slot, 3] + mapped(steps[slot, 3], driven[slot, 2])
+    for slot in range(MOVING):
+        carries[slot, 2] = driven[slot, 2] + mapped(steps[slot, 2], carries[slot, 1])
+        outgoing[slot] += mapped(last_two[slot], carries[slot, 1])
     outgoing[OWN_MAPS] = map_here[...]
     outgoing[Y_MAPS] = map_y[...]
 
@@ -506,7 +515,7 @@
     edge = shaped(MOVING, FACE, R, dtype=BF16)
     side = shaped(SEGMENT, FACE, R, dtype=BF16)
     blocks = shaped(LINES_HERE, SEGMENT, FACE, BLOCK, dtype=BF16)
-    over_core, over_y, over_pair, over_next, steps, prefixes, whole, lower, inverse, vector, tile, alive = call(
+    over_core, over_y, over_pair, over_next, steps, prefixes, last_two, whole, lower, inverse, vector, tile, alive = call(
         edges_kernel,
         (
             edge,
@@ -515,6 +524,7 @@
             side,
             shaped(MOVING, SEGMENT, FACE, FACE),
             shaped(MOVING, SEGMENT - 1, FACE, FACE),
+            shaped(MOVING, FACE, FACE),
             shaped(FACE, R),
             blocks,
             blocks,
@@ -568,6 +578,7 @@
             lifting,
             inverse,
             steps,
+            last_two,
             whole,
             map_y,
             product,

time: 72.2 us -> 71.1 us (0.985)
  blocking collectives: 26 us -> 23.2 us
  Pallas kernels: 13.5 us -> 15.8 us
    all_to_all x1, blocking collectives: 15.1 us -> 12.1 us  [per_device(): tiles = lax.all_to_all(tiles, SURF, 0, 0, tiled=True)]
    pallas_call x8, Pallas kernels: 13.5 us -> 15.8 us  [call(): pl.pallas_call(kernel, out_shape=outs, in_specs=[pl.BlockSpec(memory_spac...]
    ppermute x3, starting transfers between devices: 6.97 us -> 7.85 us  [up_chips(): return lax.ppermute(value, 'y', [(i, i + far) for i in range(ranks - far)])]
    ppermute x1, starting transfers between devices: 0.85 us -> 0.09 us  [per_device(): beside = lax.ppermute(outgoing, 'core', swap)]
  transfers between devices with their start and end apart: 10 -> 10, of which waited for: 4 -> 4; matrix products, arithmetic and copies ran while one was open for 0% -> 0% of each run, Pallas kernels for 2% -> 3%
where the time goes in v7:
time: 71.1 us; the launch traced here: 70.8 us
  starting transfers between devices  24.9 us (35%)
  blocking collectives  23.2 us (33%)
  Pallas kernels  15.8 us (22%)
  waiting for transfers between devices  6.11 us (9%)
  between operations  0.78 us (1%)
    pallas_call x8, Pallas kernels, call(): pl.pallas_call(kernel, out_shape=outs, in_specs=[pl.BlockSpec(memory_spac...  15.8 us
    all_to_all x1, blocking collectives, per_device(): tiles = lax.all_to_all(tiles, SURF, 0, 0, tiled=True)  12.1 us
    all_to_all x1, blocking collectives, per_device(): tiles = lax.all_to_all(tiles, WALL, 0, 0, tiled=True)  11.1 us
    ppermute x3, starting transfers between devices, up_chips(): return lax.ppermute(value, 'y', [(i, i + far) for i in range(ranks - far)])  7.85 us
    ppermute x1, starting transfers between devices, per_device(): lax.ppermute(over_next, SURF, nexts + [(b, a) for a, b in nexts])  6.86 us
    ppermute x1, starting transfers between devices, per_device(): over_y = lax.ppermute(over_y, WALL, rungs + [(b, a) for a, b in rungs])  3.08 us
    ppermute x1, starting transfers between devices, per_device(): lax.ppermute(over_pair, SURF, [(i, i ^ 1) for i in range(surfs)])  2.55 us
    ppermute x1, starting transfers between devices, per_device(): arriving_beside = lax.ppermute(arriving, 'core', swap)  1.95 us
  transfers between devices with their start and end apart: 10, of which 4 were waited for; matrix products, arithmetic and copies ran while one was open for 0% of the time, Pallas kernels for 3%

profile of v7, /device:TPU:1, one launch (start us, length us, event | category | flops | bytes accessed | tf_op | source)
XLA Modules:
  0.0 70.8 jit_solution(26473059535418833)
XLA Ops:
  0.6 0.0 copy-start.1
  0.6 3.4 %edges_kernel.1 = (bf16[3,80,256]{2,1,0:T(8,128)(2,1)S(1)}, bf16[3,80,256]{2,1,0:T(8,128)(2,1)S(1)}, bf16[4,80,256]{2,1,0:T(8,128)(2,1)S(1)}, bf16[4,80,256]{2,1...) custom-call(s32[4]{0:T(128)} %lengths_hbm.1, ...), custom_call_target="tpu_custom_call" | custom-call | tf_op jit(solution)/shard_map/edges_kernel/pallas_call | solution.py:492
  4.1 0.0 copy-start
  4.1 2.6 %collective-permute-start.2 = (bf16[4,80,256]{2,1,0:T(8,128)(2,1)S(1)}, bf16[4,80,256]{2,1,0:T(8,128)(2,1)S(1)}, u32[]{:S(2)}, u32[]{:S(2)}) collective-permute-start(bf16[4,80,256]{2,1,0:T(8,128)(2,1)S(1)} %get-tuple-element.32), channel_id=1, source_target_pairs={{0,1},{1,0},{2,3},{3,2},{4,5},{5,4},{6,7},{7,6},{8,9},{9,8},{10,11... | collective-permute-start | bytes 491528 | tf_op jit(solution)/shard_map/ppermute | solution.py:549
  6.6 6.9 %collective-permute-start.3 = (bf16[4,80,256]{2,1,0:T(8,128)(2,1)S(1)}, bf16[4,80,256]{2,1,0:T(8,128)(2,1)S(1)}, u32[]{:S(2)}, u32[]{:S(2)}) collective-permute-start(bf16[4,80,256]{2,1,0:T(8,128)(2,1)S(1)} %get-tuple-element.33), channel_id=1, source_target_pairs={{1,2},{3,4},{5,6},{7,8},{9,10},{11,12},{13,14},{15,16},{17,18},{19... | collective-permute-start | bytes 491528 | tf_op jit(solution)/shard_map/ppermute | solution.py:551
  13.5 1.2 %collective-permute-start = (bf16[3,80,256]{2,1,0:T(8,128)(2,1)S(1)}, bf16[3,80,256]{2,1,0:T(8,128)(2,1)S(1)}, u32[]{:S(2)}, u32[]{:S(2)}) collective-permute-start(bf16[3,80,256]{2,1,0:T(8,128)(2,1)S(1)} %get-tuple-element.30), channel_id=1, source_target_pairs={{0,32},{32,0},{1,33},{33,1},{2,34},{34,2},{3,35},{35,3},{4,36},{36... | collective-permute-start | bytes 368648 | tf_op jit(solution)/shard_map/ppermute | solution.py:546
  14.7 3.1 %collective-permute-start.1 = (bf16[3,80,256]{2,1,0:T(8,128)(2,1)S(1)}, bf16[3,80,256]{2,1,0:T(8,128)(2,1)S(1)}, u32[]{:S(2)}, u32[]{:S(2)}) collective-permute-start(bf16[3,80,256]{2,1,0:T(8,128)(2,1)S(1)} %get-tuple-element.31), channel_id=1, source_target_pairs={{32,64},{96,128},{160,192},{64,32},{128,96},{192,160},{33,65},{97,... | collective-permute-start | bytes 368648 | tf_op jit(solution)/shard_map/ppermute | solution.py:548
  17.8 1.3 %collective-permute-start.4 = (f32[80,256]{1,0:T(8,128)S(1)}, f32[80,256]{1,0:T(8,128)S(1)}, u32[]{:S(2)}, u32[]{:S(2)}) collective-permute-start(f32[80,256]{1,0:T(8,128)S(1)} %get-tuple-element.37.map_here), channel_id=1, source_target_pairs={{64,0},{128,192},{65,1},{129,193},{66,2},{130,194},{67,3},{131,195... | collective-permute-start | bytes 245768 | tf_op jit(solution)/shard_map/ppermute | solution.py:553
  19.1 0.0 copy-done.1
  19.1 2.3 %diagonal_kernel.1 = (f32[4,4,320,256]{3,2,1,0:T(8,128)S(1)}, bf16[4,4,6,80,256]{4,3,2,1,0:T(8,128)(2,1)S(1)}, f32[8,256]{1,0:T(8,128)S(1)}) custom-call(f32[16,128]{1,0:T(8,128)S(1)} %get-tuple-element.26.tile, bf16[4,4,320,256]{3,2,1,0:T(8,128)(2,1)S(1)} %get-tuple-element.27.vector, bf16[4,4,320,320]{3,2,1,0:T(8,128)(2,1)S(1)} %copy-done.1), custom_call_target="tpu_custom_call" | custom-call | tf_op jit(solution)/shard_map/diagonal_kernel/pallas_call | solution.py:492
  21.4 1.6 %collective-permute-done.4.map_y = f32[80,256]{1,0:T(8,128)S(1)} collective-permute-done((f32[80,256]{1,0:T(8,128)S(1)}, f32[80,256]{1,0:T(8,128)S(1)}, u32[]{:S(2)}, u32[]{:S(2)}) %collective-permute-start.4) | collective-permute-done | bytes 81952 | tf_op jit(solution)/shard_map/ppermute | solution.py:553
  23.0 0.0 collective-permute-done.over_core
  23.0 0.0 collective-permute-done.1.over_y
  23.0 0.0 collective-permute-done.2.over_pair
  23.0 0.0 collective-permute-done.3.over_next
  23.0 0.0 copy-done
  23.0 4.0 %product_kernel.1 = (f32[4,4,320,256]{3,2,1,0:T(8,128)S(1)}, f32[3,3,80,256]{3,2,1,0:T(8,128)S(1)}, f32[5,80,256]{2,1,0:T(8,128)S(1)}) custom-call(f32[16,128]{1,0:T(8,128)S(1)} %get-tuple-element.26.tile, bf16[4,4,6,80,256]{4,3,2,1,0:T(8,128)(2,1)S(1)} %get-tuple-element.29.traces, bf16[3,80,256]{2,1,0:T(8,128)(2,1)S(1)} %collective-permute-done.over_core, ...), custom_call_target="tpu_custom_call" | custom-call | tf_op jit(solution)/shard_map/product_kernel/pallas_call | solution.py:492
  27.1 0.1 collective-permute-start.5
  27.2 1.7 %collective-permute-done.5.other.beside = f32[5,80,256]{2,1,0:T(8,128)S(1)} collective-permute-done((f32[5,80,256]{2,1,0:T(8,128)S(1)}, f32[5,80,256]{2,1,0:T(8,128)S(1)}, u32[]{:S(2)}, u32[]{:S(2)}) %collective-permute-start.5) | collective-permute-done | bytes 409632 | tf_op jit(solution)/shard_map/ppermute | solution.py:593
  28.9 0.7 chip_kernel.1
  29.6 2.0 %collective-permute-start.6 = (f32[3,80,128]{2,1,0:T(8,128)S(1)}, f32[3,80,128]{2,1,0:T(8,128)S(1)}, u32[]{:S(2)}, u32[]{:S(2)}) collective-permute-start(f32[3,80,128]{2,1,0:T(8,128)S(1)} %get-tuple-element.44), channel_id=1, source_target_pairs={{0,64},{64,128},{128,192},{1,65},{65,129},{129,193},{2,66},{66,130... | collective-permute-start | bytes 368648 | tf_op jit(solution)/shard_map/ppermute | solution.py:591
  31.6 3.3 %collective-permute-start.8 = (f32[3,80,128]{2,1,0:T(8,128)S(1)}, f32[3,80,128]{2,1,0:T(8,128)S(1)}, u32[]{:S(2)}, u32[]{:S(2)}) collective-permute-start(f32[3,80,128]{2,1,0:T(8,128)S(1)} %get-tuple-element.45), channel_id=1, source_target_pairs={{0,192},{1,193},{2,194},{3,195},{4,196},{5,197},{6,198},{7,199},{8... | collective-permute-start | bytes 368648 | tf_op jit(solution)/shard_map/ppermute | solution.py:591
  35.0 2.5 %collective-permute-start.7 = (f32[3,80,128]{2,1,0:T(8,128)S(1)}, f32[3,80,128]{2,1,0:T(8,128)S(1)}, u32[]{:S(2)}, u32[]{:S(2)}) collective-permute-start(f32[3,80,128]{2,1,0:T(8,128)S(1)} %get-tuple-element.45), channel_id=1, source_target_pairs={{0,128},{64,192},{1,129},{65,193},{2,130},{66,194},{3,131},{67,195... | collective-permute-start | bytes 368648 | tf_op jit(solution)/shard_map/ppermute | solution.py:591
  37.5 0.0 collective-permute-done.6.one
  37.5 0.0 collective-permute-done.8.three
  37.5 1.8 %collective-permute-done.7.two = f32[3,80,128]{2,1,0:T(8,128)S(1)} collective-permute-done((f32[3,80,128]{2,1,0:T(8,128)S(1)}, f32[3,80,128]{2,1,0:T(8,128)S(1)}, u32[]{:S(2)}, u32[]{:S(2)}) %collective-permute-start.7) | collective-permute-done | bytes 122912 | tf_op jit(solution)/shard_map/ppermute | solution.py:591
  39.3 1.9 %collective-permute-start.9 = (f32[3,80,128]{2,1,0:T(8,128)S(1)}, f32[3,80,128]{2,1,0:T(8,128)S(1)}, u32[]{:S(2)}, u32[]{:S(2)}) collective-permute-start(f32[3,80,128]{2,1,0:T(8,128)S(1)} %arriving_kernel.1.mine), channel_id=1, source_target_pairs={{0,32},{32,0},{1,33},{33,1},{2,34},{34,2},{3,35},{35,3},{4,36},{36... | collective-permute-start | bytes 368648 | tf_op jit(solution)/shard_map/ppermute | solution.py:597
  41.3 1.0 %collective-permute-done.9.other = f32[3,80,128]{2,1,0:T(8,128)S(1)} collective-permute-done((f32[3,80,128]{2,1,0:T(8,128)S(1)}, f32[3,80,128]{2,1,0:T(8,128)S(1)}, u32[]{:S(2)}, u32[]{:S(2)}) %collective-permute-start.9) | collective-permute-done | bytes 122912 | tf_op jit(solution)/shard_map/ppermute | solution.py:597
  42.3 2.8 %eliminate_kernel.1 = (f32[4,4,320,256]{3,2,1,0:T(8,128)S(1)}, f32[32,8,128]{2,1,0:T(8,128)S(1)}) custom-call(f32[16,128]{1,0:T(8,128)S(1)} %get-tuple-element.26.tile, bf16[4,4,320,256]{3,2,1,0:T(8,128)(2,1)S(1)} %get-tuple-element.27.vector, f32[8,256]{1,0:T(8,128)S(1)} %get-tuple-element.28.squares, f32[4,4,320,256]{3,2,1,0:T(8,128)S(1)} %get-tuple-element.39.product, ...), custom_call_target="tpu_custom_call" | custom-call | flops 1000000000 | bytes 10000000 | tf_op jit(solution)/shard_map/eliminate_kernel/pallas_call | solution.py:492
  45.0 12.1 %all_to_all.10.tiles_in = f32[32,8,128]{2,1,0:T(8,128)S(1)} all-to-all(f32[32,8,128]{2,1,0:T(8,128)S(1)} %get-tuple-element.46), channel_id=1, replica_groups=mesh['y'=4,'core'=2,'x'=4,'z'=8] {'x','z'}, dimensions={0} | all-to-all | bytes 262144 | tf_op jit(solution)/shard_map/all_to_all | solution.py:606
  57.2 0.1 merge_kernel.1
  57.3 11.1 %all_to_all.11.tiles = f32[8,8,128]{2,1,0:T(8,128)S(1)} all-to-all(f32[8,8,128]{2,1,0:T(8,128)S(1)} %merge_kernel.1), channel_id=1, replica_groups=mesh['y'=4,'core'=2,'x'=4,'z'=8] {'y','core'}, dimensions={0} | all-to-all | bytes 65536 | tf_op jit(solution)/shard_map/all_to_all | solution.py:608
  68.3 2.4 %finish_kernel.1 = (bf16[4,4,320,256]{3,2,1,0:T(8,128)(2,1)}, f32[2,256]{1,0:T(2,128)}) custom-call(f32[4,4,8,128]{3,2,1,0:T(8,128)S(1)} %get-tuple-element.25.alive, f32[8,8,128]{2,1,0:T(8,128)S(1)} %all_to_all.11.tiles, bf16[4,4,320,256]{3,2,1,0:T(8,128)(2,1)S(1)} %get-tuple-element.27.vector, f32[4,4,320,256]{3,2,1,0:T(8,128)S(1)} %get-tuple-element.47.eliminated), custom_call_target="tpu_custom_call" | custom-call | tf_op jit(solution)/shard_map/finish_kernel/pallas_call | solution.py:492
  (1 shorter events, 0.0 us)
Async XLA Ops:
  0.6 18.5 %copy-start.1 = (bf16[4,4,320,320]{3,2,1,0:T(8,128)(2,1)S(1)}, bf16[4,4,320,320]{3,2,1,0:T(8,128)(2,1)}, u32[]{:S(2)}) copy-start(bf16[4,4,320,320]{3,2,1,0:T(8,128)(2,1)} %diagonal.1) | copy-start | bytes 9830404
  4.1 19.0 %copy-start = (bf16[4,4,6,80,320]{4,3,2,1,0:T(8,128)(2,1)S(1)}, bf16[4,4,6,80,320]{4,3,2,1,0:T(8,128)(2,1)}, u32[]{:S(2)}) copy-start(bf16[4,4,6,80,320]{4,3,2,1,0:T(8,128)(2,1)} %lifting.1) | copy-start | bytes 14745604
  4.1 18.9 %collective-permute-start.2 = (bf16[4,80,256]{2,1,0:T(8,128)(2,1)S(1)}, bf16[4,80,256]{2,1,0:T(8,128)(2,1)S(1)}, u32[]{:S(2)}, u32[]{:S(2)}) collective-permute-start(bf16[4,80,256]{2,1,0:T(8,128)(2,1)S(1)} %get-tuple-element.32), channel_id=1, source_target_pairs={{0,1},{1,0},{2,3},{3,2},{4,5},{5,4},{6,7},{7,6},{8,9},{9,8},{10,11... | collective-permute-start | bytes 491528 | tf_op jit(solution)/shard_map/ppermute | solution.py:549
  6.6 16.4 %collective-permute-start.3 = (bf16[4,80,256]{2,1,0:T(8,128)(2,1)S(1)}, bf16[4,80,256]{2,1,0:T(8,128)(2,1)S(1)}, u32[]{:S(2)}, u32[]{:S(2)}) collective-permute-start(bf16[4,80,256]{2,1,0:T(8,128)(2,1)S(1)} %get-tuple-element.33), channel_id=1, source_target_pairs={{1,2},{3,4},{5,6},{7,8},{9,10},{11,12},{13,14},{15,16},{17,18},{19... | collective-permute-start | bytes 491528 | tf_op jit(solution)/shard_map/ppermute | solution.py:551
  13.5 9.5 %collective-permute-start = (bf16[3,80,256]{2,1,0:T(8,128)(2,1)S(1)}, bf16[3,80,256]{2,1,0:T(8,128)(2,1)S(1)}, u32[]{:S(2)}, u32[]{:S(2)}) collective-permute-start(bf16[3,80,256]{2,1,0:T(8,128)(2,1)S(1)} %get-tuple-element.30), channel_id=1, source_target_pairs={{0,32},{32,0},{1,33},{33,1},{2,34},{34,2},{3,35},{35,3},{4,36},{36... | collective-permute-start | bytes 368648 | tf_op jit(solution)/shard_map/ppermute | solution.py:546
  14.7 8.3 %collective-permute-start.1 = (bf16[3,80,256]{2,1,0:T(8,128)(2,1)S(1)}, bf16[3,80,256]{2,1,0:T(8,128)(2,1)S(1)}, u32[]{:S(2)}, u32[]{:S(2)}) collective-permute-start(bf16[3,80,256]{2,1,0:T(8,128)(2,1)S(1)} %get-tuple-element.31), channel_id=1, source_target_pairs={{32,64},{96,128},{160,192},{64,32},{128,96},{192,160},{33,65},{97,... | collective-permute-start | bytes 368648 | tf_op jit(solution)/shard_map/ppermute | solution.py:548
  17.8 5.2 %collective-permute-start.4 = (f32[80,256]{1,0:T(8,128)S(1)}, f32[80,256]{1,0:T(8,128)S(1)}, u32[]{:S(2)}, u32[]{:S(2)}) collective-permute-start(f32[80,256]{1,0:T(8,128)S(1)} %get-tuple-element.37.map_here), channel_id=1, source_target_pairs={{64,0},{128,192},{65,1},{129,193},{66,2},{130,194},{67,3},{131,195... | collective-permute-start | bytes 245768 | tf_op jit(solution)/shard_map/ppermute | solution.py:553
  27.1 1.8 %collective-permute-start.5 = (f32[5,80,256]{2,1,0:T(8,128)S(1)}, f32[5,80,256]{2,1,0:T(8,128)S(1)}, u32[]{:S(2)}, u32[]{:S(2)}) collective-permute-start(f32[5,80,256]{2,1,0:T(8,128)S(1)} %get-tuple-element.43.mine), channel_id=1, source_target_pairs={{0,32},{32,0},{1,33},{33,1},{2,34},{34,2},{3,35},{35,3},{4,36},{36... | collective-permute-start | bytes 1228808 | tf_op jit(solution)/shard_map/ppermute | solution.py:593
  29.6 7.9 %collective-permute-start.6 = (f32[3,80,128]{2,1,0:T(8,128)S(1)}, f32[3,80,128]{2,1,0:T(8,128)S(1)}, u32[]{:S(2)}, u32[]{:S(2)}) collective-permute-start(f32[3,80,128]{2,1,0:T(8,128)S(1)} %get-tuple-element.44), channel_id=1, source_target_pairs={{0,64},{64,128},{128,192},{1,65},{65,129},{129,193},{2,66},{66,130... | collective-permute-start | bytes 368648 | tf_op jit(solution)/shard_map/ppermute | solution.py:591
  31.6 5.8 %collective-permute-start.8 = (f32[3,80,128]{2,1,0:T(8,128)S(1)}, f32[3,80,128]{2,1,0:T(8,128)S(1)}, u32[]{:S(2)}, u32[]{:S(2)}) collective-permute-start(f32[3,80,128]{2,1,0:T(8,128)S(1)} %get-tuple-element.45), channel_id=1, source_target_pairs={{0,192},{1,193},{2,194},{3,195},{4,196},{5,197},{6,198},{7,199},{8... | collective-permute-start | bytes 368648 | tf_op jit(solution)/shard_map/ppermute | solution.py:591
  35.0 4.3 %collective-permute-start.7 = (f32[3,80,128]{2,1,0:T(8,128)S(1)}, f32[3,80,128]{2,1,0:T(8,128)S(1)}, u32[]{:S(2)}, u32[]{:S(2)}) collective-permute-start(f32[3,80,128]{2,1,0:T(8,128)S(1)} %get-tuple-element.45), channel_id=1, source_target_pairs={{0,128},{64,192},{1,129},{65,193},{2,130},{66,194},{3,131},{67,195... | collective-permute-start | bytes 368648 | tf_op jit(solution)/shard_map/ppermute | solution.py:591
  39.3 2.9 %collective-permute-start.9 = (f32[3,80,128]{2,1,0:T(8,128)S(1)}, f32[3,80,128]{2,1,0:T(8,128)S(1)}, u32[]{:S(2)}, u32[]{:S(2)}) collective-permute-start(f32[3,80,128]{2,1,0:T(8,128)S(1)} %arriving_kernel.1.mine), channel_id=1, source_target_pairs={{0,32},{32,0},{1,33},{33,1},{2,34},{34,2},{3,35},{35,3},{4,36},{36... | collective-permute-start | bytes 368648 | tf_op jit(solution)/shard_map/ppermute | solution.py:597
